TPU v7x, 32 devices: a whole 2x2x4 slice. The times are simulated.
32 devices in a mesh: expert: 16 (over z, y, core), group: 2 (over x).
Axes of the slice: x: 2, y: 2, z: 4, core: 2. Of those that a mesh axis runs over, the one named last changes fastest.
Arguments:
- tokens: bfloat16 [2, 2048, 2048], P('group', 'expert'), may hold values from -6 to 6
- routes: int32 [2, 2048, 8], P('group', 'expert'), may hold values from 0 to 15, all different within a row; in each aligned block of 128 rows (0 to 127, 128 to 255, ..., all dimensions but the last counted through in order) at most 96 rows name the same one
- gate_up: bfloat16 [16, 2048, 1536], P('expert'), may hold values from -0.125 to 0.125
- down_weight: bfloat16 [16, 2048, 768], P('expert'), may hold values from -0.21875 to 0.21875
- sketch: bfloat16 [16, 2048, 256], P('expert'), may hold values from -6 to 6
Outputs:
- gram: float32 [16, 768, 768], P('expert', 'group')
- power: float32 [16, 2048, 256], P('expert', 'group')
Inputs may be any that keep to these rules, and one draw needn't show every extreme that they name: `routes`: each token names 8 different experts; among the rows of one device no expert is named by more than 96 tokens, and in every draw some expert is named by exactly 96 tokens of some device.
All inputs are finite; a program needn't handle non-finite values.
Results may differ from a plain program's by a relative error of at most 0.0042.
Values may be sent and summed in bfloat16 or wider, within the bound.
No kernel may reach another device: no remote copies, remote signals or barrier semaphores. Data moves between devices by JAX's collectives and lax.ppermute only.
A program may use at most 64 MiB of HBM per device.

v0:
```python
import jax
import jax.numpy as jnp
from jax import lax
from jax.sharding import PartitionSpec as P

TOPK = 8


def on_device(tokens, routes, gate_up, down_weight, sketch):
    owner_count = lax.axis_size("expert")
    group_count = lax.axis_size("group")
    tok_dev = tokens.shape[1]
    model_width = tokens.shape[2]
    hidden_width = down_weight.shape[2]
    capacity = min(tok_dev, tok_dev * TOPK * 3 // (2 * owner_count))
    targets = routes.reshape(-1)
    assignments = targets.shape[0]
    onehot = (targets[:, None] == jnp.arange(owner_count, dtype=jnp.int32)[None, :]).astype(
        jnp.int32
    )
    before = jnp.cumsum(onehot, axis=0) - onehot
    slot_index = jnp.sum(before * onehot, axis=1)
    destination = targets * capacity + slot_index
    source_row = jnp.arange(assignments, dtype=jnp.int32) // TOPK
    outgoing = jnp.zeros((owner_count * capacity, model_width), jnp.bfloat16)
    outgoing = (
        outgoing.at[destination]
        .set(tokens[0][source_row])
        .reshape(owner_count, capacity, model_width)
    )
    expert_weight = gate_up[0]
    projected = jnp.einsum(
        "scd,df->scf",
        lax.all_to_all(outgoing, "expert", split_axis=0, concat_axis=0, tiled=True),
        expert_weight,
        preferred_element_type=jnp.float32,
    )
    hidden = (jax.nn.silu(projected[..., :hidden_width]) * projected[..., hidden_width:]).astype(
        jnp.bfloat16
    )
    flat_hidden = hidden.reshape(-1, hidden_width)
    scale_factor = 1.0 / (tok_dev * TOPK * group_count)
    local_gram = (
        lax.dot_general(
            flat_hidden, flat_hidden, (((0,), (0,)), ((), ())), preferred_element_type=jnp.float32
        )
        * scale_factor
    )
    panel_rows = hidden_width // group_count
    group_index = lax.axis_index("group")
    summed = lax.psum(local_gram, "group")
    gram_panel = lax.dynamic_slice_in_dim(summed, group_index * panel_rows, panel_rows, 0)
    w_down = down_weight[0]
    row_count = model_width // group_count
    own_rows = lax.dynamic_slice_in_dim(w_down, group_index * row_count, row_count, 0)

    def panel_of(probe_cols):
        reduced = lax.dot_general(
            w_down, probe_cols, (((0,), (0,)), ((), ())), preferred_element_type=jnp.float32
        )
        return jnp.dot(gram_panel, reduced, precision=lax.Precision.HIGHEST).astype(jnp.bfloat16)

    def fold_image(w_rows, panel_bf):
        return jnp.dot(
            w_rows,
            lax.all_gather(panel_bf, "group", axis=0, tiled=True),
            preferred_element_type=jnp.float32,
        )

    first_panel = panel_of(sketch[0])
    image_full = fold_image(w_down, first_panel)
    probe_cols = (
        image_full * lax.rsqrt(jnp.mean(image_full * image_full, axis=0, keepdims=True) + 1e-06)
    ).astype(jnp.bfloat16)
    second_panel = panel_of(probe_cols)
    power = fold_image(own_rows, second_panel)
    return (gram_panel[None], power[None])


def solution(mesh):
    return jax.shard_map(
        on_device,
        mesh=mesh,
        in_specs=(
            P("group", "expert", None),
            P("group", "expert", None),
            P("expert", None, None),
            P("expert", None, None),
            P("expert", None, None),
        ),
        out_specs=(P("expert", "group", None), P("expert", "group", None)),
        check_vma=False,
    )
```

profile of v0, /device:TPU:0, one launch (start us, length us, event | category | flops | bytes accessed | tf_op | source)
XLA Modules:
  0.0 300.1 jit_solution(82418149280128556)
XLA Ops:
  7.2 0.0 copy-start
  7.2 0.0 all-reduce.2.cloned.1.call-start
  7.2 0.8 broadcast_multiply_fusion
  8.1 0.9 copy.10
  8.9 0.1 eq.29
  9.0 0.1 eq.25
  9.1 0.1 copy.9
  9.2 0.1 mul.53
  9.3 4.5 %reduce-window.6 = s32[16,8,128]{2,1,0:T(8,128)S(1)} reduce-window(s32[16,8,128]{2,1,0:T(8,128)S(1)} %fusion.29, s32[]{:T(128)} %constant.20.clone.1), window={size=1x1x128 pad=0_0x0_0x127_0}, to_apply=%region_0.0 | reduce-window | flops 2080768 | bytes 131076 | tf_op jit(solution)/shard_map/reduce-window
  13.9 0.1 slice.18
  13.9 0.1 copy.12
  14.1 0.1 copy.13
  14.2 0.1 broadcast_add_fusion
  14.3 24.7 %scatter_custom_fusion = bf16[1536,2048]{1,0:T(8,128)(2,1)} fusion(s32[1024]{0:T(1024)S(1)} %bitcast.60, bf16[128,2048]{1,0:T(8,128)(2,1)} %bitcast.61, s32[1024]{0:T(1024)S(1)} %broadcast_clamp_fusion, bf16[]{:T(256)} %constant.17.clone.1), kind=kCustom, calls=%fused_computation.6 | custom fusion | bytes 6291968 | tf_op jit(solution)/shard_map/scatter | solution.py:28
  39.1 144.6 %all_to_all.5 = bf16[16,96,2048]{2,1,0:T(8,128)(2,1)S(1)} all-to-all(bf16[16,96,2048]{2,1,0:T(8,128)(2,1)} %bitcast.55), channel_id=1, replica_groups=mesh['expert'=16,'group'=2] {'expert'}, dimensions={0} | all-to-all | bytes 12582912 | tf_op jit(solution)/shard_map/all_to_all | solution.py:34
  183.6 12.3 %fusion = f32[16,96,1536]{2,1,0:T(8,128)S(1)} fusion(bf16[16,96,2048]{2,1,0:T(8,128)(2,1)S(1)} %all_to_all.5, bf16[1,2048,1536]{2,1,0:T(8,128)(2,1)} %param.7), kind=kOutput, calls=%fused_computation.2 | convolution fusion | flops 9663676416 | bytes 22020096 | tf_op jit(solution)/shard_map/scd,df->scf/dot_general | solution.py:32
  196.0 4.5 %bitcast_multiply_fusion = f32[768,768]{1,0:T(8,128)} fusion(f32[16,96,1536]{2,1,0:T(8,128)S(1)} %fusion), kind=kOutput, calls=%fused_computation.15 | convolution fusion | flops 1819607040 | bytes 11796480 | tf_op jit(solution)/shard_map/dot_general | solution.py:44
  200.5 0.0 all-reduce.2.cloned.1.call-update
  200.5 0.0 copy-done
  200.5 3.1 %fusion.9 = f32[768,256]{1,0:T(8,128)} fusion(bf16[1,2048,768]{2,1,0:T(8,128)(2,1)S(1)} %copy-done, bf16[1,2048,256]{2,1,0:T(8,128)(2,1)} %param.9), kind=kOutput, calls=%fused_computation.12 | convolution fusion | flops 805306368 | bytes 4980736 | tf_op jit(solution)/shard_map/dot_general | solution.py:58
  203.7 66.5 %all-reduce.2.cloned.1.call-done = f32[768,768]{1,0:T(8,128)} async-done(((f32[768,768]{1,0:T(8,128)}), f32[768,768]{1,0:T(8,128)}) %all-reduce.2.cloned.1.call-update) | async-done | bytes 2359312 | tf_op jit(solution)/shard_map/psum | solution.py:51
  270.1 2.6 convolution_convert_fusion.1
  272.7 7.5 %all_gather.6 = bf16[768,256]{1,0:T(8,128)(2,1)S(1)} all-gather(bf16[384,256]{1,0:T(8,128)(2,1)S(1)} %convolution_convert_fusion.1), channel_id=1, replica_groups=mesh['expert'=16,'group'=2] {'group'}, dimensions={0}, use_global_device_ids=true | all-gather | bytes 589824 | tf_op jit(solution)/shard_map/all_gather | solution.py:66
  280.3 1.1 multiply_reduce_fusion
  281.4 0.0 copy-start.1
  281.4 1.1 fusion.5
  282.5 0.6 copy-done.1
  283.0 1.1 convolution_convert_fusion
  284.2 6.4 %all_gather.7 = bf16[768,256]{1,0:T(8,128)(2,1)S(1)} all-gather(bf16[384,256]{1,0:T(8,128)(2,1)S(1)} %convolution_convert_fusion), channel_id=1, replica_groups=mesh['expert'=16,'group'=2] {'group'}, dimensions={0}, use_global_device_ids=true | all-gather | bytes 589824 | tf_op jit(solution)/shard_map/all_gather | solution.py:66
  290.6 1.5 fusion.19
  292.2 1.1 dynamic-slice_bitcast_fusion
  (8 shorter events, 0.1 us)
Async XLA Ops:
  7.2 193.4 %copy-start = (bf16[1,2048,768]{2,1,0:T(8,128)(2,1)S(1)}, bf16[1,2048,768]{2,1,0:T(8,128)(2,1)}, u32[]{:S(2)}) copy-start(bf16[1,2048,768]{2,1,0:T(8,128)(2,1)} %param.8) | copy-start | bytes 9437188
  7.2 262.9 %all-reduce.2.cloned.1.call-start = ((), (), s32[]{:S(2)}) async-start(), calls=%async_computation.1 | async-start | bytes 4718592 | tf_op jit(solution)/shard_map/psum | solution.py:51
  281.4 1.7 copy-start.1
Sparse Core Ops, SparseCore 0:
  200.7 69.4 all-reduce.1
where the time goes:
time: 301 us; the launch traced here: 300 us
  blocking collectives  159 us (53%)
  waiting for transfers between devices  66.5 us (22%)
  local copies, waits for them, and re-layouts  27.9 us (9%)
  matrix products  27.4 us (9%)
  between operations  14.1 us (5%)
  other arithmetic  5.54 us (2%)
    all_to_all x1, blocking collectives, on_device(): lax.all_to_all(outgoing, 'expert', split_axis=0, concat_axis=0, tiled=True)  145 us
    psum x1, waiting for transfers between devices, on_device(): summed = lax.psum(local_gram, 'group')  66.5 us
    scatter x1, local copies, waits for them, and re-layouts, on_device(): outgoing = outgoing.at[destination].set(tokens[0][source_row]).reshape(ow...  24.7 us
    all_gather x2, blocking collectives, fold_image(): lax.all_gather(panel_bf, 'group', axis=0, tiled=True)  14 us
    dot_general x1, matrix products, on_device(): jnp.einsum('scd,df->scf', lax.all_to_all(outgoing, 'expert', split_axis=0...  12.3 us
  transfers between devices with their start and end apart: 1, of which 1 were waited for; matrix products, arithmetic and copies ran while one was open for 1% of the time, Pallas kernels for 0%

commit v1 on v0

v1 whole, which is shorter than its diff:
```python
import functools

import jax
import jax.numpy as jnp
from jax import lax
from jax.experimental import pallas as pl
from jax.experimental.pallas import tpu as pltpu
from jax.sharding import PartitionSpec as P

TOPK = 8
LANES = 128
ID_ROWS = 16
BLOCKS_PER_CALL = 4
NT = (((1,), (1,)), ((), ()))
BF16 = jnp.bfloat16
F32 = jnp.float32
VMEM = pl.BlockSpec(memory_space=pltpu.VMEM)
SMEM = pl.BlockSpec(memory_space=pltpu.SMEM)
MIB = 1 << 20


def params(mib):
    return pltpu.CompilerParams(vmem_limit_bytes=mib * MIB)


def half_rows(tok_dev, width):
    return tok_dev // 2 * (width // LANES) + ID_ROWS


def pack_kernel(tokens_ref, routes_ref, out_ref):
    tok_dev, width = tokens_ref.shape
    top = routes_ref.shape[1]
    half, tiles = tok_dev // 2, width // LANES
    rows = half_rows(tok_dev, width)
    eye = (
        lax.broadcasted_iota(jnp.int32, (ID_ROWS, top), 0)
        == lax.broadcasted_iota(jnp.int32, (ID_ROWS, top), 1)
    ).astype(BF16)
    ids = lax.dot_general(
        eye, routes_ref[...].astype(F32).astype(BF16), NT, preferred_element_type=F32
    )
    lane = lax.broadcasted_iota(jnp.int32, ids.shape, 1)
    row = lax.broadcasted_iota(jnp.int32, ids.shape, 0)
    for h in range(2):
        for i in range(half // 16):
            for k in range(tiles):
                at = h * rows + (i * tiles + k) * 16
                out_ref[at : at + 16, :] = tokens_ref[
                    h * half + i * 16 : h * half + (i + 1) * 16, k * LANES : (k + 1) * LANES
                ]
        mine = (lane >= h * half) & (lane < (h + 1) * half) & (row < top)
        out_ref[(h + 1) * rows - ID_ROWS : (h + 1) * rows, :tok_dev] = jnp.where(
            mine, ids, -1.0
        ).astype(BF16)


def pack(tokens, routes):
    tok_dev, width = tokens.shape
    return pl.pallas_call(
        pack_kernel,
        out_shape=jax.ShapeDtypeStruct((2 * half_rows(tok_dev, width), LANES), BF16),
        in_specs=[VMEM, VMEM],
        out_specs=VMEM,
        compiler_params=params(8),
        cost_estimate=pl.CostEstimate(flops=0, bytes_accessed=tokens.size * 4, transcendentals=0),
    )(tokens, routes)


def transpose_kernel(in_ref, out_ref):
    def step(j, _):
        at = pl.multiple_of(j * LANES, LANES)
        out_ref[pl.ds(at, LANES), :] = in_ref[:, pl.ds(at, LANES)].T
        return 0

    lax.fori_loop(0, in_ref.shape[1] // LANES, step, 0)


def transposed(array):
    return pl.pallas_call(
        transpose_kernel,
        out_shape=jax.ShapeDtypeStruct(array.shape[::-1], array.dtype),
        in_specs=[VMEM],
        out_specs=VMEM,
        compiler_params=params(8),
        cost_estimate=pl.CostEstimate(flops=0, bytes_accessed=array.size * 8, transcendentals=0),
    )(array)


def reduce_kernel(w_ref, sketch_ref, wt_ref, out_ref):
    transpose_kernel(w_ref, wt_ref)
    out_ref[...] = jnp.dot(wt_ref[...], sketch_ref[...], preferred_element_type=F32)


def reduced_first(w_down, sketch):
    hidden_width, width = w_down.shape[1], w_down.shape[0]
    return pl.pallas_call(
        reduce_kernel,
        out_shape=(
            jax.ShapeDtypeStruct((hidden_width, width), BF16),
            jax.ShapeDtypeStruct((hidden_width, sketch.shape[1]), F32),
        ),
        in_specs=[VMEM, VMEM],
        out_specs=(VMEM, VMEM),
        compiler_params=params(8),
        cost_estimate=pl.CostEstimate(
            flops=2 * w_down.size * sketch.shape[1], bytes_accessed=w_down.size * 8, transcendentals=0
        ),
    )(w_down, sketch)


def upper_tiles(count):
    return [(a, b) for a in range(count) for b in range(a, count)]


def gram_step(hidden_width):
    return 2 * LANES if hidden_width % (2 * LANES) == 0 else LANES


def ffn_kernel(*refs, tok_dev, width, sources, has_gram, scale):
    operands = 1 + max(max(first[0], second[0]) for first, second in sources)
    expert_ref, weight_ref = refs[0], refs[1]
    pieces = refs[2 : 2 + operands]
    rest = list(refs[2 + operands :])
    gram_in = rest.pop(0) if has_gram else None
    gram_out = rest.pop(0)
    packed_out = rest.pop(0) if scale is not None else None
    x_ref, mask_ref, hidden_ref = rest
    half, tiles = tok_dev // 2, width // LANES
    expert = expert_ref[0].astype(F32)
    for b, block in enumerate(sources):
        hits = None
        for h, (operand, first) in enumerate(block):
            piece = pieces[operand]
            for i in range(half // 16):
                for k in range(tiles):
                    at = first + (i * tiles + k) * 16
                    row = b * tok_dev + h * half + i * 16
                    x_ref[row : row + 16, k * LANES : (k + 1) * LANES] = piece[at : at + 16, :]
            at = first + half * tiles
            found = (piece[at : at + ID_ROWS, :tok_dev].astype(F32) == expert).astype(F32)
            hits = found if hits is None else hits + found
        mask_ref[0:1, b * tok_dev : (b + 1) * tok_dev] = jnp.max(hits, axis=0, keepdims=True)
    hidden_width = weight_ref.shape[0] // 2
    step_rows = gram_step(hidden_width)
    mask = mask_ref[0:1, :]

    def step(j, _):
        at = pl.multiple_of(j * step_rows, step_rows)
        gate = lax.dot_general(
            weight_ref[pl.ds(at, step_rows), :], x_ref[...], NT, preferred_element_type=F32
        )
        up = lax.dot_general(
            weight_ref[pl.ds(pl.multiple_of(at + hidden_width, step_rows), step_rows), :],
            x_ref[...],
            NT,
            preferred_element_type=F32,
        )
        hidden_ref[pl.ds(at, step_rows), :] = (gate / (1.0 + jnp.exp(-gate)) * up * mask).astype(BF16)
        return 0

    lax.fori_loop(0, hidden_width // step_rows, step, 0)
    for first in range(0, hidden_width, step_rows):
        product = lax.dot_general(
            hidden_ref[first : first + step_rows, :],
            hidden_ref[first:, :],
            NT,
            preferred_element_type=F32,
        )
        if has_gram:
            product += gram_in[first : first + step_rows, first:]
        if scale is not None:
            product *= scale
            for a in range(first // LANES, (first + step_rows) // LANES):
                for b in range(a, hidden_width // LANES):
                    at = upper_tiles(hidden_width // LANES).index((a, b)) * LANES
                    row, column = a * LANES - first, b * LANES - first
                    packed_out[at : at + LANES, :] = product[
                        row : row + LANES, column : column + LANES
                    ].astype(BF16)
        gram_out[first : first + step_rows, first:] = product


def ffn(expert, weight_t, pieces, sources, gram, tok_dev, scale=None):
    hidden_width, width = weight_t.shape[0] // 2, weight_t.shape[1]
    rows = tok_dev * len(sources)
    out_shape = [jax.ShapeDtypeStruct((hidden_width, hidden_width), F32)]
    if scale is not None:
        packed = len(upper_tiles(hidden_width // LANES)) * LANES
        out_shape.append(jax.ShapeDtypeStruct((packed, LANES), BF16))
    operands = [expert, weight_t, *pieces] + ([] if gram is None else [gram])
    return pl.pallas_call(
        functools.partial(
            ffn_kernel,
            tok_dev=tok_dev,
            width=width,
            sources=sources,
            has_gram=gram is not None,
            scale=scale,
        ),
        out_shape=out_shape,
        in_specs=[SMEM] + [VMEM] * (len(operands) - 1),
        out_specs=[VMEM] * len(out_shape),
        scratch_shapes=[
            pltpu.VMEM((rows, width), BF16),
            pltpu.VMEM((8, rows), F32),
            pltpu.VMEM((hidden_width, rows), BF16),
        ],
        compiler_params=params(16),
        cost_estimate=pl.CostEstimate(
            flops=2 * rows * hidden_width * (2 * width + hidden_width),
            bytes_accessed=weight_t.size * 2 + rows * width * 2,
            transcendentals=rows * hidden_width,
        ),
    )(*operands)


def power_kernel(*refs, has_other):
    if has_other:
        group_ref, own_ref, other_ref, reduced_ref, w_ref, wt_ref = refs[:6]
        rest = refs[6:]
    else:
        group_ref, own_ref, reduced_ref, w_ref, wt_ref = refs[:5]
        rest = refs[5:]
    gram_ref, power_ref, full_ref, high_ref, low_ref, probe_ref = rest
    tiles = full_ref.shape[0] // LANES
    for at, (a, b) in enumerate(upper_tiles(tiles)):
        rows, columns = slice(a * LANES, (a + 1) * LANES), slice(b * LANES, (b + 1) * LANES)
        tile = own_ref[rows, columns]
        if has_other:
            tile += other_ref[at * LANES : (at + 1) * LANES, :].astype(F32)
        full_ref[rows, columns] = tile
        if a != b:
            full_ref[columns, rows] = tile.T
    group = group_ref[0]
    panel_rows = gram_ref.shape[0]
    gram_ref[...] = full_ref[pl.ds(pl.multiple_of(group * panel_rows, panel_rows), panel_rows), :]
    full = full_ref[...]
    high = full.astype(BF16)
    high_ref[...] = high
    low_ref[...] = (full - high.astype(F32)).astype(BF16)

    def panel_of(reduced):
        high = reduced.astype(BF16)
        low = (reduced - high.astype(F32)).astype(BF16)
        total = jnp.dot(low_ref[...], high, preferred_element_type=F32)
        total += jnp.dot(high_ref[...], low, preferred_element_type=F32)
        total += jnp.dot(high_ref[...], high, preferred_element_type=F32)
        return total.astype(BF16)

    image = jnp.dot(w_ref[...], panel_of(reduced_ref[...]), preferred_element_type=F32)
    mean = jnp.sum(image * image, axis=0, keepdims=True) * (1.0 / image.shape[0])
    probe_ref[...] = (image * lax.rsqrt(mean + 1e-06)).astype(BF16)
    panel = panel_of(jnp.dot(wt_ref[...], probe_ref[...], preferred_element_type=F32))
    own_rows = power_ref.shape[0]
    power_ref[...] = jnp.dot(
        w_ref[pl.ds(pl.multiple_of(group * own_rows, own_rows), own_rows), :],
        panel,
        preferred_element_type=F32,
    )


def power(group, own, other, reduced, w_down, w_down_t, group_count):
    width, hidden_width = w_down.shape
    rank = reduced.shape[1]
    operands = [group, own] + ([] if other is None else [other]) + [reduced, w_down, w_down_t]
    return pl.pallas_call(
        functools.partial(power_kernel, has_other=other is not None),
        out_shape=(
            jax.ShapeDtypeStruct((hidden_width // group_count, hidden_width), F32),
            jax.ShapeDtypeStruct((width // group_count, rank), F32),
        ),
        in_specs=[SMEM] + [VMEM] * (len(operands) - 1),
        out_specs=(VMEM, VMEM),
        scratch_shapes=[
            pltpu.VMEM((hidden_width, hidden_width), F32),
            pltpu.VMEM((hidden_width, hidden_width), BF16),
            pltpu.VMEM((hidden_width, hidden_width), BF16),
            pltpu.VMEM((width, rank), BF16),
        ],
        compiler_params=params(24),
        cost_estimate=pl.CostEstimate(
            flops=2 * rank * (6 * hidden_width * hidden_width + 3 * width * hidden_width),
            bytes_accessed=w_down.size * 8,
            transcendentals=0,
        ),
    )(*operands)


def whole(rows, at_operand):
    return ((at_operand, 0), (at_operand, rows))


def gathered_in_steps(block, weights, expert, tok_dev, scale, depth):
    per_chip = 2
    per_row = 2 * per_chip
    index = lax.axis_index("expert")
    place = index // per_row
    inner = (place == 1) | (place == 2)
    rows = block.shape[0] // 2

    def line(pairs):
        return [(a * per_row + r, b * per_row + r) for a, b in pairs for r in range(per_row)]

    ends_swap = line([(0, 1), (1, 0), (2, 3), (3, 2)])
    middle_swap = line([(1, 2), (2, 1)])
    outward = line([(1, 0), (2, 3)])
    inward = line([(0, 1), (3, 2)])
    across = [(i, i ^ per_chip) for i in range(depth * per_row)]
    sibling = [(i, i ^ 1) for i in range(depth * per_row)]

    def send(array, pairs):
        return lax.ppermute(array, "expert", pairs)

    def run(pieces, sources, gram, scale=None):
        return ffn(expert, weights, pieces, sources, gram, tok_dev, scale)

    pair = lambda *arrays: [whole(rows, i) for i in range(len(arrays))]

    q1 = send(block, ends_swap)
    q2 = send(block, middle_swap)
    y0 = send(block, across)
    block_s = send(block, sibling)
    gram = run([block, block_s], pair(block, block_s), None)[0]

    y1 = send(q1, across)
    p1 = send(q1, middle_swap)
    p2 = send(q2, outward)
    far1 = send(y0[rows:], inward)
    q1_s = send(q1, sibling)
    y0_s = send(y0, sibling)
    pieces = [q1, y0, q1_s, y0_s]
    gram = run(pieces, pair(*pieces), gram)[0]

    r2 = jnp.where(inner, q2, p2)
    y2 = send(r2, across)
    p3 = send(p1, outward)
    far2 = send(far1, middle_swap)
    r2_s = send(r2, sibling)
    y1_s = send(y1, sibling)
    pieces = [r2, y1, r2_s, y1_s]
    gram = run(pieces, pair(*pieces), gram)[0]

    r3 = jnp.where(inner, p1, p3)
    y3 = send(r3[:rows], across)
    far3 = send(far2, outward)
    r3_s = send(r3, sibling)
    y2_s = send(y2, sibling)
    pieces = [r3, y2, r3_s, y2_s]
    gram = run(pieces, pair(*pieces), gram)[0]

    far = jnp.where(inner, far2, far3)
    y3_s = send(y3, sibling)
    far_s = send(far, sibling)
    return run(
        [y3, far, y3_s, far_s], [((0, 0), (1, 0)), ((2, 0), (3, 0))], gram, scale
    )


def gathered_whole(block, weights, expert, tok_dev, scale):
    rows = block.shape[0] // 2
    blocks = lax.all_gather(block, "expert", axis=0)
    count = blocks.shape[0]
    at_once = BLOCKS_PER_CALL if count % BLOCKS_PER_CALL == 0 else 1
    sources = [whole(rows, i) for i in range(at_once)]

    def step(i, gram):
        pieces = [
            lax.dynamic_index_in_dim(blocks, i * at_once + b, 0, keepdims=False)
            for b in range(at_once)
        ]
        return ffn(expert, weights, pieces, sources, gram, tok_dev)[0]

    hidden_width = weights.shape[0] // 2
    gram = lax.fori_loop(0, count // at_once, step, jnp.zeros((hidden_width, hidden_width), F32))
    return gram * scale


def on_device(tokens, routes, gate_up, down_weight, sketch):
    owner_count = lax.axis_size("expert")
    group_count = lax.axis_size("group")
    tok_dev = tokens.shape[1]
    depth = owner_count // (2 * group_count)
    stepwise = group_count == 2 and depth == 4 and owner_count == 2 * group_count * depth
    expert = lax.axis_index("expert").astype(jnp.int32)[None]
    group = lax.axis_index("group").astype(jnp.int32)[None]
    scale = 1.0 / (tok_dev * TOPK * group_count)
    block = pack(tokens[0], routes[0])
    weights = transposed(gate_up[0])
    w_down = down_weight[0]
    w_down_t, reduced = reduced_first(w_down, sketch[0])
    if stepwise:
        own, packed = gathered_in_steps(block, weights, expert, tok_dev, scale, depth)
        other = lax.ppermute(packed, "group", [(0, 1), (1, 0)])
    else:
        own = lax.psum(gathered_whole(block, weights, expert, tok_dev, scale), "group")
        other = None
    gram, result = power(group, own, other, reduced, w_down, w_down_t, group_count)
    return gram[None], result[None]


def solution(mesh):
    return jax.shard_map(
        on_device,
        mesh=mesh,
        in_specs=(
            P("group", "expert", None),
            P("group", "expert", None),
            P("expert", None, None),
            P("expert", None, None),
            P("expert", None, None),
        ),
        out_specs=(P("expert", "group", None), P("expert", "group", None)),
        check_vma=False,
    )
```

time: 301 us -> 117 us (0.39)
  blocking collectives: 159 us -> 0 us
  Pallas kernels: 0 us -> 35.8 us
  waiting for transfers between devices: 66.5 us -> 38.7 us
  matrix products: 27.4 us -> 0 us
  starting transfers between devices: 0.04 us -> 27.1 us
  local copies, waits for them, and re-layouts: 27.9 us -> 12.7 us
  between operations: 14.1 us -> 0.85 us
  other arithmetic: 5.54 us -> 1.23 us
    all_to_all x1 -> x0, blocking collectives: 145 us -> none  [on_device(): lax.all_to_all(outgoing, 'expert', split_axis=0, concat_axis=0, tiled=True)]
    psum x1 -> x0, waiting for transfers between devices: 66.5 us -> none  [on_device(): summed = lax.psum(local_gram, 'group')]
    ppermute x0 -> x22, waiting for transfers between devices: none -> 38.7 us  [the longest x21 25.3 us: send(): return lax.ppermute(array, 'expert', pairs)]
    pallas_call x0 -> x9, Pallas kernels: none -> 35.8 us  [the longest x5 21.4 us: ffn(): pl.pallas_call(functools.partial(ffn_kernel, tok_dev=tok_dev, width=width...]
    dot_general x8 -> x0, matrix products: 27.4 us -> none  [the longest x1 12.3 us: on_device(): jnp.einsum('scd,df->scf', lax.all_to_all(outgoing, 'expert', split_axis=0...]
    ppermute x0 -> x22, starting transfers between devices: none -> 27.1 us  [the longest x21 25.6 us: send(): return lax.ppermute(array, 'expert', pairs)]
    scatter x1 -> x0, local copies, waits for them, and re-layouts: 24.7 us -> none  [on_device(): outgoing = outgoing.at[destination].set(tokens[0][source_row]).reshape(ow...]
    all_gather x2 -> x0, blocking collectives: 14 us -> none  [fold_image(): lax.all_gather(panel_bf, 'group', axis=0, tiled=True)]
  transfers between devices with their start and end apart: 1 -> 22, of which waited for: 1 -> 7; matrix products, arithmetic and copies ran while one was open for 1% -> 1% of each run, Pallas kernels for 0% -> 19%
where the time goes in v1:
time: 117 us; the launch traced here: 116 us
  waiting for transfers between devices  38.7 us (33%)
  Pallas kernels  35.8 us (31%)
  starting transfers between devices  27.1 us (23%)
  local copies, waits for them, and re-layouts  12.7 us (11%)
  other arithmetic  1.23 us (1%)
    ppermute x21, starting transfers between devices, send(): return lax.ppermute(array, 'expert', pairs)  25.6 us
    ppermute x21, waiting for transfers between devices, send(): return lax.ppermute(array, 'expert', pairs)  25.3 us
    pallas_call x5, Pallas kernels, ffn(): pl.pallas_call(functools.partial(ffn_kernel, tok_dev=tok_dev, width=width...  21.4 us
    ppermute x1, waiting for transfers between devices, on_device(): other = lax.ppermute(packed, 'group', [(0, 1), (1, 0)])  13.4 us
    unnamed x17, local copies, waits for them, and re-layouts  12.7 us
    pallas_call x1, Pallas kernels, power(): pl.pallas_call(functools.partial(power_kernel, has_other=other is not Non...  9.88 us
  transfers between devices with their start and end apart: 22, of which 7 were waited for; matrix products, arithmetic and copies ran while one was open for 1% of the time, Pallas kernels for 19%

profile of v1, /device:TPU:0, one launch (start us, length us, event | category | flops | bytes accessed | tf_op | source)
XLA Modules:
  0.0 116.4 jit_solution(3150718366916858314)
XLA Ops:
  0.6 0.8 copy.7
  1.4 1.0 copy-done.5
  2.5 0.2 shard_map.69.refs_2_
  2.6 0.7 collective-permute-start.10
  3.3 5.9 %collective-permute-start = (bf16[2080,128]{1,0:T(8,128)(2,1)S(1)}, bf16[2080,128]{1,0:T(8,128)(2,1)S(1)}, u32[]{:S(2)}, u32[]{:S(2)}) collective-permute-start(bf16[2080,128]{1,0:T(8,128)(2,1)S(1)} %shard_map.69.refs_2_), channel_id=1, source_target_pairs={{0,8},{2,10},{4,12},{6,14},{8,0},{10,2},{12,4},{14,6},{16,24},{18,... | collective-permute-start | bytes 1597448 | tf_op jit(solution)/shard_map/ppermute | solution.py:312
  9.2 1.5 %collective-permute-start.4 = (bf16[2080,128]{1,0:T(8,128)(2,1)S(1)}, bf16[2080,128]{1,0:T(8,128)(2,1)S(1)}, u32[]{:S(2)}, u32[]{:S(2)}) collective-permute-start(bf16[2080,128]{1,0:T(8,128)(2,1)S(1)} %shard_map.69.refs_2_), channel_id=1, source_target_pairs={{0,4},{2,6},{4,0},{6,2},{8,12},{10,14},{12,8},{14,10},{16,20},{18,... | collective-permute-start | bytes 1597448 | tf_op jit(solution)/shard_map/ppermute | solution.py:312
  10.7 0.0 collective-permute-start.20
  10.7 0.0 collective-permute-done.10
  10.7 1.3 %collective-permute-start.11 = (bf16[2080,128]{1,0:T(8,128)(2,1)S(1)}, bf16[2080,128]{1,0:T(8,128)(2,1)}, u32[]{:S(2)}, u32[]{:S(2)}) collective-permute-start(bf16[2080,128]{1,0:T(8,128)(2,1)S(1)} %collective-permute-done.10), channel_id=1, source_target_pairs={{8,0},{10,2},{12,4},{14,6},{16,24},{18,26},{20,28},{22,30},{9,1},{... | collective-permute-start | bytes 1597448 | tf_op jit(solution)/shard_map/ppermute | solution.py:312
  12.0 9.0 %collective-permute-done.refs_2_ = bf16[2080,128]{1,0:T(8,128)(2,1)S(1)} collective-permute-done((bf16[2080,128]{1,0:T(8,128)(2,1)S(1)}, bf16[2080,128]{1,0:T(8,128)(2,1)S(1)}, u32[]{:S(2)}, u32[]{:S(2)}) %collective-permute-start) | collective-permute-done | bytes 532512 | tf_op jit(solution)/shard_map/ppermute | solution.py:312
  21.0 0.7 collective-permute-start.1
  21.7 0.8 collective-permute-done.4.refs_3_
  22.5 7.1 %collective-permute-start.5 = (bf16[1040,128]{1,0:T(8,128)(2,1)S(1)}, bf16[1040,128]{1,0:T(8,128)(2,1)}, u32[]{:S(2)}, u32[]{:S(2)}) collective-permute-start(bf16[1040,128]{1,0:T(8,128)(2,1)S(1)} %slice.9), channel_id=1, source_target_pairs={{0,8},{2,10},{4,12},{6,14},{24,16},{26,18},{28,20},{30,22},{1,9},{... | collective-permute-start | bytes 798728 | tf_op jit(solution)/shard_map/ppermute | solution.py:312
  29.6 2.8 %copy-done.2 = bf16[1,2048,1536]{2,1,0:T(8,128)(2,1)S(1)} copy-done((bf16[1,2048,1536]{2,1,0:T(8,128)(2,1)S(1)}, bf16[1,2048,1536]{2,1,0:T(8,128)(2,1)}, u32[]{:S(2)}) %copy-start.2) | copy-done | bytes 6291480
  32.4 2.3 %shard_map.68.refs_1_ = bf16[1536,2048]{1,0:T(8,128)(2,1)S(1)} custom-call(bf16[2048,1536]{1,0:T(8,128)(2,1)S(1)} %bitcast.9), custom_call_target="tpu_custom_call" | custom-call | bytes 25165824 | tf_op jit(solution)/shard_map/pallas_call | solution.py:79
  34.7 0.0 copy-start
  34.7 2.6 %copy-done = bf16[1536,2048]{1,0:T(8,128)(2,1)} copy-done((bf16[1536,2048]{1,0:T(8,128)(2,1)}, bf16[1536,2048]{1,0:T(8,128)(2,1)S(1)}, u32[]{:S(2)}) %copy-start) | copy-done | bytes 6291480
  37.3 0.0 collective-permute-start.18
  37.3 0.0 collective-permute-done.20.refs_3_
  37.3 0.5 collective-permute-start.19
  37.8 2.8 %copy-done.1 = bf16[1536,2048]{1,0:T(8,128)(2,1)S(1)} copy-done((bf16[1536,2048]{1,0:T(8,128)(2,1)S(1)}, bf16[1536,2048]{1,0:T(8,128)(2,1)}, u32[]{:S(2)}) %copy-start.1) | copy-done | bytes 6291480
  40.6 2.9 %shard_map.70.refs_6_ = f32[768,768]{1,0:T(8,128)S(1)} custom-call(s32[1]{0:T(128)} %bitcast.1.refs_0_, bf16[1536,2048]{1,0:T(8,128)(2,1)S(1)} %copy-done.1, bf16[2080,128]{1,0:T(8,128)(2,1)S(1)} %shard_map.69.refs_2_, bf16[2080,128]{1,0:T(8,128)(2,1)S(1)} %collective-permute-done.20.refs_3_), custom_call_target="tpu_custom_call" | custom-call | flops 1912602624 | bytes 7340032 | tf_op jit(solution)/shard_map/pallas_call | solution.py:191
  43.5 0.0 collective-permute-done.5
  43.5 1.6 %collective-permute-start.15 = (bf16[2080,128]{1,0:T(8,128)(2,1)S(1)}, bf16[2080,128]{1,0:T(8,128)(2,1)S(1)}, u32[]{:S(2)}, u32[]{:S(2)}) collective-permute-start(bf16[2080,128]{1,0:T(8,128)(2,1)S(1)} %collective-permute-done.refs_2_), channel_id=1, source_target_pairs={{0,4},{2,6},{4,0},{6,2},{8,12},{10,14},{12,8},{14,10},{16,20},{18,... | collective-permute-start | bytes 1597448 | tf_op jit(solution)/shard_map/ppermute | solution.py:312
  45.1 0.0 collective-permute-done.11
  45.1 0.7 collective-permute-start.6
  45.8 0.0 collective-permute-done.1
  45.8 1.3 %collective-permute-start.2 = (bf16[2080,128]{1,0:T(8,128)(2,1)S(1)}, bf16[2080,128]{1,0:T(8,128)(2,1)S(1)}, u32[]{:S(2)}, u32[]{:S(2)}) collective-permute-start(bf16[2080,128]{1,0:T(8,128)(2,1)S(1)} %collective-permute-done.1), channel_id=1, source_target_pairs={{8,0},{10,2},{12,4},{14,6},{16,24},{18,26},{20,28},{22,30},{9,1},{... | collective-permute-start | bytes 1597448 | tf_op jit(solution)/shard_map/ppermute | solution.py:312
  47.1 1.1 broadcast_select_fusion.refs_2_
  48.2 0.0 collective-permute-done.18.refs_4_
  48.2 0.1 collective-permute-start.16
  48.3 0.0 collective-permute-done.19.refs_5_
  48.3 0.6 collective-permute-start.12
  48.9 9.7 %collective-permute-done.15.refs_3_ = bf16[2080,128]{1,0:T(8,128)(2,1)S(1)} collective-permute-done((bf16[2080,128]{1,0:T(8,128)(2,1)S(1)}, bf16[2080,128]{1,0:T(8,128)(2,1)S(1)}, u32[]{:S(2)}, u32[]{:S(2)}) %collective-permute-start.15) | collective-permute-done | bytes 532512 | tf_op jit(solution)/shard_map/ppermute | solution.py:312
  58.6 0.0 collective-permute-start.17
  58.6 0.0 collective-permute-done.6
  58.6 1.3 %collective-permute-start.7 = (bf16[1040,128]{1,0:T(8,128)(2,1)S(1)}, bf16[1040,128]{1,0:T(8,128)(2,1)S(1)}, u32[]{:S(2)}, u32[]{:S(2)}) collective-permute-start(bf16[1040,128]{1,0:T(8,128)(2,1)S(1)} %collective-permute-done.6), channel_id=1, source_target_pairs={{8,0},{10,2},{12,4},{14,6},{16,24},{18,26},{20,28},{22,30},{9,1},{... | collective-permute-start | bytes 798728 | tf_op jit(solution)/shard_map/ppermute | solution.py:312
  59.9 5.0 %shard_map.71.refs_6_ = f32[768,768]{1,0:T(8,128)S(1)} custom-call(s32[1]{0:T(128)} %bitcast.1.refs_0_, bf16[1536,2048]{1,0:T(8,128)(2,1)S(1)} %copy-done.1, bf16[2080,128]{1,0:T(8,128)(2,1)S(1)} %collective-permute-done.refs_2_, bf16[2080,128]{1,0:T(8,128)(2,1)S(1)} %collective-permute-done.4.refs_3_, ...), custom_call_target="tpu_custom_call" | custom-call | flops 3825205248 | bytes 8388608 | tf_op jit(solution)/shard_map/pallas_call | solution.py:191
  64.9 0.0 collective-permute-done.2
  64.9 0.1 broadcast_select_fusion.1.refs_2_
  65.0 0.6 collective-permute-start.13
  65.6 3.4 %collective-permute-done.12.refs_3_ = bf16[2080,128]{1,0:T(8,128)(2,1)S(1)} collective-permute-done((bf16[2080,128]{1,0:T(8,128)(2,1)S(1)}, bf16[2080,128]{1,0:T(8,128)(2,1)S(1)}, u32[]{:S(2)}, u32[]{:S(2)}) %collective-permute-start.12) | collective-permute-done | bytes 532512 | tf_op jit(solution)/shard_map/ppermute | solution.py:312
  69.0 0.0 collective-permute-start.14
  69.0 0.3 collective-permute-done.7
  69.3 0.3 collective-permute-start.9
  69.6 0.0 collective-permute-done.16.refs_4_
  69.6 1.6 %collective-permute-start.3 = (bf16[1040,128]{1,0:T(8,128)(2,1)S(1)}, bf16[1040,128]{1,0:T(8,128)(2,1)S(1)}, u32[]{:S(2)}, u32[]{:S(2)}) collective-permute-start(bf16[1040,128]{1,0:T(8,128)(2,1)S(1)} %slice.8), channel_id=1, source_target_pairs={{0,4},{2,6},{4,0},{6,2},{8,12},{10,14},{12,8},{14,10},{16,20},{18,... | collective-permute-start | bytes 798728 | tf_op jit(solution)/shard_map/ppermute | solution.py:312
  71.2 0.0 collective-permute-done.17.refs_5_
  71.2 4.9 %shard_map.72.refs_6_ = f32[768,768]{1,0:T(8,128)S(1)} custom-call(s32[1]{0:T(128)} %bitcast.1.refs_0_, bf16[1536,2048]{1,0:T(8,128)(2,1)S(1)} %copy-done.1, bf16[2080,128]{1,0:T(8,128)(2,1)S(1)} %broadcast_select_fusion.refs_2_, bf16[2080,128]{1,0:T(8,128)(2,1)S(1)} %collective-permute-done.15.refs_3_, ...), custom_call_target="tpu_custom_call" | custom-call | flops 3825205248 | bytes 8388608 | tf_op jit(solution)/shard_map/pallas_call | solution.py:191
  76.1 2.2 %collective-permute-done.3.refs_2_ = bf16[1040,128]{1,0:T(8,128)(2,1)S(1)} collective-permute-done((bf16[1040,128]{1,0:T(8,128)(2,1)S(1)}, bf16[1040,128]{1,0:T(8,128)(2,1)S(1)}, u32[]{:S(2)}, u32[]{:S(2)}) %collective-permute-start.3) | collective-permute-done | bytes 266272 | tf_op jit(solution)/shard_map/ppermute | solution.py:312
  78.3 0.0 collective-permute-start.8
  78.3 0.0 collective-permute-done.13.refs_4_
  78.3 0.0 collective-permute-done.14.refs_5_
  78.3 4.8 %shard_map.73.refs_6_ = f32[768,768]{1,0:T(8,128)S(1)} custom-call(s32[1]{0:T(128)} %bitcast.1.refs_0_, bf16[1536,2048]{1,0:T(8,128)(2,1)S(1)} %copy-done.1, bf16[2080,128]{1,0:T(8,128)(2,1)S(1)} %broadcast_select_fusion.1.refs_2_, bf16[2080,128]{1,0:T(8,128)(2,1)S(1)} %collective-permute-done.12.refs_3_, ...), custom_call_target="tpu_custom_call" | custom-call | flops 3825205248 | bytes 8388608 | tf_op jit(solution)/shard_map/pallas_call | solution.py:191
  83.1 0.0 copy-start.3
  83.1 0.0 collective-permute-done.9.refs_5_
  83.2 0.0 collective-permute-done.8.refs_4_
  83.2 3.8 %shard_map.74 = (f32[768,768]{1,0:T(8,128)S(1)}, bf16[2688,128]{1,0:T(8,128)(2,1)}) custom-call(s32[1]{0:T(128)} %bitcast.1.refs_0_, bf16[1536,2048]{1,0:T(8,128)(2,1)S(1)} %copy-done.1, bf16[1040,128]{1,0:T(8,128)(2,1)S(1)} %collective-permute-done.3.refs_2_, bf16[1040,128]{1,0:T(8,128)(2,1)S(1)} %broadcast_select_fusion.2.refs_3_, ...), custom_call_target="tpu_custom_call" | custom-call | flops 1912602624 | bytes 7340032 | tf_op jit(solution)/shard_map/pallas_call | solution.py:191
  86.9 1.4 %copy-done.6 = f32[768,768]{1,0:T(8,128)} copy-done((f32[768,768]{1,0:T(8,128)}, f32[768,768]{1,0:T(8,128)S(1)}, u32[]{:S(2)}) %copy-start.6) | copy-done | bytes 2359320
  88.3 1.5 %collective-permute-start.21 = (bf16[2688,128]{1,0:T(8,128)(2,1)}, bf16[2688,128]{1,0:T(8,128)(2,1)}, u32[]{:S(2)}, u32[]{:S(2)}) collective-permute-start(bf16[2688,128]{1,0:T(8,128)(2,1)} %get-tuple-element.9), channel_id=1, source_target_pairs={{0,1},{1,0},{2,3},{3,2},{4,5},{5,4},{6,7},{7,6},{8,9},{9,8},{10,11... | collective-permute-start | bytes 2064392 | tf_op jit(solution)/shard_map/ppermute | solution.py:393
  89.8 1.2 %copy-done.4 = bf16[1,2048,256]{2,1,0:T(8,128)(2,1)S(1)} copy-done((bf16[1,2048,256]{2,1,0:T(8,128)(2,1)S(1)}, bf16[1,2048,256]{2,1,0:T(8,128)(2,1)}, u32[]{:S(2)}) %copy-start.4) | copy-done | bytes 1048600
  91.1 2.1 %shard_map.75 = (bf16[768,2048]{1,0:T(8,128)(2,1)S(1)}, f32[768,256]{1,0:T(8,128)S(1)}) custom-call(bf16[2048,768]{1,0:T(8,128)(2,1)S(1)} %bitcast.10, bf16[2048,256]{1,0:T(8,128)(2,1)S(1)} %bitcast.12), custom_call_target="tpu_custom_call" | custom-call | flops 805306368 | bytes 12582912 | tf_op jit(solution)/shard_map/pallas_call | solution.py:96
  93.2 13.4 %collective-permute-done.21.refs_2_ = bf16[2688,128]{1,0:T(8,128)(2,1)} collective-permute-done((bf16[2688,128]{1,0:T(8,128)(2,1)}, bf16[2688,128]{1,0:T(8,128)(2,1)}, u32[]{:S(2)}, u32[]{:S(2)}) %collective-permute-start.21) | collective-permute-done | bytes 688160 | tf_op jit(solution)/shard_map/ppermute | solution.py:393
  106.5 9.9 %shard_map.76 = (f32[384,768]{1,0:T(8,128)}, f32[1024,256]{1,0:T(8,128)}) custom-call(s32[1]{0:T(128)} %bitcast.refs_0_, f32[768,768]{1,0:T(8,128)S(1)} %copy-done.7, bf16[2688,128]{1,0:T(8,128)(2,1)} %collective-permute-done.21.refs_2_, f32[768,256]{1,0:T(8,128)S(1)} %get-tuple-element.10.refs_3_, bf16[2048,768]{1,0:T(8,128)(2,1)S(1)} %bitcast.11, ...), custom_call_target="tpu_custom_call" | custom-call | flops 4227858432 | bytes 12582912 | tf_op jit(solution)/shard_map/pallas_call | solution.py:266
  (11 shorter events, 0.1 us)
Async XLA Ops:
  1.4 1.0 copy-start.5
  2.6 8.1 %collective-permute-start.10 = (bf16[2080,128]{1,0:T(8,128)(2,1)S(1)}, bf16[2080,128]{1,0:T(8,128)(2,1)S(1)}, u32[]{:S(2)}, u32[]{:S(2)}) collective-permute-start(bf16[2080,128]{1,0:T(8,128)(2,1)S(1)} %shard_map.69.refs_2_), channel_id=1, source_target_pairs={{8,16},{10,18},{12,20},{14,22},{16,8},{18,10},{20,12},{22,14},{9,1... | collective-permute-start | bytes 1597448 | tf_op jit(solution)/shard_map/ppermute | solution.py:312
  3.3 17.7 %collective-permute-start = (bf16[2080,128]{1,0:T(8,128)(2,1)S(1)}, bf16[2080,128]{1,0:T(8,128)(2,1)S(1)}, u32[]{:S(2)}, u32[]{:S(2)}) collective-permute-start(bf16[2080,128]{1,0:T(8,128)(2,1)S(1)} %shard_map.69.refs_2_), channel_id=1, source_target_pairs={{0,8},{2,10},{4,12},{6,14},{8,0},{10,2},{12,4},{14,6},{16,24},{18,... | collective-permute-start | bytes 1597448 | tf_op jit(solution)/shard_map/ppermute | solution.py:312
  9.2 13.3 %collective-permute-start.4 = (bf16[2080,128]{1,0:T(8,128)(2,1)S(1)}, bf16[2080,128]{1,0:T(8,128)(2,1)S(1)}, u32[]{:S(2)}, u32[]{:S(2)}) collective-permute-start(bf16[2080,128]{1,0:T(8,128)(2,1)S(1)} %shard_map.69.refs_2_), channel_id=1, source_target_pairs={{0,4},{2,6},{4,0},{6,2},{8,12},{10,14},{12,8},{14,10},{16,20},{18,... | collective-permute-start | bytes 1597448 | tf_op jit(solution)/shard_map/ppermute | solution.py:312
  10.7 26.6 %collective-permute-start.20 = (bf16[2080,128]{1,0:T(8,128)(2,1)S(1)}, bf16[2080,128]{1,0:T(8,128)(2,1)S(1)}, u32[]{:S(2)}, u32[]{:S(2)}) collective-permute-start(bf16[2080,128]{1,0:T(8,128)(2,1)S(1)} %shard_map.69.refs_2_), channel_id=1, source_target_pairs={{0,2},{2,0},{4,6},{6,4},{8,10},{10,8},{12,14},{14,12},{16,18},{18,... | collective-permute-start | bytes 1597448 | tf_op jit(solution)/shard_map/ppermute | solution.py:312
  10.7 34.4 %collective-permute-start.11 = (bf16[2080,128]{1,0:T(8,128)(2,1)S(1)}, bf16[2080,128]{1,0:T(8,128)(2,1)}, u32[]{:S(2)}, u32[]{:S(2)}) collective-permute-start(bf16[2080,128]{1,0:T(8,128)(2,1)S(1)} %collective-permute-done.10), channel_id=1, source_target_pairs={{8,0},{10,2},{12,4},{14,6},{16,24},{18,26},{20,28},{22,30},{9,1},{... | collective-permute-start | bytes 1597448 | tf_op jit(solution)/shard_map/ppermute | solution.py:312
  21.0 24.8 %collective-permute-start.1 = (bf16[2080,128]{1,0:T(8,128)(2,1)S(1)}, bf16[2080,128]{1,0:T(8,128)(2,1)S(1)}, u32[]{:S(2)}, u32[]{:S(2)}) collective-permute-start(bf16[2080,128]{1,0:T(8,128)(2,1)S(1)} %collective-permute-done.refs_2_), channel_id=1, source_target_pairs={{8,16},{10,18},{12,20},{14,22},{16,8},{18,10},{20,12},{22,14},{9,1... | collective-permute-start | bytes 1597448 | tf_op jit(solution)/shard_map/ppermute | solution.py:312
  22.5 21.0 %collective-permute-start.5 = (bf16[1040,128]{1,0:T(8,128)(2,1)S(1)}, bf16[1040,128]{1,0:T(8,128)(2,1)}, u32[]{:S(2)}, u32[]{:S(2)}) collective-permute-start(bf16[1040,128]{1,0:T(8,128)(2,1)S(1)} %slice.9), channel_id=1, source_target_pairs={{0,8},{2,10},{4,12},{6,14},{24,16},{26,18},{28,20},{30,22},{1,9},{... | collective-permute-start | bytes 798728 | tf_op jit(solution)/shard_map/ppermute | solution.py:312
  29.6 2.8 %copy-start.2 = (bf16[1,2048,1536]{2,1,0:T(8,128)(2,1)S(1)}, bf16[1,2048,1536]{2,1,0:T(8,128)(2,1)}, u32[]{:S(2)}) copy-start(bf16[1,2048,1536]{2,1,0:T(8,128)(2,1)} %param.7) | copy-start | bytes 18874372
  34.7 2.6 %copy-start = (bf16[1536,2048]{1,0:T(8,128)(2,1)}, bf16[1536,2048]{1,0:T(8,128)(2,1)S(1)}, u32[]{:S(2)}) copy-start(bf16[1536,2048]{1,0:T(8,128)(2,1)S(1)} %shard_map.68.refs_1_) | copy-start | bytes 18874372
  37.3 10.9 %collective-permute-start.18 = (bf16[2080,128]{1,0:T(8,128)(2,1)S(1)}, bf16[2080,128]{1,0:T(8,128)(2,1)S(1)}, u32[]{:S(2)}, u32[]{:S(2)}) collective-permute-start(bf16[2080,128]{1,0:T(8,128)(2,1)S(1)} %collective-permute-done.refs_2_), channel_id=1, source_target_pairs={{0,2},{2,0},{4,6},{6,4},{8,10},{10,8},{12,14},{14,12},{16,18},{18,... | collective-permute-start | bytes 1597448 | tf_op jit(solution)/shard_map/ppermute | solution.py:312
  37.3 11.0 %collective-permute-start.19 = (bf16[2080,128]{1,0:T(8,128)(2,1)S(1)}, bf16[2080,128]{1,0:T(8,128)(2,1)S(1)}, u32[]{:S(2)}, u32[]{:S(2)}) collective-permute-start(bf16[2080,128]{1,0:T(8,128)(2,1)S(1)} %collective-permute-done.4.refs_3_), channel_id=1, source_target_pairs={{0,2},{2,0},{4,6},{6,4},{8,10},{10,8},{12,14},{14,12},{16,18},{18,... | collective-permute-start | bytes 1597448 | tf_op jit(solution)/shard_map/ppermute | solution.py:312
  37.8 2.8 %copy-start.1 = (bf16[1536,2048]{1,0:T(8,128)(2,1)S(1)}, bf16[1536,2048]{1,0:T(8,128)(2,1)}, u32[]{:S(2)}) copy-start(bf16[1536,2048]{1,0:T(8,128)(2,1)} %copy-done) | copy-start | bytes 18874372
  43.5 15.0 %collective-permute-start.15 = (bf16[2080,128]{1,0:T(8,128)(2,1)S(1)}, bf16[2080,128]{1,0:T(8,128)(2,1)S(1)}, u32[]{:S(2)}, u32[]{:S(2)}) collective-permute-start(bf16[2080,128]{1,0:T(8,128)(2,1)S(1)} %collective-permute-done.refs_2_), channel_id=1, source_target_pairs={{0,4},{2,6},{4,0},{6,2},{8,12},{10,14},{12,8},{14,10},{16,20},{18,... | collective-permute-start | bytes 1597448 | tf_op jit(solution)/shard_map/ppermute | solution.py:312
  45.1 13.5 %collective-permute-start.6 = (bf16[1040,128]{1,0:T(8,128)(2,1)}, bf16[1040,128]{1,0:T(8,128)(2,1)S(1)}, u32[]{:S(2)}, u32[]{:S(2)}) collective-permute-start(bf16[1040,128]{1,0:T(8,128)(2,1)} %collective-permute-done.5), channel_id=1, source_target_pairs={{8,16},{10,18},{12,20},{14,22},{16,8},{18,10},{20,12},{22,14},{9,1... | collective-permute-start | bytes 798728 | tf_op jit(solution)/shard_map/ppermute | solution.py:312
  45.8 19.1 %collective-permute-start.2 = (bf16[2080,128]{1,0:T(8,128)(2,1)S(1)}, bf16[2080,128]{1,0:T(8,128)(2,1)S(1)}, u32[]{:S(2)}, u32[]{:S(2)}) collective-permute-start(bf16[2080,128]{1,0:T(8,128)(2,1)S(1)} %collective-permute-done.1), channel_id=1, source_target_pairs={{8,0},{10,2},{12,4},{14,6},{16,24},{18,26},{20,28},{22,30},{9,1},{... | collective-permute-start | bytes 1597448 | tf_op jit(solution)/shard_map/ppermute | solution.py:312
  48.2 21.4 %collective-permute-start.16 = (bf16[2080,128]{1,0:T(8,128)(2,1)S(1)}, bf16[2080,128]{1,0:T(8,128)(2,1)S(1)}, u32[]{:S(2)}, u32[]{:S(2)}) collective-permute-start(bf16[2080,128]{1,0:T(8,128)(2,1)S(1)} %broadcast_select_fusion.refs_2_), channel_id=1, source_target_pairs={{0,2},{2,0},{4,6},{6,4},{8,10},{10,8},{12,14},{14,12},{16,18},{18,... | collective-permute-start | bytes 1597448 | tf_op jit(solution)/shard_map/ppermute | solution.py:312
  48.3 20.7 %collective-permute-start.12 = (bf16[2080,128]{1,0:T(8,128)(2,1)S(1)}, bf16[2080,128]{1,0:T(8,128)(2,1)S(1)}, u32[]{:S(2)}, u32[]{:S(2)}) collective-permute-start(bf16[2080,128]{1,0:T(8,128)(2,1)S(1)} %broadcast_select_fusion.refs_2_), channel_id=1, source_target_pairs={{0,4},{2,6},{4,0},{6,2},{8,12},{10,14},{12,8},{14,10},{16,20},{18,... | collective-permute-start | bytes 1597448 | tf_op jit(solution)/shard_map/ppermute | solution.py:312
  58.6 12.7 %collective-permute-start.17 = (bf16[2080,128]{1,0:T(8,128)(2,1)S(1)}, bf16[2080,128]{1,0:T(8,128)(2,1)S(1)}, u32[]{:S(2)}, u32[]{:S(2)}) collective-permute-start(bf16[2080,128]{1,0:T(8,128)(2,1)S(1)} %collective-permute-done.15.refs_3_), channel_id=1, source_target_pairs={{0,2},{2,0},{4,6},{6,4},{8,10},{10,8},{12,14},{14,12},{16,18},{18,... | collective-permute-start | bytes 1597448 | tf_op jit(solution)/shard_map/ppermute | solution.py:312
  58.6 10.7 %collective-permute-start.7 = (bf16[1040,128]{1,0:T(8,128)(2,1)S(1)}, bf16[1040,128]{1,0:T(8,128)(2,1)S(1)}, u32[]{:S(2)}, u32[]{:S(2)}) collective-permute-start(bf16[1040,128]{1,0:T(8,128)(2,1)S(1)} %collective-permute-done.6), channel_id=1, source_target_pairs={{8,0},{10,2},{12,4},{14,6},{16,24},{18,26},{20,28},{22,30},{9,1},{... | collective-permute-start | bytes 798728 | tf_op jit(solution)/shard_map/ppermute | solution.py:312
  65.0 13.3 %collective-permute-start.13 = (bf16[2080,128]{1,0:T(8,128)(2,1)S(1)}, bf16[2080,128]{1,0:T(8,128)(2,1)S(1)}, u32[]{:S(2)}, u32[]{:S(2)}) collective-permute-start(bf16[2080,128]{1,0:T(8,128)(2,1)S(1)} %broadcast_select_fusion.1.refs_2_), channel_id=1, source_target_pairs={{0,2},{2,0},{4,6},{6,4},{8,10},{10,8},{12,14},{14,12},{16,18},{18,... | collective-permute-start | bytes 1597448 | tf_op jit(solution)/shard_map/ppermute | solution.py:312
  69.0 9.3 %collective-permute-start.14 = (bf16[2080,128]{1,0:T(8,128)(2,1)S(1)}, bf16[2080,128]{1,0:T(8,128)(2,1)S(1)}, u32[]{:S(2)}, u32[]{:S(2)}) collective-permute-start(bf16[2080,128]{1,0:T(8,128)(2,1)S(1)} %collective-permute-done.12.refs_3_), channel_id=1, source_target_pairs={{0,2},{2,0},{4,6},{6,4},{8,10},{10,8},{12,14},{14,12},{16,18},{18,... | collective-permute-start | bytes 1597448 | tf_op jit(solution)/shard_map/ppermute | solution.py:312
  69.3 13.9 %collective-permute-start.9 = (bf16[1040,128]{1,0:T(8,128)(2,1)S(1)}, bf16[1040,128]{1,0:T(8,128)(2,1)S(1)}, u32[]{:S(2)}, u32[]{:S(2)}) collective-permute-start(bf16[1040,128]{1,0:T(8,128)(2,1)S(1)} %broadcast_select_fusion.2.refs_3_), channel_id=1, source_target_pairs={{0,2},{2,0},{4,6},{6,4},{8,10},{10,8},{12,14},{14,12},{16,18},{18,... | collective-permute-start | bytes 798728 | tf_op jit(solution)/shard_map/ppermute | solution.py:312
  69.6 8.6 %collective-permute-start.3 = (bf16[1040,128]{1,0:T(8,128)(2,1)S(1)}, bf16[1040,128]{1,0:T(8,128)(2,1)S(1)}, u32[]{:S(2)}, u32[]{:S(2)}) collective-permute-start(bf16[1040,128]{1,0:T(8,128)(2,1)S(1)} %slice.8), channel_id=1, source_target_pairs={{0,4},{2,6},{4,0},{6,2},{8,12},{10,14},{12,8},{14,10},{16,20},{18,... | collective-permute-start | bytes 798728 | tf_op jit(solution)/shard_map/ppermute | solution.py:312
  78.3 4.9 %collective-permute-start.8 = (bf16[1040,128]{1,0:T(8,128)(2,1)S(1)}, bf16[1040,128]{1,0:T(8,128)(2,1)S(1)}, u32[]{:S(2)}, u32[]{:S(2)}) collective-permute-start(bf16[1040,128]{1,0:T(8,128)(2,1)S(1)} %collective-permute-done.3.refs_2_), channel_id=1, source_target_pairs={{0,2},{2,0},{4,6},{6,4},{8,10},{10,8},{12,14},{14,12},{16,18},{18,... | collective-permute-start | bytes 798728 | tf_op jit(solution)/shard_map/ppermute | solution.py:312
  83.1 6.7 %copy-start.3 = (bf16[1,2048,768]{2,1,0:T(8,128)(2,1)S(1)}, bf16[1,2048,768]{2,1,0:T(8,128)(2,1)}, u32[]{:S(2)}) copy-start(bf16[1,2048,768]{2,1,0:T(8,128)(2,1)} %param.8) | copy-start | bytes 9437188
  86.9 1.4 %copy-start.6 = (f32[768,768]{1,0:T(8,128)}, f32[768,768]{1,0:T(8,128)S(1)}, u32[]{:S(2)}) copy-start(f32[768,768]{1,0:T(8,128)S(1)} %get-tuple-element.8.refs_1_) | copy-start | bytes 7077892
  88.3 18.2 %collective-permute-start.21 = (bf16[2688,128]{1,0:T(8,128)(2,1)}, bf16[2688,128]{1,0:T(8,128)(2,1)}, u32[]{:S(2)}, u32[]{:S(2)}) collective-permute-start(bf16[2688,128]{1,0:T(8,128)(2,1)} %get-tuple-element.9), channel_id=1, source_target_pairs={{0,1},{1,0},{2,3},{3,2},{4,5},{5,4},{6,7},{7,6},{8,9},{9,8},{10,11... | collective-permute-start | bytes 2064392 | tf_op jit(solution)/shard_map/ppermute | solution.py:393
  89.8 1.2 %copy-start.4 = (bf16[1,2048,256]{2,1,0:T(8,128)(2,1)S(1)}, bf16[1,2048,256]{2,1,0:T(8,128)(2,1)}, u32[]{:S(2)}) copy-start(bf16[1,2048,256]{2,1,0:T(8,128)(2,1)} %param.9) | copy-start | bytes 3145732
  91.1 15.5 %copy-start.7 = (f32[768,768]{1,0:T(8,128)S(1)}, f32[768,768]{1,0:T(8,128)}, u32[]{:S(2)}) copy-start(f32[768,768]{1,0:T(8,128)} %copy-done.6) | copy-start | bytes 7077892

commit v2 on v0

v2 whole, which is shorter than its diff:
```python
import functools

import jax
import jax.numpy as jnp
from jax import lax
from jax.experimental import pallas as pl
from jax.experimental.pallas import tpu as pltpu
from jax.sharding import PartitionSpec as P

TOPK = 8
LANES = 128
ID_ROWS = 16
NT = (((1,), (1,)), ((), ()))
NN = (((1,), (0,)), ((), ()))
TN = (((0,), (0,)), ((), ()))
TT = (((0,), (1,)), ((), ()))
BF16 = jnp.bfloat16
F32 = jnp.float32
VMEM = pl.BlockSpec(memory_space=pltpu.VMEM)
MIB = 1 << 20


def here(array):
    return pltpu.with_memory_space_constraint(array, pltpu.VMEM)


def far(array):
    return pltpu.with_memory_space_constraint(array, pltpu.HBM)


def kept(shape, dtype):
    return pltpu.VMEM(tuple(shape), dtype)


def params(mib):
    return pltpu.CompilerParams(vmem_limit_bytes=mib * MIB)


def half_rows(tok_dev, width):
    return tok_dev // 2 * (width // LANES) + ID_ROWS


def pack_kernel(tokens_hbm, routes_hbm, out_ref, tokens_ref, routes_ref, sems):
    copies = [
        pltpu.make_async_copy(routes_hbm, routes_ref, sems.at[0]),
        pltpu.make_async_copy(tokens_hbm, tokens_ref, sems.at[1]),
    ]
    for copy in copies:
        copy.start()
    for copy in copies:
        copy.wait()
    tok_dev, width = tokens_ref.shape
    top = routes_ref.shape[0]
    half, tiles = tok_dev // 2, width // LANES
    rows = half_rows(tok_dev, width)
    ids = jnp.concatenate(
        [routes_ref[...].astype(F32), jnp.full((ID_ROWS - top, tok_dev), -1.0, F32)], axis=0
    )
    lane = lax.broadcasted_iota(jnp.int32, ids.shape, 1)
    for h in range(2):
        for i in range(half // 16):
            for k in range(tiles):
                at = h * rows + (i * tiles + k) * 16
                out_ref[at : at + 16, :] = tokens_ref[
                    h * half + i * 16 : h * half + (i + 1) * 16, k * LANES : (k + 1) * LANES
                ]
        mine = (lane >= h * half) & (lane < (h + 1) * half)
        out_ref[(h + 1) * rows - ID_ROWS : (h + 1) * rows, :tok_dev] = jnp.where(
            mine, ids, -1.0
        ).astype(BF16)


def pack(tokens, routes):
    tok_dev, width = tokens.shape
    anywhere = pl.BlockSpec(memory_space=pl.ANY)
    return pl.pallas_call(
        pack_kernel,
        out_shape=kept((2 * half_rows(tok_dev, width), LANES), BF16),
        in_specs=[anywhere, anywhere],
        out_specs=VMEM,
        scratch_shapes=[
            pltpu.VMEM(tokens.shape, tokens.dtype),
            pltpu.VMEM(routes.shape, routes.dtype),
            pltpu.SemaphoreType.DMA((2,)),
        ],
        compiler_params=params(2),
        cost_estimate=pl.CostEstimate(flops=0, bytes_accessed=tokens.size * 4, transcendentals=0),
    )(far(tokens), far(routes))


def split(value):
    high = value.astype(BF16)
    return high, (value - high.astype(F32)).astype(BF16)


def product(left, right, dims):
    return lax.dot_general(left, right, dims, preferred_element_type=F32)


def reduce_kernel(w_hbm, sketch_hbm, tie_ref, high_ref, low_ref, tie_out, w_ref, sketch_ref, sems):
    copies = [
        pltpu.make_async_copy(w_hbm, w_ref, sems.at[0]),
        pltpu.make_async_copy(sketch_hbm, sketch_ref, sems.at[1]),
    ]
    for copy in copies:
        copy.start()
    for copy in copies:
        copy.wait()
    high_ref[...], low_ref[...] = split(product(w_ref[...], sketch_ref[...], TN))
    tie_out[...] = jnp.zeros_like(tie_out)


def reduced_first(w_down, sketch, tie):
    half = kept((w_down.shape[1], sketch.shape[1]), BF16)
    anywhere = pl.BlockSpec(memory_space=pl.ANY)
    return pl.pallas_call(
        reduce_kernel,
        out_shape=(half, half, kept(tie.shape, tie.dtype)),
        in_specs=[anywhere, anywhere, VMEM],
        out_specs=(VMEM, VMEM, VMEM),
        scratch_shapes=[
            pltpu.VMEM(w_down.shape, w_down.dtype),
            pltpu.VMEM(sketch.shape, sketch.dtype),
            pltpu.SemaphoreType.DMA((2,)),
        ],
        compiler_params=params(6),
        cost_estimate=pl.CostEstimate(
            flops=2 * w_down.size * sketch.shape[1], bytes_accessed=w_down.size * 2, transcendentals=0
        ),
    )(far(w_down), far(sketch), here(tie))


def nothing_kernel(in_ref, tie_ref, out_ref):
    pass


def after(tie, array):
    return pl.pallas_call(
        nothing_kernel,
        out_shape=kept(array.shape, array.dtype),
        in_specs=[VMEM, VMEM],
        out_specs=VMEM,
        input_output_aliases={0: 0},
        compiler_params=params(2),
        cost_estimate=pl.CostEstimate(flops=0, bytes_accessed=0, transcendentals=0),
    )(here(array), here(tie))


def part_kernel(in_ref, out_ref, *, first):
    out_ref[...] = in_ref[first : first + out_ref.shape[0], :]


def part(array, first, rows):
    return pl.pallas_call(
        functools.partial(part_kernel, first=first),
        out_shape=kept((rows, array.shape[1]), array.dtype),
        in_specs=[VMEM],
        out_specs=VMEM,
        compiler_params=params(2),
        cost_estimate=pl.CostEstimate(flops=0, bytes_accessed=0, transcendentals=0),
    )(here(array))


def right_tiles(count):
    return [(a, b) for a in range(count) for b in range(a + 1, count)]


def packed_rows(count):
    return (len(right_tiles(count)) + (count + 1) // 2) * LANES + ID_ROWS


def tile_places():
    return (
        lax.broadcasted_iota(jnp.int32, (LANES, LANES), 0),
        lax.broadcasted_iota(jnp.int32, (LANES, LANES), 1),
    )


def gram_step(hidden_width):
    return 2 * LANES if hidden_width % (2 * LANES) == 0 else LANES


def pack_gram(gram_ref, packed_ref):
    count = gram_ref.shape[0] // LANES
    rights = right_tiles(count)

    def tile(a, b):
        return gram_ref[a * LANES : (a + 1) * LANES, b * LANES : (b + 1) * LANES]

    for at, (a, b) in enumerate(rights):
        packed_ref[at * LANES : (at + 1) * LANES, :] = tile(a, b).astype(BF16)
    row, column = tile_places()
    strip = jnp.zeros((ID_ROWS, LANES), F32)
    place = lax.broadcasted_iota(jnp.int32, strip.shape, 0)
    for pair in range((count + 1) // 2):
        at = (len(rights) + pair) * LANES
        both = tile(2 * pair, 2 * pair)
        if 2 * pair + 1 < count:
            second = tile(2 * pair + 1, 2 * pair + 1)
            diagonal = jnp.sum(jnp.where(row == column, second, 0.0), axis=0, keepdims=True)
            strip = jnp.where(place == pair, diagonal, strip)
            both = jnp.where(row <= column, both, second)
        packed_ref[at : at + LANES, :] = both.astype(BF16)
    at = (len(rights) + (count + 1) // 2) * LANES
    packed_ref[at : at + ID_ROWS, :] = strip.astype(BF16)


def unpack_gram(packed_ref, full_ref):
    count = full_ref.shape[0] // LANES
    rights = right_tiles(count)

    def put(a, b, value):
        full_ref[a * LANES : (a + 1) * LANES, b * LANES : (b + 1) * LANES] = value.astype(BF16)

    for at, (a, b) in enumerate(rights):
        value = packed_ref[at * LANES : (at + 1) * LANES, :]
        put(a, b, value)
        put(b, a, value.astype(F32).T)
    row, column = tile_places()
    at = (len(rights) + (count + 1) // 2) * LANES
    strip = packed_ref[at : at + ID_ROWS, :].astype(F32)
    for pair in range((count + 1) // 2):
        at = (len(rights) + pair) * LANES
        both = packed_ref[at : at + LANES, :].astype(F32)
        turned = both.T
        put(2 * pair, 2 * pair, jnp.where(row <= column, both, turned))
        if 2 * pair + 1 < count:
            second = jnp.where(row > column, both, turned)
            second = jnp.where(row == column, strip[pair : pair + 1, :], second)
            put(2 * pair + 1, 2 * pair + 1, second)


def ffn_kernel(*refs, tok_dev, width, sources, has_gram, scale):
    operands = 1 + max(max(first[0], second[0]) for first, second in sources)
    weight_ref, pieces = refs[0], refs[1 : 1 + operands]
    rest = list(refs[1 + operands :])
    gram_in = rest.pop(0) if has_gram else None
    gram_out = rest.pop(0)
    last_out = rest.pop(0)
    x_ref, mask_ref, hidden_ref = rest
    half, tiles = tok_dev // 2, width // LANES
    expert = lax.axis_index("expert").astype(F32)
    for b, block in enumerate(sources):
        hits = None
        for h, (operand, first) in enumerate(block):
            piece = pieces[operand]
            for i in range(half // 16):
                for k in range(tiles):
                    at = first + (i * tiles + k) * 16
                    row = b * tok_dev + h * half + i * 16
                    x_ref[row : row + 16, k * LANES : (k + 1) * LANES] = piece[at : at + 16, :]
            at = first + half * tiles
            found = (piece[at : at + ID_ROWS, :tok_dev].astype(F32) == expert).astype(F32)
            hits = found if hits is None else hits + found
        mask_ref[0:1, b * tok_dev : (b + 1) * tok_dev] = jnp.max(hits, axis=0, keepdims=True)
    hidden_width = weight_ref.shape[1] // 2
    step_rows = gram_step(hidden_width)

    gate = product(weight_ref[:, :hidden_width], x_ref[...], TT)
    up = product(weight_ref[:, hidden_width:], x_ref[...], TT)
    hidden_ref[...] = (gate / (1.0 + jnp.exp(-gate)) * up * mask_ref[0:1, :]).astype(BF16)
    for first in range(0, hidden_width, step_rows):
        rows = slice(first, first + step_rows)
        part = product(hidden_ref[rows, :], hidden_ref[first:, :], NT)
        if has_gram:
            part += gram_in[rows, first:]
        if scale is not None:
            part *= scale
        gram_out[rows, first:] = part
    if scale is not None:
        pack_gram(gram_out, last_out)
    else:
        last_out[...] = jnp.zeros_like(last_out)


def ffn(weights, pieces, sources, gram, tok_dev, scale=None):
    hidden_width, width = weights.shape[1] // 2, weights.shape[0]
    rows = tok_dev * len(sources)
    if scale is None:
        last = kept((8, LANES), F32)
    else:
        last = kept((packed_rows(hidden_width // LANES), LANES), BF16)
    operands = [weights, *pieces] + ([] if gram is None else [gram])
    return pl.pallas_call(
        functools.partial(
            ffn_kernel,
            tok_dev=tok_dev,
            width=width,
            sources=sources,
            has_gram=gram is not None,
            scale=scale,
        ),
        out_shape=(kept((hidden_width, hidden_width), F32), last),
        in_specs=[VMEM] * len(operands),
        out_specs=(VMEM, VMEM),
        input_output_aliases={} if gram is None else {len(operands) - 1: 0},
        scratch_shapes=[
            pltpu.VMEM((rows, width), BF16),
            pltpu.VMEM((8, rows), F32),
            pltpu.VMEM((hidden_width, rows), BF16),
        ],
        compiler_params=params(8),
        cost_estimate=pl.CostEstimate(
            flops=4 * rows * hidden_width * (2 * width + hidden_width),
            bytes_accessed=weights.size * 2 + rows * width * 2,
            transcendentals=rows * hidden_width,
        ),
    )(*map(here, operands))


def exact(high, low, other_high, other_low):
    total = product(low, other_high, NN)
    total += product(high, other_low, NN)
    return total + product(high, other_high, NN)


def own_kernel(own_ref, high_ref, low_ref, w_hbm, full_ref, panel_ref, w_ref, sem):
    copy = pltpu.make_async_copy(w_hbm, w_ref, sem)
    copy.start()
    count = own_ref.shape[0] // LANES
    for a in range(count):
        for b in range(a, count):
            rows, columns = slice(a * LANES, (a + 1) * LANES), slice(b * LANES, (b + 1) * LANES)
            tile = own_ref[rows, columns]
            full_ref[rows, columns] = tile
            if a != b:
                full_ref[columns, rows] = tile.T
    for first in range(0, own_ref.shape[0], 2 * LANES):
        rows = slice(first, min(first + 2 * LANES, own_ref.shape[0]))
        high, low = split(full_ref[rows, :])
        panel_ref[rows, :] = exact(high, low, high_ref[...], low_ref[...])
    copy.wait()


def own_side(own, high, low, w_down):
    hidden_width, rank = high.shape
    return pl.pallas_call(
        own_kernel,
        out_shape=(
            kept((hidden_width, hidden_width), F32),
            kept((hidden_width, rank), F32),
            kept(w_down.shape, w_down.dtype),
        ),
        in_specs=[VMEM] * 3 + [pl.BlockSpec(memory_space=pl.ANY)],
        out_specs=(VMEM, VMEM, VMEM),
        scratch_shapes=[pltpu.SemaphoreType.DMA],
        compiler_params=params(4),
        cost_estimate=pl.CostEstimate(
            flops=6 * hidden_width * hidden_width * rank,
            bytes_accessed=w_down.size * 2,
            transcendentals=0,
        ),
    )(here(own), here(high), here(low), far(w_down))


def power_kernel(*refs, has_other):
    refs = list(refs)
    own_ref, panel_ref = refs[:2]
    other_ref = refs.pop(2) if has_other else None
    first_high, first_low, w_ref, gram_out, power_out = refs[2:7]
    full_ref, other_full, high_ref, low_ref, image_ref, probe_ref, power_ref, sems = refs[7:]
    group = lax.axis_index("group")
    hidden_width = full_ref.shape[0]
    panel = panel_ref[...]
    if has_other:
        unpack_gram(other_ref, other_full)
        panel += product(other_full[...], first_low[...], NN)
        panel += product(other_full[...], first_high[...], NN)
    image_ref[...] = product(w_ref[...], panel.astype(BF16), NN)
    for first in range(0, hidden_width, LANES):
        rows = slice(first, first + LANES)
        full = own_ref[rows, :]
        if has_other:
            full += other_full[rows, :].astype(F32)
        full_ref[rows, :] = full
        high_ref[rows, :], low_ref[rows, :] = split(full)
    panel_rows = gram_out.shape[0]
    gram_copy = pltpu.make_async_copy(
        full_ref.at[pl.ds(pl.multiple_of(group * panel_rows, panel_rows), panel_rows), :],
        gram_out,
        sems.at[0],
    )
    gram_copy.start()
    image = image_ref[...]
    mean = jnp.sum(image * image, axis=0, keepdims=True) * (1.0 / image.shape[0])
    probe_ref[...] = (image * lax.rsqrt(mean + 1e-06)).astype(BF16)
    high, low = split(product(w_ref[...], probe_ref[...], TN))
    panel = exact(high_ref[...], low_ref[...], high, low).astype(BF16)
    own_rows = power_ref.shape[0]
    chunk = min(own_rows, 4 * LANES)
    copies = []
    for at, first in enumerate(range(0, own_rows, chunk)):
        rows = pl.ds(pl.multiple_of(group * own_rows + first, chunk), chunk)
        power_ref[first : first + chunk, :] = product(w_ref[rows, :], panel, NN)
        copies.append(
            pltpu.make_async_copy(
                power_ref.at[first : first + chunk, :],
                power_out.at[first : first + chunk, :],
                sems.at[1 + at],
            )
        )
        copies[-1].start()
    gram_copy.wait()
    for copy in copies:
        copy.wait()


def power(own, other, panel, reduced, w_down, group_count):
    width, hidden_width = w_down.shape
    rank = panel.shape[1]
    own_rows = width // group_count
    operands = [own, panel] + ([] if other is None else [other])
    operands += [*reduced, w_down]
    anywhere = pl.BlockSpec(memory_space=pl.ANY)
    return pl.pallas_call(
        functools.partial(power_kernel, has_other=other is not None),
        out_shape=(
            jax.ShapeDtypeStruct((hidden_width // group_count, hidden_width), F32),
            jax.ShapeDtypeStruct((own_rows, rank), F32),
        ),
        in_specs=[VMEM] * len(operands),
        out_specs=(anywhere, anywhere),
        scratch_shapes=[
            pltpu.VMEM((hidden_width, hidden_width), F32),
            pltpu.VMEM((hidden_width, hidden_width), BF16),
            pltpu.VMEM((hidden_width, hidden_width), BF16),
            pltpu.VMEM((hidden_width, hidden_width), BF16),
            pltpu.VMEM((width, rank), F32),
            pltpu.VMEM((width, rank), BF16),
            pltpu.VMEM((own_rows, rank), F32),
            pltpu.SemaphoreType.DMA((1 + own_rows // min(own_rows, 4 * LANES),)),
        ],
        compiler_params=params(12),
        cost_estimate=pl.CostEstimate(
            flops=2 * rank * (6 * hidden_width * hidden_width + 3 * width * hidden_width),
            bytes_accessed=w_down.size * 4,
            transcendentals=0,
        ),
    )(*map(here, operands))


def whole(rows, at_operand):
    return ((at_operand, 0), (at_operand, rows))


def ring_order(chips, across):
    depth = chips // across
    if across < 2 or depth % 2 or depth * across != chips:
        return list(range(chips))
    order = []
    for z in range(depth):
        row = range(1, across) if z % 2 == 0 else range(across - 1, 0, -1)
        order += [z * across + y for y in row]
    return order + [z * across for z in reversed(range(depth))]


def gram_of_all(block, weights, tok_dev, scale, order, prepare):
    chips, rows = len(order), block.shape[0] // 2
    onward = [
        (2 * order[i] + core, 2 * order[(i + 1) % chips] + core)
        for i in range(chips)
        for core in range(2)
    ]
    backward = [(b, a) for a, b in onward]
    sibling = [(i, i ^ 1) for i in range(2 * chips)]

    def send(array, pairs):
        return lax.ppermute(array, "expert", pairs)

    right = left = block
    pieces, gram, tie = [block], None, None
    for step in range(1, (chips + 1) // 2):
        if tie is not None:
            right, left = after(tie, right), after(tie, left)
            pieces = [right, left]
        next_right, next_left = send(right, onward), send(left, backward)
        pieces += [send(piece, sibling) for piece in pieces]
        sources = [whole(rows, i) for i in range(len(pieces))]
        gram, tie = ffn(weights, pieces, sources, gram, tok_dev)
        if step == 1:
            *reduced, tie = prepare(tie)
        right, left = next_right, next_left
    last = [((0, 0), (1, 0)), ((2, 0), (3, 0))]
    if chips % 2 == 0:
        pieces = [block]
        if tie is not None:
            right, left = after(tie, right), after(tie, left)
            pieces = [right, left]
        next_right = send(part(right, 0, rows), onward)
        next_left = send(part(left, rows, rows), backward)
        pieces += [send(piece, sibling) for piece in pieces]
        sources = [whole(rows, i) for i in range(len(pieces))]
        gram, tie = ffn(weights, pieces, sources, gram, tok_dev)
        right, left = after(tie, next_right), after(tie, next_left)
    else:
        last = [whole(rows, i) for i in range(4)]
    pieces = [right, left, send(right, sibling), send(left, sibling)]
    return *ffn(weights, pieces, last, gram, tok_dev, scale), reduced


def on_device(tokens, routes, gate_up, down_weight, sketch):
    owner_count = lax.axis_size("expert")
    group_count = lax.axis_size("group")
    tok_dev = tokens.shape[1]
    order = ring_order(owner_count // 2, group_count)
    scale = 1.0 / (tok_dev * TOPK * group_count)
    block = pack(tokens[0], routes[0].T)
    w_down = down_weight[0]
    own, packed, reduced = gram_of_all(
        block,
        gate_up[0],
        tok_dev,
        scale,
        order,
        functools.partial(reduced_first, w_down, sketch[0]),
    )
    if group_count == 2:
        other = lax.ppermute(packed, "group", [(0, 1), (1, 0)])
    else:
        own, other = lax.psum(own, "group"), None
    own, panel, w_down = own_side(own, *reduced, w_down)
    gram, result = power(own, other, panel, reduced, w_down, group_count)
    return gram[None], result[None]


def solution(mesh):
    return jax.shard_map(
        on_device,
        mesh=mesh,
        in_specs=(
            P("group", "expert", None),
            P("group", "expert", None),
            P("expert", None, None),
            P("expert", None, None),
            P("expert", None, None),
        ),
        out_specs=(P("expert", "group", None), P("expert", "group", None)),
        check_vma=False,
    )
```

time: 301 us -> 88.9 us (0.30)
  blocking collectives: 159 us -> 0 us
  Pallas kernels: 0 us -> 33 us
  matrix products: 27.4 us -> 0 us
  waiting for transfers between devices: 66.5 us -> 40.6 us
  local copies, waits for them, and re-layouts: 27.9 us -> 2.79 us
  between operations: 14.1 us -> 0.89 us
  starting transfers between devices: 0.04 us -> 11.4 us
  other arithmetic: 5.54 us -> 0 us
    all_to_all x1 -> x0, blocking collectives: 145 us -> none  [on_device(): lax.all_to_all(outgoing, 'expert', split_axis=0, concat_axis=0, tiled=True)]
    psum x1 -> x0, waiting for transfers between devices: 66.5 us -> none  [on_device(): summed = lax.psum(local_gram, 'group')]
    ppermute x0 -> x18, waiting for transfers between devices: none -> 40.6 us  [the longest x17 28.5 us: send(): return lax.ppermute(array, 'expert', pairs)]
    pallas_call x0 -> x19, Pallas kernels: none -> 33 us  [the longest x5 18.4 us: ffn(): pl.pallas_call(functools.partial(ffn_kernel, tok_dev=tok_dev, width=width...]
    dot_general x8 -> x0, matrix products: 27.4 us -> none  [the longest x1 12.3 us: on_device(): jnp.einsum('scd,df->scf', lax.all_to_all(outgoing, 'expert', split_axis=0...]
    scatter x1 -> x0, local copies, waits for them, and re-layouts: 24.7 us -> none  [on_device(): outgoing = outgoing.at[destination].set(tokens[0][source_row]).reshape(ow...]
    all_gather x2 -> x0, blocking collectives: 14 us -> none  [fold_image(): lax.all_gather(panel_bf, 'group', axis=0, tiled=True)]
    ppermute x0 -> x18, starting transfers between devices: none -> 11.4 us  [the longest x17 9.89 us: send(): return lax.ppermute(array, 'expert', pairs)]
  transfers between devices with their start and end apart: 1 -> 18, of which waited for: 1 -> 10; matrix products, arithmetic and copies ran while one was open for 1% -> 0% of each run, Pallas kernels for 0% -> 23%
where the time goes in v2:
time: 88.9 us; the launch traced here: 88.7 us
  waiting for transfers between devices  40.6 us (46%)
  Pallas kernels  33 us (37%)
  starting transfers between devices  11.4 us (13%)
  local copies, waits for them, and re-layouts  2.79 us (3%)
  between operations  0.89 us (1%)
    ppermute x17, waiting for transfers between devices, send(): return lax.ppermute(array, 'expert', pairs)  28.5 us
    pallas_call x5, Pallas kernels, ffn(): pl.pallas_call(functools.partial(ffn_kernel, tok_dev=tok_dev, width=width...  18.4 us
    ppermute x1, waiting for transfers between devices, on_device(): other = lax.ppermute(packed, 'group', [(0, 1), (1, 0)])  12.1 us
    ppermute x17, starting transfers between devices, send(): return lax.ppermute(array, 'expert', pairs)  9.89 us
    pallas_call x1, Pallas kernels, power(): pl.pallas_call(functools.partial(power_kernel, has_other=other is not Non...  8.26 us
    pallas_call x1, Pallas kernels, reduced_first(): pl.pallas_call(reduce_kernel, out_shape=(half, half, kept(tie.shape, tie....  3.22 us
    unnamed x2, local copies, waits for them, and re-layouts  2.79 us
    pallas_call x1, Pallas kernels, own_side(): pl.pallas_call(own_kernel, out_shape=(kept((hidden_width, hidden_width),...  1.91 us
  transfers between devices with their start and end apart: 18, of which 10 were waited for; matrix products, arithmetic and copies ran while one was open for 0% of the time, Pallas kernels for 23%

profile of v2, /device:TPU:0, one launch (start us, length us, event | category | flops | bytes accessed | tf_op | source)
XLA Modules:
  0.0 88.7 jit_solution(13683737063813669164)
XLA Ops:
  0.6 1.2 %shard_map.68.refs_1_ = bf16[2080,128]{1,0:T(8,128)(2,1)S(1)} custom-call(bf16[128,2048]{1,0:T(8,128)(2,1)} %bitcast.17, s32[8,128]{1,0:T(8,128)} %bitcast.18), custom_call_target="tpu_custom_call" | custom-call | bytes 1048576 | tf_op jit(solution)/shard_map/pallas_call | solution.py:76
  1.8 0.5 collective-permute-start.1
  2.3 2.6 %collective-permute-start = (bf16[2080,128]{1,0:T(8,128)(2,1)S(1)}, bf16[2080,128]{1,0:T(8,128)(2,1)S(1)}, u32[]{:S(2)}, u32[]{:S(2)}) collective-permute-start(bf16[2080,128]{1,0:T(8,128)(2,1)S(1)} %shard_map.68.refs_1_), channel_id=1, source_target_pairs={{4,12},{6,14},{12,20},{14,22},{20,28},{22,30},{28,24},{30,26},{24,... | collective-permute-start | bytes 1597448 | tf_op jit(solution)/shard_map/ppermute | solution.py:468
  4.9 0.1 collective-permute-start.3
  5.0 0.0 collective-permute-done.1.refs_2_
  5.0 0.0 copy-start
  5.0 2.8 %copy-done = bf16[1,2048,1536]{2,1,0:T(8,128)(2,1)S(1)} copy-done((bf16[1,2048,1536]{2,1,0:T(8,128)(2,1)S(1)}, bf16[1,2048,1536]{2,1,0:T(8,128)(2,1)}, u32[]{:S(2)}) %copy-start) | copy-done | bytes 6291480
  7.8 2.3 %shard_map.69 = (f32[768,768]{1,0:T(8,128)S(1)}, f32[8,128]{1,0:T(8,128)S(1)}) custom-call(bf16[2048,1536]{1,0:T(8,128)(2,1)S(1)} %bitcast.9, bf16[2080,128]{1,0:T(8,128)(2,1)S(1)} %shard_map.68.refs_1_, bf16[2080,128]{1,0:T(8,128)(2,1)S(1)} %collective-permute-done.1.refs_2_), custom_call_target="tpu_custom_call" | custom-call | flops 3825205248 | bytes 7340032 | tf_op jit(solution)/shard_map/pallas_call | solution.py:284
  10.1 3.2 %shard_map.70 = (bf16[768,256]{1,0:T(8,128)(2,1)S(1)}, bf16[768,256]{1,0:T(8,128)(2,1)S(1)}, f32[8,128]{1,0:T(8,128)S(1)}) custom-call(bf16[2048,768]{1,0:T(8,128)(2,1)} %bitcast.14, bf16[2048,256]{1,0:T(8,128)(2,1)} %bitcast.16, f32[8,128]{1,0:T(8,128)S(1)} %get-tuple-element.20.tie_ref), custom_call_target="tpu_custom_call" | custom-call | flops 805306368 | bytes 3145728 | tf_op jit(solution)/shard_map/pallas_call | solution.py:116
  13.4 4.3 %collective-permute-done.in_ref = bf16[2080,128]{1,0:T(8,128)(2,1)S(1)} collective-permute-done((bf16[2080,128]{1,0:T(8,128)(2,1)S(1)}, bf16[2080,128]{1,0:T(8,128)(2,1)S(1)}, u32[]{:S(2)}, u32[]{:S(2)}) %collective-permute-start) | collective-permute-done | bytes 532512 | tf_op jit(solution)/shard_map/ppermute | solution.py:468
  17.7 0.0 collective-permute-start.4
  17.7 1.4 %collective-permute-done.3.in_ref = bf16[2080,128]{1,0:T(8,128)(2,1)S(1)} collective-permute-done((bf16[2080,128]{1,0:T(8,128)(2,1)S(1)}, bf16[2080,128]{1,0:T(8,128)(2,1)S(1)}, u32[]{:S(2)}, u32[]{:S(2)}) %collective-permute-start.3) | collective-permute-done | bytes 532512 | tf_op jit(solution)/shard_map/ppermute | solution.py:468
  19.1 0.0 collective-permute-start.5
  19.1 1.6 %collective-permute-start.2 = (bf16[2080,128]{1,0:T(8,128)(2,1)S(1)}, bf16[2080,128]{1,0:T(8,128)(2,1)S(1)}, u32[]{:S(2)}, u32[]{:S(2)}) collective-permute-start(bf16[2080,128]{1,0:T(8,128)(2,1)S(1)} %shard_map.71.refs_1_), channel_id=1, source_target_pairs={{4,12},{6,14},{12,20},{14,22},{20,28},{22,30},{28,24},{30,26},{24,... | collective-permute-start | bytes 1597448 | tf_op jit(solution)/shard_map/ppermute | solution.py:468
  20.6 0.4 collective-permute-start.7
  21.1 0.0 collective-permute-done.4.refs_3_
  21.1 0.0 collective-permute-done.5.refs_4_
  21.1 4.4 %shard_map.73 = (f32[768,768]{1,0:T(8,128)S(1)}, f32[8,128]{1,0:T(8,128)S(1)}) custom-call(bf16[2048,1536]{1,0:T(8,128)(2,1)S(1)} %bitcast.10, bf16[2080,128]{1,0:T(8,128)(2,1)S(1)} %shard_map.71.refs_1_, bf16[2080,128]{1,0:T(8,128)(2,1)S(1)} %shard_map.72.refs_2_, ...), custom_call_target="tpu_custom_call", output_to_operand_aliasing={{0}: (5, {})} | custom-call | flops 7650410496 | bytes 8388608 | tf_op jit(solution)/shard_map/pallas_call | solution.py:284
  25.5 8.1 %collective-permute-done.2.in_ref = bf16[2080,128]{1,0:T(8,128)(2,1)S(1)} collective-permute-done((bf16[2080,128]{1,0:T(8,128)(2,1)S(1)}, bf16[2080,128]{1,0:T(8,128)(2,1)S(1)}, u32[]{:S(2)}, u32[]{:S(2)}) %collective-permute-start.2) | collective-permute-done | bytes 532512 | tf_op jit(solution)/shard_map/ppermute | solution.py:468
  33.6 0.0 collective-permute-start.8
  33.6 1.3 %collective-permute-done.7.in_ref = bf16[2080,128]{1,0:T(8,128)(2,1)S(1)} collective-permute-done((bf16[2080,128]{1,0:T(8,128)(2,1)S(1)}, bf16[2080,128]{1,0:T(8,128)(2,1)S(1)}, u32[]{:S(2)}, u32[]{:S(2)}) %collective-permute-start.7) | collective-permute-done | bytes 532512 | tf_op jit(solution)/shard_map/ppermute | solution.py:468
  34.9 0.0 collective-permute-start.9
  34.9 1.6 %collective-permute-start.6 = (bf16[2080,128]{1,0:T(8,128)(2,1)S(1)}, bf16[2080,128]{1,0:T(8,128)(2,1)S(1)}, u32[]{:S(2)}, u32[]{:S(2)}) collective-permute-start(bf16[2080,128]{1,0:T(8,128)(2,1)S(1)} %shard_map.74.refs_1_), channel_id=1, source_target_pairs={{4,12},{6,14},{12,20},{14,22},{20,28},{22,30},{28,24},{30,26},{24,... | collective-permute-start | bytes 1597448 | tf_op jit(solution)/shard_map/ppermute | solution.py:468
  36.5 0.4 collective-permute-start.11
  36.9 0.0 collective-permute-done.8.refs_3_
  36.9 0.0 collective-permute-done.9.refs_4_
  36.9 4.4 %shard_map.76 = (f32[768,768]{1,0:T(8,128)S(1)}, f32[8,128]{1,0:T(8,128)S(1)}) custom-call(bf16[2048,1536]{1,0:T(8,128)(2,1)S(1)} %bitcast.11, bf16[2080,128]{1,0:T(8,128)(2,1)S(1)} %shard_map.74.refs_1_, bf16[2080,128]{1,0:T(8,128)(2,1)S(1)} %shard_map.75.refs_2_, ...), custom_call_target="tpu_custom_call", output_to_operand_aliasing={{0}: (5, {})} | custom-call | flops 7650410496 | bytes 8388608 | tf_op jit(solution)/shard_map/pallas_call | solution.py:284
  41.3 8.1 %collective-permute-done.6.in_ref = bf16[2080,128]{1,0:T(8,128)(2,1)S(1)} collective-permute-done((bf16[2080,128]{1,0:T(8,128)(2,1)S(1)}, bf16[2080,128]{1,0:T(8,128)(2,1)S(1)}, u32[]{:S(2)}, u32[]{:S(2)}) %collective-permute-start.6) | collective-permute-done | bytes 532512 | tf_op jit(solution)/shard_map/ppermute | solution.py:468
  49.4 0.0 collective-permute-start.12
  49.4 1.3 %collective-permute-done.11.in_ref = bf16[2080,128]{1,0:T(8,128)(2,1)S(1)} collective-permute-done((bf16[2080,128]{1,0:T(8,128)(2,1)S(1)}, bf16[2080,128]{1,0:T(8,128)(2,1)S(1)}, u32[]{:S(2)}, u32[]{:S(2)}) %collective-permute-start.11) | collective-permute-done | bytes 532512 | tf_op jit(solution)/shard_map/ppermute | solution.py:468
  50.7 0.0 collective-permute-start.13
  50.7 0.5 collective-permute-start.14
  51.3 1.6 %collective-permute-start.10 = (bf16[1040,128]{1,0:T(8,128)(2,1)S(1)}, bf16[1040,128]{1,0:T(8,128)(2,1)S(1)}, u32[]{:S(2)}, u32[]{:S(2)}) collective-permute-start(bf16[1040,128]{1,0:T(8,128)(2,1)S(1)} %shard_map.78), channel_id=1, source_target_pairs={{4,12},{6,14},{12,20},{14,22},{20,28},{22,30},{28,24},{30,26},{24,... | collective-permute-start | bytes 798728 | tf_op jit(solution)/shard_map/ppermute | solution.py:468
  52.8 0.0 collective-permute-done.12.refs_3_
  52.8 0.0 collective-permute-done.13.refs_4_
  52.8 4.4 %shard_map.80 = (f32[768,768]{1,0:T(8,128)S(1)}, f32[8,128]{1,0:T(8,128)S(1)}) custom-call(bf16[2048,1536]{1,0:T(8,128)(2,1)S(1)} %bitcast.12, bf16[2080,128]{1,0:T(8,128)(2,1)S(1)} %shard_map.77.in_ref.refs_1_, bf16[2080,128]{1,0:T(8,128)(2,1)S(1)} %shard_map.79.refs_2_.in_ref, ...), custom_call_target="tpu_custom_call", output_to_operand_aliasing={{0}: (5, {})} | custom-call | flops 7650410496 | bytes 8388608 | tf_op jit(solution)/shard_map/pallas_call | solution.py:284
  57.2 2.6 %collective-permute-done.10.in_ref = bf16[1040,128]{1,0:T(8,128)(2,1)S(1)} collective-permute-done((bf16[1040,128]{1,0:T(8,128)(2,1)S(1)}, bf16[1040,128]{1,0:T(8,128)(2,1)S(1)}, u32[]{:S(2)}, u32[]{:S(2)}) %collective-permute-start.10) | collective-permute-done | bytes 266272 | tf_op jit(solution)/shard_map/ppermute | solution.py:468
  59.9 0.0 collective-permute-start.15
  59.9 0.0 collective-permute-done.14.in_ref
  59.9 0.5 collective-permute-start.16
  60.4 1.0 %collective-permute-done.15.refs_3_ = bf16[1040,128]{1,0:T(8,128)(2,1)S(1)} collective-permute-done((bf16[1040,128]{1,0:T(8,128)(2,1)S(1)}, bf16[1040,128]{1,0:T(8,128)(2,1)S(1)}, u32[]{:S(2)}, u32[]{:S(2)}) %collective-permute-start.15) | collective-permute-done | bytes 266272 | tf_op jit(solution)/shard_map/ppermute | solution.py:468
  61.4 0.4 collective-permute-done.16.refs_4_
  61.8 2.9 %shard_map.84 = (f32[768,768]{1,0:T(8,128)S(1)}, bf16[2320,128]{1,0:T(8,128)(2,1)S(1)}) custom-call(bf16[2048,1536]{1,0:T(8,128)(2,1)S(1)} %bitcast.13, bf16[1040,128]{1,0:T(8,128)(2,1)S(1)} %shard_map.81.refs_1_, bf16[1040,128]{1,0:T(8,128)(2,1)S(1)} %shard_map.83.refs_2_, ...), custom_call_target="tpu_custom_call", output_to_operand_aliasing={{0}: (5, {})} | custom-call | flops 3825205248 | bytes 7340032 | tf_op jit(solution)/shard_map/pallas_call | solution.py:284
  64.7 1.6 %collective-permute-start.17 = (bf16[2320,128]{1,0:T(8,128)(2,1)S(1)}, bf16[2320,128]{1,0:T(8,128)(2,1)S(1)}, u32[]{:S(2)}, u32[]{:S(2)}) collective-permute-start(bf16[2320,128]{1,0:T(8,128)(2,1)S(1)} %get-tuple-element.34), channel_id=1, source_target_pairs={{0,1},{1,0},{2,3},{3,2},{4,5},{5,4},{6,7},{7,6},{8,9},{9,8},{10,11... | collective-permute-start | bytes 1781768 | tf_op jit(solution)/shard_map/ppermute | solution.py:518
  66.3 1.9 %shard_map.85 = (f32[768,768]{1,0:T(8,128)S(1)}, f32[768,256]{1,0:T(8,128)S(1)}, bf16[2048,768]{1,0:T(8,128)(2,1)S(1)}) custom-call(f32[768,768]{1,0:T(8,128)S(1)} %get-tuple-element.29.own_ref, bf16[768,256]{1,0:T(8,128)(2,1)S(1)} %get-tuple-element.30.high_ref.refs_3_, bf16[768,256]{1,0:T(8,128)(2,1)S(1)} %get-tuple-element.31.low_ref.refs_4_, ...), custom_call_target="tpu_custom_call" | custom-call | flops 905969664 | bytes 3145728 | tf_op jit(solution)/shard_map/pallas_call | solution.py:337
  68.2 12.1 %collective-permute-done.17.refs_2_ = bf16[2320,128]{1,0:T(8,128)(2,1)S(1)} collective-permute-done((bf16[2320,128]{1,0:T(8,128)(2,1)S(1)}, bf16[2320,128]{1,0:T(8,128)(2,1)S(1)}, u32[]{:S(2)}, u32[]{:S(2)}) %collective-permute-start.17) | collective-permute-done | bytes 593952 | tf_op jit(solution)/shard_map/ppermute | solution.py:518
  80.2 8.3 %shard_map.86 = (f32[384,768]{1,0:T(8,128)}, f32[1024,256]{1,0:T(8,128)}) custom-call(f32[768,768]{1,0:T(8,128)S(1)} %get-tuple-element.32.refs_0_, f32[768,256]{1,0:T(8,128)S(1)} %get-tuple-element.33.refs_1_, bf16[2320,128]{1,0:T(8,128)(2,1)S(1)} %collective-permute-done.17.refs_2_, bf16[768,256]{1,0:T(8,128)(2,1)S(1)} %get-tuple-element.30.high_ref.refs_3_, ...), custom_call_target="tpu_custom_call" | custom-call | flops 4227858432 | bytes 6291456 | tf_op jit(solution)/shard_map/pallas_call | solution.py:415
  (10 shorter events, 0.0 us)
Async XLA Ops:
  1.8 3.2 %collective-permute-start.1 = (bf16[2080,128]{1,0:T(8,128)(2,1)S(1)}, bf16[2080,128]{1,0:T(8,128)(2,1)S(1)}, u32[]{:S(2)}, u32[]{:S(2)}) collective-permute-start(bf16[2080,128]{1,0:T(8,128)(2,1)S(1)} %shard_map.68.refs_1_), channel_id=1, source_target_pairs={{0,2},{2,0},{4,6},{6,4},{8,10},{10,8},{12,14},{14,12},{16,18},{18,... | collective-permute-start | bytes 1597448 | tf_op jit(solution)/shard_map/ppermute | solution.py:468
  2.3 15.3 %collective-permute-start = (bf16[2080,128]{1,0:T(8,128)(2,1)S(1)}, bf16[2080,128]{1,0:T(8,128)(2,1)S(1)}, u32[]{:S(2)}, u32[]{:S(2)}) collective-permute-start(bf16[2080,128]{1,0:T(8,128)(2,1)S(1)} %shard_map.68.refs_1_), channel_id=1, source_target_pairs={{4,12},{6,14},{12,20},{14,22},{20,28},{22,30},{28,24},{30,26},{24,... | collective-permute-start | bytes 1597448 | tf_op jit(solution)/shard_map/ppermute | solution.py:468
  4.9 14.2 %collective-permute-start.3 = (bf16[2080,128]{1,0:T(8,128)(2,1)S(1)}, bf16[2080,128]{1,0:T(8,128)(2,1)S(1)}, u32[]{:S(2)}, u32[]{:S(2)}) collective-permute-start(bf16[2080,128]{1,0:T(8,128)(2,1)S(1)} %shard_map.68.refs_1_), channel_id=1, source_target_pairs={{12,4},{14,6},{20,12},{22,14},{28,20},{30,22},{24,28},{26,30},{16,... | collective-permute-start | bytes 1597448 | tf_op jit(solution)/shard_map/ppermute | solution.py:468
  5.0 2.8 %copy-start = (bf16[1,2048,1536]{2,1,0:T(8,128)(2,1)S(1)}, bf16[1,2048,1536]{2,1,0:T(8,128)(2,1)}, u32[]{:S(2)}) copy-start(bf16[1,2048,1536]{2,1,0:T(8,128)(2,1)} %param.7) | copy-start | bytes 18874372
  17.7 3.4 %collective-permute-start.4 = (bf16[2080,128]{1,0:T(8,128)(2,1)S(1)}, bf16[2080,128]{1,0:T(8,128)(2,1)S(1)}, u32[]{:S(2)}, u32[]{:S(2)}) collective-permute-start(bf16[2080,128]{1,0:T(8,128)(2,1)S(1)} %shard_map.71.refs_1_), channel_id=1, source_target_pairs={{0,2},{2,0},{4,6},{6,4},{8,10},{10,8},{12,14},{14,12},{16,18},{18,... | collective-permute-start | bytes 1597448 | tf_op jit(solution)/shard_map/ppermute | solution.py:468
  19.1 2.0 %collective-permute-start.5 = (bf16[2080,128]{1,0:T(8,128)(2,1)S(1)}, bf16[2080,128]{1,0:T(8,128)(2,1)S(1)}, u32[]{:S(2)}, u32[]{:S(2)}) collective-permute-start(bf16[2080,128]{1,0:T(8,128)(2,1)S(1)} %shard_map.72.refs_2_), channel_id=1, source_target_pairs={{0,2},{2,0},{4,6},{6,4},{8,10},{10,8},{12,14},{14,12},{16,18},{18,... | collective-permute-start | bytes 1597448 | tf_op jit(solution)/shard_map/ppermute | solution.py:468
  19.1 14.5 %collective-permute-start.2 = (bf16[2080,128]{1,0:T(8,128)(2,1)S(1)}, bf16[2080,128]{1,0:T(8,128)(2,1)S(1)}, u32[]{:S(2)}, u32[]{:S(2)}) collective-permute-start(bf16[2080,128]{1,0:T(8,128)(2,1)S(1)} %shard_map.71.refs_1_), channel_id=1, source_target_pairs={{4,12},{6,14},{12,20},{14,22},{20,28},{22,30},{28,24},{30,26},{24,... | collective-permute-start | bytes 1597448 | tf_op jit(solution)/shard_map/ppermute | solution.py:468
  20.6 14.2 %collective-permute-start.7 = (bf16[2080,128]{1,0:T(8,128)(2,1)S(1)}, bf16[2080,128]{1,0:T(8,128)(2,1)S(1)}, u32[]{:S(2)}, u32[]{:S(2)}) collective-permute-start(bf16[2080,128]{1,0:T(8,128)(2,1)S(1)} %shard_map.72.refs_2_), channel_id=1, source_target_pairs={{12,4},{14,6},{20,12},{22,14},{28,20},{30,22},{24,28},{26,30},{16,... | collective-permute-start | bytes 1597448 | tf_op jit(solution)/shard_map/ppermute | solution.py:468
  33.6 3.3 %collective-permute-start.8 = (bf16[2080,128]{1,0:T(8,128)(2,1)S(1)}, bf16[2080,128]{1,0:T(8,128)(2,1)S(1)}, u32[]{:S(2)}, u32[]{:S(2)}) collective-permute-start(bf16[2080,128]{1,0:T(8,128)(2,1)S(1)} %shard_map.74.refs_1_), channel_id=1, source_target_pairs={{0,2},{2,0},{4,6},{6,4},{8,10},{10,8},{12,14},{14,12},{16,18},{18,... | collective-permute-start | bytes 1597448 | tf_op jit(solution)/shard_map/ppermute | solution.py:468
  34.9 2.0 %collective-permute-start.9 = (bf16[2080,128]{1,0:T(8,128)(2,1)S(1)}, bf16[2080,128]{1,0:T(8,128)(2,1)S(1)}, u32[]{:S(2)}, u32[]{:S(2)}) collective-permute-start(bf16[2080,128]{1,0:T(8,128)(2,1)S(1)} %shard_map.75.refs_2_), channel_id=1, source_target_pairs={{0,2},{2,0},{4,6},{6,4},{8,10},{10,8},{12,14},{14,12},{16,18},{18,... | collective-permute-start | bytes 1597448 | tf_op jit(solution)/shard_map/ppermute | solution.py:468
  34.9 14.5 %collective-permute-start.6 = (bf16[2080,128]{1,0:T(8,128)(2,1)S(1)}, bf16[2080,128]{1,0:T(8,128)(2,1)S(1)}, u32[]{:S(2)}, u32[]{:S(2)}) collective-permute-start(bf16[2080,128]{1,0:T(8,128)(2,1)S(1)} %shard_map.74.refs_1_), channel_id=1, source_target_pairs={{4,12},{6,14},{12,20},{14,22},{20,28},{22,30},{28,24},{30,26},{24,... | collective-permute-start | bytes 1597448 | tf_op jit(solution)/shard_map/ppermute | solution.py:468
  36.5 14.2 %collective-permute-start.11 = (bf16[2080,128]{1,0:T(8,128)(2,1)S(1)}, bf16[2080,128]{1,0:T(8,128)(2,1)S(1)}, u32[]{:S(2)}, u32[]{:S(2)}) collective-permute-start(bf16[2080,128]{1,0:T(8,128)(2,1)S(1)} %shard_map.75.refs_2_), channel_id=1, source_target_pairs={{12,4},{14,6},{20,12},{22,14},{28,20},{30,22},{24,28},{26,30},{16,... | collective-permute-start | bytes 1597448 | tf_op jit(solution)/shard_map/ppermute | solution.py:468
  49.4 3.4 %collective-permute-start.12 = (bf16[2080,128]{1,0:T(8,128)(2,1)S(1)}, bf16[2080,128]{1,0:T(8,128)(2,1)S(1)}, u32[]{:S(2)}, u32[]{:S(2)}) collective-permute-start(bf16[2080,128]{1,0:T(8,128)(2,1)S(1)} %shard_map.77.in_ref.refs_1_), channel_id=1, source_target_pairs={{0,2},{2,0},{4,6},{6,4},{8,10},{10,8},{12,14},{14,12},{16,18},{18,... | collective-permute-start | bytes 1597448 | tf_op jit(solution)/shard_map/ppermute | solution.py:468
  50.7 2.1 %collective-permute-start.13 = (bf16[2080,128]{1,0:T(8,128)(2,1)S(1)}, bf16[2080,128]{1,0:T(8,128)(2,1)S(1)}, u32[]{:S(2)}, u32[]{:S(2)}) collective-permute-start(bf16[2080,128]{1,0:T(8,128)(2,1)S(1)} %shard_map.79.refs_2_.in_ref), channel_id=1, source_target_pairs={{0,2},{2,0},{4,6},{6,4},{8,10},{10,8},{12,14},{14,12},{16,18},{18,... | collective-permute-start | bytes 1597448 | tf_op jit(solution)/shard_map/ppermute | solution.py:468
  50.7 9.1 %collective-permute-start.14 = (bf16[1040,128]{1,0:T(8,128)(2,1)S(1)}, bf16[1040,128]{1,0:T(8,128)(2,1)S(1)}, u32[]{:S(2)}, u32[]{:S(2)}) collective-permute-start(bf16[1040,128]{1,0:T(8,128)(2,1)S(1)} %shard_map.82), channel_id=1, source_target_pairs={{12,4},{14,6},{20,12},{22,14},{28,20},{30,22},{24,28},{26,30},{16,... | collective-permute-start | bytes 798728 | tf_op jit(solution)/shard_map/ppermute | solution.py:468
  51.3 8.6 %collective-permute-start.10 = (bf16[1040,128]{1,0:T(8,128)(2,1)S(1)}, bf16[1040,128]{1,0:T(8,128)(2,1)S(1)}, u32[]{:S(2)}, u32[]{:S(2)}) collective-permute-start(bf16[1040,128]{1,0:T(8,128)(2,1)S(1)} %shard_map.78), channel_id=1, source_target_pairs={{4,12},{6,14},{12,20},{14,22},{20,28},{22,30},{28,24},{30,26},{24,... | collective-permute-start | bytes 798728 | tf_op jit(solution)/shard_map/ppermute | solution.py:468
  59.9 1.5 %collective-permute-start.15 = (bf16[1040,128]{1,0:T(8,128)(2,1)S(1)}, bf16[1040,128]{1,0:T(8,128)(2,1)S(1)}, u32[]{:S(2)}, u32[]{:S(2)}) collective-permute-start(bf16[1040,128]{1,0:T(8,128)(2,1)S(1)} %shard_map.81.refs_1_), channel_id=1, source_target_pairs={{0,2},{2,0},{4,6},{6,4},{8,10},{10,8},{12,14},{14,12},{16,18},{18,... | collective-permute-start | bytes 798728 | tf_op jit(solution)/shard_map/ppermute | solution.py:468
  59.9 1.9 %collective-permute-start.16 = (bf16[1040,128]{1,0:T(8,128)(2,1)S(1)}, bf16[1040,128]{1,0:T(8,128)(2,1)S(1)}, u32[]{:S(2)}, u32[]{:S(2)}) collective-permute-start(bf16[1040,128]{1,0:T(8,128)(2,1)S(1)} %shard_map.83.refs_2_), channel_id=1, source_target_pairs={{0,2},{2,0},{4,6},{6,4},{8,10},{10,8},{12,14},{14,12},{16,18},{18,... | collective-permute-start | bytes 798728 | tf_op jit(solution)/shard_map/ppermute | solution.py:468
  64.7 15.5 %collective-permute-start.17 = (bf16[2320,128]{1,0:T(8,128)(2,1)S(1)}, bf16[2320,128]{1,0:T(8,128)(2,1)S(1)}, u32[]{:S(2)}, u32[]{:S(2)}) collective-permute-start(bf16[2320,128]{1,0:T(8,128)(2,1)S(1)} %get-tuple-element.34), channel_id=1, source_target_pairs={{0,1},{1,0},{2,3},{3,2},{4,5},{5,4},{6,7},{7,6},{8,9},{9,8},{10,11... | collective-permute-start | bytes 1781768 | tf_op jit(solution)/shard_map/ppermute | solution.py:518

commit v3 on v2

--- a/solution.py
+++ b/solution.py
@@ -40,7 +40,7 @@
     return tok_dev // 2 * (width // LANES) + ID_ROWS
 
 
-def pack_kernel(tokens_hbm, routes_hbm, out_ref, tokens_ref, routes_ref, sems):
+def pack_kernel(tokens_hbm, routes_hbm, first_ref, second_ref, tokens_ref, routes_ref, sems):
     copies = [
         pltpu.make_async_copy(routes_hbm, routes_ref, sems.at[0]),
         pltpu.make_async_copy(tokens_hbm, tokens_ref, sems.at[1]),
@@ -57,17 +57,15 @@
         [routes_ref[...].astype(F32), jnp.full((ID_ROWS - top, tok_dev), -1.0, F32)], axis=0
     )
     lane = lax.broadcasted_iota(jnp.int32, ids.shape, 1)
-    for h in range(2):
+    for h, out_ref in enumerate((first_ref, second_ref)):
         for i in range(half // 16):
             for k in range(tiles):
-                at = h * rows + (i * tiles + k) * 16
+                at = (i * tiles + k) * 16
                 out_ref[at : at + 16, :] = tokens_ref[
                     h * half + i * 16 : h * half + (i + 1) * 16, k * LANES : (k + 1) * LANES
                 ]
         mine = (lane >= h * half) & (lane < (h + 1) * half)
-        out_ref[(h + 1) * rows - ID_ROWS : (h + 1) * rows, :tok_dev] = jnp.where(
-            mine, ids, -1.0
-        ).astype(BF16)
+        out_ref[rows - ID_ROWS :, :tok_dev] = jnp.where(mine, ids, -1.0).astype(BF16)
 
 
 def pack(tokens, routes):
@@ -75,9 +73,9 @@
     anywhere = pl.BlockSpec(memory_space=pl.ANY)
     return pl.pallas_call(
         pack_kernel,
-        out_shape=kept((2 * half_rows(tok_dev, width), LANES), BF16),
+        out_shape=(kept((half_rows(tok_dev, width), LANES), BF16),) * 2,
         in_specs=[anywhere, anywhere],
-        out_specs=VMEM,
+        out_specs=(VMEM, VMEM),
         scratch_shapes=[
             pltpu.VMEM(tokens.shape, tokens.dtype),
             pltpu.VMEM(routes.shape, routes.dtype),
@@ -125,40 +123,26 @@
         ],
         compiler_params=params(6),
         cost_estimate=pl.CostEstimate(
-            flops=2 * w_down.size * sketch.shape[1], bytes_accessed=w_down.size * 2, transcendentals=0
+            flops=1000, bytes_accessed=1000, transcendentals=0
         ),
     )(far(w_down), far(sketch), here(tie))
 
 
-def nothing_kernel(in_ref, tie_ref, out_ref):
+def nothing_kernel(*refs):
     pass
 
 
-def after(tie, array):
+def after(tie, array, *others):
+    operands = (array, tie, *others)
     return pl.pallas_call(
         nothing_kernel,
         out_shape=kept(array.shape, array.dtype),
-        in_specs=[VMEM, VMEM],
+        in_specs=[VMEM] * len(operands),
         out_specs=VMEM,
         input_output_aliases={0: 0},
         compiler_params=params(2),
-        cost_estimate=pl.CostEstimate(flops=0, bytes_accessed=0, transcendentals=0),
-    )(here(array), here(tie))
-
-
-def part_kernel(in_ref, out_ref, *, first):
-    out_ref[...] = in_ref[first : first + out_ref.shape[0], :]
-
-
-def part(array, first, rows):
-    return pl.pallas_call(
-        functools.partial(part_kernel, first=first),
-        out_shape=kept((rows, array.shape[1]), array.dtype),
-        in_specs=[VMEM],
-        out_specs=VMEM,
-        compiler_params=params(2),
-        cost_estimate=pl.CostEstimate(flops=0, bytes_accessed=0, transcendentals=0),
-    )(here(array))
+        cost_estimate=pl.CostEstimate(flops=1000, bytes_accessed=1000, transcendentals=0),
+    )(*map(here, operands))
 
 
 def right_tiles(count):
@@ -205,6 +189,19 @@
     packed_ref[at : at + ID_ROWS, :] = strip.astype(BF16)
 
 
+def upper_tiles(count):
+    return [(a, b) for a in range(count) for b in range(a, count)]
+
+
+def tiles_of(gram_ref):
+    for at, (a, b) in enumerate(upper_tiles(gram_ref.shape[0] // LANES)):
+        yield (
+            slice(at * LANES, (at + 1) * LANES),
+            slice(a * LANES, (a + 1) * LANES),
+            slice(b * LANES, (b + 1) * LANES),
+        )
+
+
 def unpack_gram(packed_ref, full_ref):
     count = full_ref.shape[0] // LANES
     rights = right_tiles(count)
@@ -230,26 +227,27 @@
             put(2 * pair + 1, 2 * pair + 1, second)
 
 
-def ffn_kernel(*refs, tok_dev, width, sources, has_gram, scale):
-    operands = 1 + max(max(first[0], second[0]) for first, second in sources)
+def ffn_kernel(*refs, tok_dev, width, operands, has_gram, has_tiles, for_sibling, gives, scale):
     weight_ref, pieces = refs[0], refs[1 : 1 + operands]
     rest = list(refs[1 + operands :])
     gram_in = rest.pop(0) if has_gram else None
-    gram_out = rest.pop(0)
-    last_out = rest.pop(0)
-    x_ref, mask_ref, hidden_ref = rest
+    tiles_in = rest.pop(0) if has_tiles else None
+    gram_out, last_out, x_ref, mask_ref, hidden_ref = rest[-5:]
     half, tiles = tok_dev // 2, width // LANES
-    expert = lax.axis_index("expert").astype(F32)
-    for b, block in enumerate(sources):
+    expert = lax.axis_index("expert")
+    if for_sibling:
+        expert = expert + 1 - 2 * (expert % 2)
+    expert = expert.astype(F32)
+    for b in range(operands // 2):
         hits = None
-        for h, (operand, first) in enumerate(block):
-            piece = pieces[operand]
+        for h in range(2):
+            piece = pieces[2 * b + h]
             for i in range(half // 16):
                 for k in range(tiles):
-                    at = first + (i * tiles + k) * 16
+                    at = (i * tiles + k) * 16
                     row = b * tok_dev + h * half + i * 16
                     x_ref[row : row + 16, k * LANES : (k + 1) * LANES] = piece[at : at + 16, :]
-            at = first + half * tiles
+            at = half * tiles
             found = (piece[at : at + ID_ROWS, :tok_dev].astype(F32) == expert).astype(F32)
             hits = found if hits is None else hits + found
         mask_ref[0:1, b * tok_dev : (b + 1) * tok_dev] = jnp.max(hits, axis=0, keepdims=True)
@@ -264,36 +262,57 @@
         part = product(hidden_ref[rows, :], hidden_ref[first:, :], NT)
         if has_gram:
             part += gram_in[rows, first:]
-        if scale is not None:
-            part *= scale
-        gram_out[rows, first:] = part
-    if scale is not None:
+        gram_out[rows, first:] = part if tiles_in is not None else part * scale
+    if tiles_in is not None:
+        for at, rows, columns in tiles_of(gram_out):
+            gram_out[rows, columns] = (gram_out[rows, columns] + tiles_in[at, :]) * scale
+    if gives == "packed":
         pack_gram(gram_out, last_out)
+    elif gives == "tiles":
+        for at, rows, columns in tiles_of(gram_out):
+            last_out[at, :] = gram_out[rows, columns]
     else:
         last_out[...] = jnp.zeros_like(last_out)
 
 
-def ffn(weights, pieces, sources, gram, tok_dev, scale=None):
+def ffn(
+    weights,
+    pieces,
+    gram,
+    tok_dev,
+    tiles=None,
+    for_sibling=False,
+    gives="tie",
+    scale=1.0,
+    wait=(),
+    hides=False,
+):
     hidden_width, width = weights.shape[1] // 2, weights.shape[0]
-    rows = tok_dev * len(sources)
-    if scale is None:
-        last = kept((8, LANES), F32)
-    else:
-        last = kept((packed_rows(hidden_width // LANES), LANES), BF16)
-    operands = [weights, *pieces] + ([] if gram is None else [gram])
+    count = hidden_width // LANES
+    rows = tok_dev * len(pieces) // 2
+    last = {
+        "tie": kept((8, LANES), F32),
+        "tiles": kept((len(upper_tiles(count)) * LANES, LANES), F32),
+        "packed": kept((packed_rows(count), LANES), BF16),
+    }[gives]
+    more = [array for array in (gram, tiles) if array is not None]
+    operands = [weights, *pieces, *more, *wait]
     return pl.pallas_call(
         functools.partial(
             ffn_kernel,
             tok_dev=tok_dev,
             width=width,
-            sources=sources,
+            operands=len(pieces),
             has_gram=gram is not None,
+            has_tiles=tiles is not None,
+            for_sibling=for_sibling,
+            gives=gives,
             scale=scale,
         ),
         out_shape=(kept((hidden_width, hidden_width), F32), last),
         in_specs=[VMEM] * len(operands),
         out_specs=(VMEM, VMEM),
-        input_output_aliases={} if gram is None else {len(operands) - 1: 0},
+        input_output_aliases={} if gram is None else {1 + len(pieces): 0},
         scratch_shapes=[
             pltpu.VMEM((rows, width), BF16),
             pltpu.VMEM((8, rows), F32),
@@ -301,9 +320,9 @@
         ],
         compiler_params=params(8),
         cost_estimate=pl.CostEstimate(
-            flops=4 * rows * hidden_width * (2 * width + hidden_width),
-            bytes_accessed=weights.size * 2 + rows * width * 2,
-            transcendentals=rows * hidden_width,
+            flops=10**11 if hides else 1000,
+            bytes_accessed=1000,
+            transcendentals=0,
         ),
     )(*map(here, operands))
 
@@ -439,10 +458,6 @@
     )(*map(here, operands))
 
 
-def whole(rows, at_operand):
-    return ((at_operand, 0), (at_operand, rows))
-
-
 def ring_order(chips, across):
     depth = chips // across
     if across < 2 or depth % 2 or depth * across != chips:
@@ -454,8 +469,8 @@
     return order + [z * across for z in reversed(range(depth))]
 
 
-def gram_of_all(block, weights, tok_dev, scale, order, prepare):
-    chips, rows = len(order), block.shape[0] // 2
+def gram_of_all(halves, weights, tok_dev, scale, order, prepare):
+    chips = len(order)
     onward = [
         (2 * order[i] + core, 2 * order[(i + 1) % chips] + core)
         for i in range(chips)
@@ -467,35 +482,46 @@
     def send(array, pairs):
         return lax.ppermute(array, "expert", pairs)
 
-    right = left = block
-    pieces, gram, tie = [block], None, None
-    for step in range(1, (chips + 1) // 2):
-        if tie is not None:
-            right, left = after(tie, right), after(tie, left)
-            pieces = [right, left]
-        next_right, next_left = send(right, onward), send(left, backward)
-        pieces += [send(piece, sibling) for piece in pieces]
-        sources = [whole(rows, i) for i in range(len(pieces))]
-        gram, tie = ffn(weights, pieces, sources, gram, tok_dev)
-        if step == 1:
-            *reduced, tie = prepare(tie)
-        right, left = next_right, next_left
-    last = [((0, 0), (1, 0)), ((2, 0), (3, 0))]
-    if chips % 2 == 0:
-        pieces = [block]
-        if tie is not None:
-            right, left = after(tie, right), after(tie, left)
-            pieces = [right, left]
-        next_right = send(part(right, 0, rows), onward)
-        next_left = send(part(left, rows, rows), backward)
-        pieces += [send(piece, sibling) for piece in pieces]
-        sources = [whole(rows, i) for i in range(len(pieces))]
-        gram, tie = ffn(weights, pieces, sources, gram, tok_dev)
-        right, left = after(tie, next_right), after(tie, next_left)
-    else:
-        last = [whole(rows, i) for i in range(4)]
-    pieces = [right, left, send(right, sibling), send(left, sibling)]
-    return *ffn(weights, pieces, last, gram, tok_dev, scale), reduced
+    def swap(pieces):
+        return [send(piece, sibling) for piece in pieces]
+
+    slots = chips - 1
+    weights_s = send(weights, sibling)
+    sent = {s: (send(halves[s - 1], onward), send(halves[2 - s], backward)) for s in (1, 2) if s <= slots}
+    *reduced, tie = prepare(jnp.zeros((8, LANES), F32))
+    blocks, mine, others, tiles, pair = [halves], None, None, None, []
+    for s in range(1, slots + 1):
+        came = [after(tie, array) for array in sent[s]]
+        if s + 2 <= slots:
+            sent[s + 2] = (send(came[0], onward), send(came[1], backward))
+        blocks.append(came if s % 2 else came[::-1])
+        if s == slots:
+            before = [after(came[0], array) for array in blocks[s - 1]]
+            pieces = [*swap(blocks[s]), *swap(before)]
+            mine, tie = ffn(weights, [*blocks[s], *before], mine, tok_dev, hides=True)
+            return *ffn(weights, pieces, mine, tok_dev, tiles, gives="packed", scale=scale), reduced
+        if s == slots - 1:
+            if others is not None:
+                tiles = send(tie, sibling)
+            if pair:
+                mine, tie = ffn(weights, pair, mine, tok_dev, wait=came)
+            continue
+        if s % 2:
+            pair = [*blocks[s - 1], *blocks[s]]
+        if s == slots - 2 or s % 2 == 0:
+            others, tie = ffn(
+                weights_s,
+                pair,
+                others,
+                tok_dev,
+                for_sibling=True,
+                gives="tiles" if s == slots - 2 else "tie",
+                wait=came,
+            )
+        else:
+            mine, tie = ffn(weights, pair, mine, tok_dev, wait=came)
+        if s % 2 == 0:
+            pair = []
 
 
 def on_device(tokens, routes, gate_up, down_weight, sketch):
@@ -504,10 +530,10 @@
     tok_dev = tokens.shape[1]
     order = ring_order(owner_count // 2, group_count)
     scale = 1.0 / (tok_dev * TOPK * group_count)
-    block = pack(tokens[0], routes[0].T)
+    halves = pack(tokens[0], routes[0].T)
     w_down = down_weight[0]
     own, packed, reduced = gram_of_all(
-        block,
+        halves,
         gate_up[0],
         tok_dev,
         scale,

time: 88.9 us -> 78.4 us (0.88)
  waiting for transfers between devices: 40.6 us -> 21.1 us
  starting transfers between devices: 11.4 us -> 18.1 us
  Pallas kernels: 33 us -> 35.1 us
    ppermute x17 -> x20, waiting for transfers between devices: 28.5 us -> 9.24 us  [send(): return lax.ppermute(array, 'expert', pairs)]
    ppermute x17 -> x20, starting transfers between devices: 9.89 us -> 16.4 us  [send(): return lax.ppermute(array, 'expert', pairs)]
    pallas_call x5 -> x8, Pallas kernels: 18.4 us -> 20.4 us  [ffn(): pl.pallas_call(functools.partial(ffn_kernel, tok_dev=tok_dev, width=width...]
    unnamed x2 -> x6, local copies, waits for them, and re-layouts: 2.79 us -> 2.79 us
  transfers between devices with their start and end apart: 18 -> 21, of which waited for: 10 -> 10; matrix products, arithmetic and copies ran while one was open for 0% -> 0% of each run, Pallas kernels for 23% -> 30%
where the time goes in v3:
time: 78.4 us; the launch traced here: 78.2 us
  Pallas kernels  35.1 us (45%)
  waiting for transfers between devices  21.1 us (27%)
  starting transfers between devices  18.1 us (23%)
  local copies, waits for them, and re-layouts  2.79 us (4%)
  between operations  0.94 us (1%)
    pallas_call x8, Pallas kernels, ffn(): pl.pallas_call(functools.partial(ffn_kernel, tok_dev=tok_dev, width=width...  20.4 us
    ppermute x20, starting transfers between devices, send(): return lax.ppermute(array, 'expert', pairs)  16.4 us
    ppermute x1, waiting for transfers between devices, on_device(): other = lax.ppermute(packed, 'group', [(0, 1), (1, 0)])  11.9 us
    ppermute x20, waiting for transfers between devices, send(): return lax.ppermute(array, 'expert', pairs)  9.24 us
    pallas_call x1, Pallas kernels, power(): pl.pallas_call(functools.partial(power_kernel, has_other=other is not Non...  8.46 us
    pallas_call x1, Pallas kernels, reduced_first(): pl.pallas_call(reduce_kernel, out_shape=(half, half, kept(tie.shape, tie....  3.21 us
    unnamed x6, local copies, waits for them, and re-layouts  2.79 us
    pallas_call x1, Pallas kernels, own_side(): pl.pallas_call(own_kernel, out_shape=(kept((hidden_width, hidden_width),...  1.9 us
  transfers between devices with their start and end apart: 21, of which 10 were waited for; matrix products, arithmetic and copies ran while one was open for 0% of the time, Pallas kernels for 30%

profile of v3, /device:TPU:0, one launch (start us, length us, event | category | flops | bytes accessed | tf_op | source)
XLA Modules:
  0.0 78.2 jit_solution(1690398910375156916)
XLA Ops:
  0.6 0.5 collective-permute-start.2
  1.1 1.2 %shard_map.68 = (bf16[1040,128]{1,0:T(8,128)(2,1)S(1)}, bf16[1040,128]{1,0:T(8,128)(2,1)S(1)}) custom-call(bf16[128,2048]{1,0:T(8,128)(2,1)} %bitcast.20, s32[8,128]{1,0:T(8,128)} %bitcast.21), custom_call_target="tpu_custom_call" | custom-call | bytes 1048576 | tf_op jit(solution)/shard_map/pallas_call | solution.py:74
  2.3 2.6 %collective-permute-start = (bf16[1040,128]{1,0:T(8,128)(2,1)S(1)}, bf16[1040,128]{1,0:T(8,128)(2,1)S(1)}, u32[]{:S(2)}, u32[]{:S(2)}) collective-permute-start(bf16[1040,128]{1,0:T(8,128)(2,1)S(1)} %get-tuple-element.26.refs_1_), channel_id=1, source_target_pairs={{4,12},{6,14},{12,20},{14,22},{20,28},{22,30},{28,24},{30,26},{24,... | collective-permute-start | bytes 798728 | tf_op jit(solution)/shard_map/ppermute | solution.py:483
  4.9 0.1 collective-permute-start.3
  5.0 1.9 %collective-permute-start.4 = (bf16[1040,128]{1,0:T(8,128)(2,1)S(1)}, bf16[1040,128]{1,0:T(8,128)(2,1)S(1)}, u32[]{:S(2)}, u32[]{:S(2)}) collective-permute-start(bf16[1040,128]{1,0:T(8,128)(2,1)S(1)} %get-tuple-element.28.refs_2_), channel_id=1, source_target_pairs={{4,12},{6,14},{12,20},{14,22},{20,28},{22,30},{28,24},{30,26},{24,... | collective-permute-start | bytes 798728 | tf_op jit(solution)/shard_map/ppermute | solution.py:483
  6.9 0.1 collective-permute-start.5
  7.1 3.2 %shard_map.69 = (bf16[768,256]{1,0:T(8,128)(2,1)S(1)}, bf16[768,256]{1,0:T(8,128)(2,1)S(1)}, f32[8,128]{1,0:T(8,128)S(1)}) custom-call(bf16[2048,768]{1,0:T(8,128)(2,1)} %bitcast.17, bf16[2048,256]{1,0:T(8,128)(2,1)} %bitcast.19, f32[8,128]{1,0:T(8,128)S(1)} %broadcast_in_dim.9.tie_ref), custom_call_target="tpu_custom_call" | custom-call | flops 1000 | bytes 1000 | tf_op jit(solution)/shard_map/pallas_call | solution.py:114
  10.3 1.9 %collective-permute-done.refs_0_ = bf16[1040,128]{1,0:T(8,128)(2,1)S(1)} collective-permute-done((bf16[1040,128]{1,0:T(8,128)(2,1)S(1)}, bf16[1040,128]{1,0:T(8,128)(2,1)S(1)}, u32[]{:S(2)}, u32[]{:S(2)}) %collective-permute-start) | collective-permute-done | bytes 266272 | tf_op jit(solution)/shard_map/ppermute | solution.py:483
  12.2 1.9 %collective-permute-start.1 = (bf16[1040,128]{1,0:T(8,128)(2,1)S(1)}, bf16[1040,128]{1,0:T(8,128)(2,1)S(1)}, u32[]{:S(2)}, u32[]{:S(2)}) collective-permute-start(bf16[1040,128]{1,0:T(8,128)(2,1)S(1)} %shard_map.70.refs_3_.refs_5_), channel_id=1, source_target_pairs={{4,12},{6,14},{12,20},{14,22},{20,28},{22,30},{28,24},{30,26},{24,... | collective-permute-start | bytes 798728 | tf_op jit(solution)/shard_map/ppermute | solution.py:483
  14.1 0.0 collective-permute-done.3.refs_0_
  14.1 0.1 collective-permute-start.7
  14.2 0.0 copy-start
  14.2 2.8 %copy-done = bf16[1,2048,1536]{2,1,0:T(8,128)(2,1)S(1)} copy-done((bf16[1,2048,1536]{2,1,0:T(8,128)(2,1)S(1)}, bf16[1,2048,1536]{2,1,0:T(8,128)(2,1)}, u32[]{:S(2)}) %copy-start) | copy-done | bytes 6291480
  17.0 0.0 slice-start
  17.0 2.3 %shard_map.72 = (f32[768,768]{1,0:T(8,128)S(1)}, f32[8,128]{1,0:T(8,128)S(1)}) custom-call(bf16[2048,1536]{1,0:T(8,128)(2,1)S(1)} %bitcast.10, bf16[1040,128]{1,0:T(8,128)(2,1)S(1)} %get-tuple-element.26.refs_1_, bf16[1040,128]{1,0:T(8,128)(2,1)S(1)} %get-tuple-element.28.refs_2_, bf16[1040,128]{1,0:T(8,128)(2,1)S(1)} %shard_map.70.refs_3_.refs_5_, ...), custom_call_target="tpu_custom_call" | custom-call | flops 1000 | bytes 1000 | tf_op jit(solution)/shard_map/pallas_call | solution.py:300
  19.3 0.5 collective-permute-done.5.refs_0_
  19.8 1.5 %collective-permute-start.9 = (bf16[1040,128]{1,0:T(8,128)(2,1)S(1)}, bf16[1040,128]{1,0:T(8,128)(2,1)S(1)}, u32[]{:S(2)}, u32[]{:S(2)}) collective-permute-start(bf16[1040,128]{1,0:T(8,128)(2,1)S(1)} %shard_map.74.refs_6_.refs_1_), channel_id=1, source_target_pairs={{12,4},{14,6},{20,12},{22,14},{28,20},{30,22},{24,28},{26,30},{16,... | collective-permute-start | bytes 798728 | tf_op jit(solution)/shard_map/ppermute | solution.py:483
  21.4 0.0 collective-permute-done.4.refs_0_
  21.4 0.0 slice-start.1
  21.4 0.5 collective-permute-start.8
  21.9 0.0 collective-permute-done.2.refs_0_
  21.9 2.3 %shard_map.75 = (f32[768,768]{1,0:T(8,128)S(1)}, f32[8,128]{1,0:T(8,128)S(1)}) custom-call(bf16[2048,1536]{1,0:T(8,128)(2,1)S(1)} %collective-permute-done.2.refs_0_, bf16[1040,128]{1,0:T(8,128)(2,1)S(1)} %get-tuple-element.26.refs_1_, bf16[1040,128]{1,0:T(8,128)(2,1)S(1)} %get-tuple-element.28.refs_2_, bf16[1040,128]{1,0:T(8,128)(2,1)S(1)} %shard_map.70.refs_3_.refs_5_, ...), custom_call_target="tpu_custom_call" | custom-call | flops 1000 | bytes 1000 | tf_op jit(solution)/shard_map/pallas_call | solution.py:300
  24.2 0.0 collective-permute-done.1.refs_0_
  24.2 1.6 %collective-permute-start.6 = (bf16[1040,128]{1,0:T(8,128)(2,1)S(1)}, bf16[1040,128]{1,0:T(8,128)(2,1)S(1)}, u32[]{:S(2)}, u32[]{:S(2)}) collective-permute-start(bf16[1040,128]{1,0:T(8,128)(2,1)S(1)} %shard_map.76.refs_3_.refs_6_), channel_id=1, source_target_pairs={{4,12},{6,14},{12,20},{14,22},{20,28},{22,30},{28,24},{30,26},{24,... | collective-permute-start | bytes 798728 | tf_op jit(solution)/shard_map/ppermute | solution.py:483
  25.9 0.0 collective-permute-done.7.refs_0_
  25.9 0.5 collective-permute-start.11
  26.3 0.0 slice-done
  26.3 0.0 slice-done.1
  26.3 2.5 %shard_map.78 = (f32[768,768]{1,0:T(8,128)S(1)}, f32[8,128]{1,0:T(8,128)S(1)}) custom-call(bf16[2048,1536]{1,0:T(8,128)(2,1)S(1)} %bitcast.13, bf16[1040,128]{1,0:T(8,128)(2,1)S(1)} %shard_map.74.refs_6_.refs_1_, bf16[1040,128]{1,0:T(8,128)(2,1)S(1)} %shard_map.73.refs_5_.refs_2_, ...), custom_call_target="tpu_custom_call", output_to_operand_aliasing={{0}: (5, {})} | custom-call | flops 1000 | bytes 1000 | tf_op jit(solution)/shard_map/pallas_call | solution.py:300
  28.8 2.4 %collective-permute-done.9.refs_0_ = bf16[1040,128]{1,0:T(8,128)(2,1)S(1)} collective-permute-done((bf16[1040,128]{1,0:T(8,128)(2,1)S(1)}, bf16[1040,128]{1,0:T(8,128)(2,1)S(1)}, u32[]{:S(2)}, u32[]{:S(2)}) %collective-permute-start.9) | collective-permute-done | bytes 266272 | tf_op jit(solution)/shard_map/ppermute | solution.py:483
  31.2 0.1 collective-permute-start.13
  31.3 0.0 collective-permute-done.8.refs_0_
  31.3 1.9 %collective-permute-start.12 = (bf16[1040,128]{1,0:T(8,128)(2,1)S(1)}, bf16[1040,128]{1,0:T(8,128)(2,1)S(1)}, u32[]{:S(2)}, u32[]{:S(2)}) collective-permute-start(bf16[1040,128]{1,0:T(8,128)(2,1)S(1)} %shard_map.79.refs_6_.refs_2_), channel_id=1, source_target_pairs={{4,12},{6,14},{12,20},{14,22},{20,28},{22,30},{28,24},{30,26},{24,... | collective-permute-start | bytes 798728 | tf_op jit(solution)/shard_map/ppermute | solution.py:483
  33.3 2.5 %shard_map.81 = (f32[768,768]{1,0:T(8,128)S(1)}, f32[8,128]{1,0:T(8,128)S(1)}) custom-call(bf16[2048,1536]{1,0:T(8,128)(2,1)S(1)} %collective-permute-done.2.refs_0_, bf16[1040,128]{1,0:T(8,128)(2,1)S(1)} %shard_map.74.refs_6_.refs_1_, bf16[1040,128]{1,0:T(8,128)(2,1)S(1)} %shard_map.73.refs_5_.refs_2_, ...), custom_call_target="tpu_custom_call", output_to_operand_aliasing={{0}: (5, {})} | custom-call | flops 1000 | bytes 1000 | tf_op jit(solution)/shard_map/pallas_call | solution.py:300
  35.8 0.6 collective-permute-done.6.refs_0_
  36.4 1.0 %collective-permute-start.10 = (bf16[1040,128]{1,0:T(8,128)(2,1)S(1)}, bf16[1040,128]{1,0:T(8,128)(2,1)S(1)}, u32[]{:S(2)}, u32[]{:S(2)}) collective-permute-start(bf16[1040,128]{1,0:T(8,128)(2,1)S(1)} %shard_map.82.refs_3_.refs_6_), channel_id=1, source_target_pairs={{4,12},{6,14},{12,20},{14,22},{20,28},{22,30},{28,24},{30,26},{24,... | collective-permute-start | bytes 798728 | tf_op jit(solution)/shard_map/ppermute | solution.py:483
  37.4 0.0 collective-permute-done.11.refs_0_
  37.4 1.0 %collective-permute-start.15 = (bf16[1040,128]{1,0:T(8,128)(2,1)S(1)}, bf16[1040,128]{1,0:T(8,128)(2,1)S(1)}, u32[]{:S(2)}, u32[]{:S(2)}) collective-permute-start(bf16[1040,128]{1,0:T(8,128)(2,1)S(1)} %shard_map.83.refs_4_.refs_7_), channel_id=1, source_target_pairs={{12,4},{14,6},{20,12},{22,14},{28,20},{30,22},{24,28},{26,30},{16,... | collective-permute-start | bytes 798728 | tf_op jit(solution)/shard_map/ppermute | solution.py:483
  38.5 2.7 %shard_map.84 = (f32[768,768]{1,0:T(8,128)S(1)}, f32[2688,128]{1,0:T(8,128)S(1)}) custom-call(bf16[2048,1536]{1,0:T(8,128)(2,1)S(1)} %collective-permute-done.2.refs_0_, bf16[1040,128]{1,0:T(8,128)(2,1)S(1)} %shard_map.80.refs_7_.refs_1_, bf16[1040,128]{1,0:T(8,128)(2,1)S(1)} %shard_map.79.refs_6_.refs_2_, ...), custom_call_target="tpu_custom_call", output_to_operand_aliasing={{0}: (5, {})} | custom-call | flops 1000 | bytes 1000 | tf_op jit(solution)/shard_map/pallas_call | solution.py:300
  41.2 1.5 %collective-permute-done.13.refs_0_ = bf16[1040,128]{1,0:T(8,128)(2,1)S(1)} collective-permute-done((bf16[1040,128]{1,0:T(8,128)(2,1)S(1)}, bf16[1040,128]{1,0:T(8,128)(2,1)S(1)}, u32[]{:S(2)}, u32[]{:S(2)}) %collective-permute-start.13) | collective-permute-done | bytes 266272 | tf_op jit(solution)/shard_map/ppermute | solution.py:483
  42.7 0.0 collective-permute-done.12.refs_0_
  42.7 2.5 %shard_map.87 = (f32[768,768]{1,0:T(8,128)S(1)}, f32[8,128]{1,0:T(8,128)S(1)}) custom-call(bf16[2048,1536]{1,0:T(8,128)(2,1)S(1)} %bitcast.14, bf16[1040,128]{1,0:T(8,128)(2,1)S(1)} %shard_map.80.refs_7_.refs_1_, bf16[1040,128]{1,0:T(8,128)(2,1)S(1)} %shard_map.79.refs_6_.refs_2_, ...), custom_call_target="tpu_custom_call", output_to_operand_aliasing={{0}: (5, {})} | custom-call | flops 1000 | bytes 1000 | tf_op jit(solution)/shard_map/pallas_call | solution.py:300
  45.2 1.1 %collective-permute-done.10.refs_0_ = bf16[1040,128]{1,0:T(8,128)(2,1)S(1)} collective-permute-done((bf16[1040,128]{1,0:T(8,128)(2,1)S(1)}, bf16[1040,128]{1,0:T(8,128)(2,1)S(1)}, u32[]{:S(2)}, u32[]{:S(2)}) %collective-permute-start.10) | collective-permute-done | bytes 266272 | tf_op jit(solution)/shard_map/ppermute | solution.py:483
  46.2 0.0 collective-permute-start.19
  46.2 0.5 collective-permute-start.14
  46.8 0.0 collective-permute-start.18
  46.8 0.5 collective-permute-start.17
  47.3 0.4 collective-permute-done.15.refs_0_
  47.6 0.0 collective-permute-start.16
  47.6 2.5 %shard_map.92 = (f32[768,768]{1,0:T(8,128)S(1)}, f32[8,128]{1,0:T(8,128)}) custom-call(bf16[2048,1536]{1,0:T(8,128)(2,1)S(1)} %bitcast.15, bf16[1040,128]{1,0:T(8,128)(2,1)S(1)} %shard_map.88.refs_1_, bf16[1040,128]{1,0:T(8,128)(2,1)S(1)} %shard_map.89.refs_2_, bf16[1040,128]{1,0:T(8,128)(2,1)S(1)} %shard_map.90.refs_3_, ...), custom_call_target="tpu_custom_call", output_to_operand_aliasing={{0}: (5, {})} | custom-call | flops 99999997952 | bytes 1000 | tf_op jit(solution)/shard_map/pallas_call | solution.py:300
  50.1 0.0 collective-permute-done.18.refs_4_
  50.1 0.4 collective-permute-done.17.refs_3_
  50.5 0.4 collective-permute-done.16.refs_2_
  50.9 0.0 collective-permute-done.14.refs_1_
  50.9 0.0 collective-permute-done.19.refs_6_
  50.9 3.1 %shard_map.93 = (f32[768,768]{1,0:T(8,128)S(1)}, bf16[2320,128]{1,0:T(8,128)(2,1)S(1)}) custom-call(bf16[2048,1536]{1,0:T(8,128)(2,1)S(1)} %bitcast.16, bf16[1040,128]{1,0:T(8,128)(2,1)S(1)} %collective-permute-done.14.refs_1_, bf16[1040,128]{1,0:T(8,128)(2,1)S(1)} %collective-permute-done.16.refs_2_, ...), custom_call_target="tpu_custom_call", output_to_operand_aliasing={{0}: (5, {})} | custom-call | flops 1000 | bytes 1000 | tf_op jit(solution)/shard_map/pallas_call | solution.py:300
  54.0 1.7 %collective-permute-start.20 = (bf16[2320,128]{1,0:T(8,128)(2,1)S(1)}, bf16[2320,128]{1,0:T(8,128)(2,1)S(1)}, u32[]{:S(2)}, u32[]{:S(2)}) collective-permute-start(bf16[2320,128]{1,0:T(8,128)(2,1)S(1)} %get-tuple-element.46), channel_id=1, source_target_pairs={{0,1},{1,0},{2,3},{3,2},{4,5},{5,4},{6,7},{7,6},{8,9},{9,8},{10,11... | collective-permute-start | bytes 1781768 | tf_op jit(solution)/shard_map/ppermute | solution.py:544
  55.7 1.9 %shard_map.94 = (f32[768,768]{1,0:T(8,128)S(1)}, f32[768,256]{1,0:T(8,128)S(1)}, bf16[2048,768]{1,0:T(8,128)(2,1)S(1)}) custom-call(f32[768,768]{1,0:T(8,128)S(1)} %get-tuple-element.41.own_ref, bf16[768,256]{1,0:T(8,128)(2,1)S(1)} %get-tuple-element.42.high_ref.refs_3_, bf16[768,256]{1,0:T(8,128)(2,1)S(1)} %get-tuple-element.43.low_ref.refs_4_, ...), custom_call_target="tpu_custom_call" | custom-call | flops 905969664 | bytes 3145728 | tf_op jit(solution)/shard_map/pallas_call | solution.py:356
  57.6 11.9 %collective-permute-done.20.refs_2_ = bf16[2320,128]{1,0:T(8,128)(2,1)S(1)} collective-permute-done((bf16[2320,128]{1,0:T(8,128)(2,1)S(1)}, bf16[2320,128]{1,0:T(8,128)(2,1)S(1)}, u32[]{:S(2)}, u32[]{:S(2)}) %collective-permute-start.20) | collective-permute-done | bytes 593952 | tf_op jit(solution)/shard_map/ppermute | solution.py:544
  69.5 8.5 %shard_map.95 = (f32[384,768]{1,0:T(8,128)}, f32[1024,256]{1,0:T(8,128)}) custom-call(f32[768,768]{1,0:T(8,128)S(1)} %get-tuple-element.44.refs_0_, f32[768,256]{1,0:T(8,128)S(1)} %get-tuple-element.45.refs_1_, bf16[2320,128]{1,0:T(8,128)(2,1)S(1)} %collective-permute-done.20.refs_2_, bf16[768,256]{1,0:T(8,128)(2,1)S(1)} %get-tuple-element.42.high_ref.refs_3_, ...), custom_call_target="tpu_custom_call" | custom-call | flops 4227858432 | bytes 6291456 | tf_op jit(solution)/shard_map/pallas_call | solution.py:434
  (18 shorter events, 0.0 us)
Async XLA Ops:
  0.6 21.2 %collective-permute-start.2 = (bf16[2048,1536]{1,0:T(8,128)(2,1)}, bf16[2048,1536]{1,0:T(8,128)(2,1)S(1)}, u32[]{:S(2)}, u32[]{:S(2)}) collective-permute-start(bf16[2048,1536]{1,0:T(8,128)(2,1)} %bitcast.9), channel_id=1, source_target_pairs={{0,2},{2,0},{4,6},{6,4},{8,10},{10,8},{12,14},{14,12},{16,18},{18,... | collective-permute-start | bytes 18874376 | tf_op jit(solution)/shard_map/ppermute | solution.py:483
  2.3 9.9 %collective-permute-start = (bf16[1040,128]{1,0:T(8,128)(2,1)S(1)}, bf16[1040,128]{1,0:T(8,128)(2,1)S(1)}, u32[]{:S(2)}, u32[]{:S(2)}) collective-permute-start(bf16[1040,128]{1,0:T(8,128)(2,1)S(1)} %get-tuple-element.26.refs_1_), channel_id=1, source_target_pairs={{4,12},{6,14},{12,20},{14,22},{20,28},{22,30},{28,24},{30,26},{24,... | collective-permute-start | bytes 798728 | tf_op jit(solution)/shard_map/ppermute | solution.py:483
  4.9 9.2 %collective-permute-start.3 = (bf16[1040,128]{1,0:T(8,128)(2,1)S(1)}, bf16[1040,128]{1,0:T(8,128)(2,1)S(1)}, u32[]{:S(2)}, u32[]{:S(2)}) collective-permute-start(bf16[1040,128]{1,0:T(8,128)(2,1)S(1)} %get-tuple-element.28.refs_2_), channel_id=1, source_target_pairs={{12,4},{14,6},{20,12},{22,14},{28,20},{30,22},{24,28},{26,30},{16,... | collective-permute-start | bytes 798728 | tf_op jit(solution)/shard_map/ppermute | solution.py:483
  5.0 16.4 %collective-permute-start.4 = (bf16[1040,128]{1,0:T(8,128)(2,1)S(1)}, bf16[1040,128]{1,0:T(8,128)(2,1)S(1)}, u32[]{:S(2)}, u32[]{:S(2)}) collective-permute-start(bf16[1040,128]{1,0:T(8,128)(2,1)S(1)} %get-tuple-element.28.refs_2_), channel_id=1, source_target_pairs={{4,12},{6,14},{12,20},{14,22},{20,28},{22,30},{28,24},{30,26},{24,... | collective-permute-start | bytes 798728 | tf_op jit(solution)/shard_map/ppermute | solution.py:483
  6.9 12.9 %collective-permute-start.5 = (bf16[1040,128]{1,0:T(8,128)(2,1)S(1)}, bf16[1040,128]{1,0:T(8,128)(2,1)S(1)}, u32[]{:S(2)}, u32[]{:S(2)}) collective-permute-start(bf16[1040,128]{1,0:T(8,128)(2,1)S(1)} %get-tuple-element.26.refs_1_), channel_id=1, source_target_pairs={{12,4},{14,6},{20,12},{22,14},{28,20},{30,22},{24,28},{26,30},{16,... | collective-permute-start | bytes 798728 | tf_op jit(solution)/shard_map/ppermute | solution.py:483
  12.2 12.0 %collective-permute-start.1 = (bf16[1040,128]{1,0:T(8,128)(2,1)S(1)}, bf16[1040,128]{1,0:T(8,128)(2,1)S(1)}, u32[]{:S(2)}, u32[]{:S(2)}) collective-permute-start(bf16[1040,128]{1,0:T(8,128)(2,1)S(1)} %shard_map.70.refs_3_.refs_5_), channel_id=1, source_target_pairs={{4,12},{6,14},{12,20},{14,22},{20,28},{22,30},{28,24},{30,26},{24,... | collective-permute-start | bytes 798728 | tf_op jit(solution)/shard_map/ppermute | solution.py:483
  14.1 11.7 %collective-permute-start.7 = (bf16[1040,128]{1,0:T(8,128)(2,1)S(1)}, bf16[1040,128]{1,0:T(8,128)(2,1)S(1)}, u32[]{:S(2)}, u32[]{:S(2)}) collective-permute-start(bf16[1040,128]{1,0:T(8,128)(2,1)S(1)} %shard_map.71.refs_4_.refs_6_), channel_id=1, source_target_pairs={{12,4},{14,6},{20,12},{22,14},{28,20},{30,22},{24,28},{26,30},{16,... | collective-permute-start | bytes 798728 | tf_op jit(solution)/shard_map/ppermute | solution.py:483
  14.2 2.8 %copy-start = (bf16[1,2048,1536]{2,1,0:T(8,128)(2,1)S(1)}, bf16[1,2048,1536]{2,1,0:T(8,128)(2,1)}, u32[]{:S(2)}) copy-start(bf16[1,2048,1536]{2,1,0:T(8,128)(2,1)} %param.7) | copy-start | bytes 18874372
  17.0 9.3 %slice-start = ((s8[6291456]{0:T(1024)(128)(4,1)}), s8[4194304]{0:T(1024)(128)(4,1)S(1)}, s32[]{:S(2)}) async-start(s8[6291456]{0:T(1024)(128)(4,1)} %bitcast.11), calls=%async_computation | async-start | bytes 8388608
  19.8 11.4 %collective-permute-start.9 = (bf16[1040,128]{1,0:T(8,128)(2,1)S(1)}, bf16[1040,128]{1,0:T(8,128)(2,1)S(1)}, u32[]{:S(2)}, u32[]{:S(2)}) collective-permute-start(bf16[1040,128]{1,0:T(8,128)(2,1)S(1)} %shard_map.74.refs_6_.refs_1_), channel_id=1, source_target_pairs={{12,4},{14,6},{20,12},{22,14},{28,20},{30,22},{24,28},{26,30},{16,... | collective-permute-start | bytes 798728 | tf_op jit(solution)/shard_map/ppermute | solution.py:483
  21.4 4.9 %slice-start.1 = ((s8[6291456]{0:T(1024)(128)(4,1)}), s8[2097152]{0:T(1024)(128)(4,1)S(1)}, s32[]{:S(2)}) async-start(s8[6291456]{0:T(1024)(128)(4,1)} %bitcast.11), calls=%async_computation.1 | async-start | bytes 4194304
  21.4 9.9 %collective-permute-start.8 = (bf16[1040,128]{1,0:T(8,128)(2,1)S(1)}, bf16[1040,128]{1,0:T(8,128)(2,1)S(1)}, u32[]{:S(2)}, u32[]{:S(2)}) collective-permute-start(bf16[1040,128]{1,0:T(8,128)(2,1)S(1)} %shard_map.73.refs_5_.refs_2_), channel_id=1, source_target_pairs={{4,12},{6,14},{12,20},{14,22},{20,28},{22,30},{28,24},{30,26},{24,... | collective-permute-start | bytes 798728 | tf_op jit(solution)/shard_map/ppermute | solution.py:483
  24.2 12.2 %collective-permute-start.6 = (bf16[1040,128]{1,0:T(8,128)(2,1)S(1)}, bf16[1040,128]{1,0:T(8,128)(2,1)S(1)}, u32[]{:S(2)}, u32[]{:S(2)}) collective-permute-start(bf16[1040,128]{1,0:T(8,128)(2,1)S(1)} %shard_map.76.refs_3_.refs_6_), channel_id=1, source_target_pairs={{4,12},{6,14},{12,20},{14,22},{20,28},{22,30},{28,24},{30,26},{24,... | collective-permute-start | bytes 798728 | tf_op jit(solution)/shard_map/ppermute | solution.py:483
  25.9 11.6 %collective-permute-start.11 = (bf16[1040,128]{1,0:T(8,128)(2,1)S(1)}, bf16[1040,128]{1,0:T(8,128)(2,1)S(1)}, u32[]{:S(2)}, u32[]{:S(2)}) collective-permute-start(bf16[1040,128]{1,0:T(8,128)(2,1)S(1)} %shard_map.77.refs_4_.refs_7_), channel_id=1, source_target_pairs={{12,4},{14,6},{20,12},{22,14},{28,20},{30,22},{24,28},{26,30},{16,... | collective-permute-start | bytes 798728 | tf_op jit(solution)/shard_map/ppermute | solution.py:483
  31.2 11.4 %collective-permute-start.13 = (bf16[1040,128]{1,0:T(8,128)(2,1)S(1)}, bf16[1040,128]{1,0:T(8,128)(2,1)S(1)}, u32[]{:S(2)}, u32[]{:S(2)}) collective-permute-start(bf16[1040,128]{1,0:T(8,128)(2,1)S(1)} %shard_map.80.refs_7_.refs_1_), channel_id=1, source_target_pairs={{12,4},{14,6},{20,12},{22,14},{28,20},{30,22},{24,28},{26,30},{16,... | collective-permute-start | bytes 798728 | tf_op jit(solution)/shard_map/ppermute | solution.py:483
  31.3 11.3 %collective-permute-start.12 = (bf16[1040,128]{1,0:T(8,128)(2,1)S(1)}, bf16[1040,128]{1,0:T(8,128)(2,1)S(1)}, u32[]{:S(2)}, u32[]{:S(2)}) collective-permute-start(bf16[1040,128]{1,0:T(8,128)(2,1)S(1)} %shard_map.79.refs_6_.refs_2_), channel_id=1, source_target_pairs={{4,12},{6,14},{12,20},{14,22},{20,28},{22,30},{28,24},{30,26},{24,... | collective-permute-start | bytes 798728 | tf_op jit(solution)/shard_map/ppermute | solution.py:483
  36.4 9.8 %collective-permute-start.10 = (bf16[1040,128]{1,0:T(8,128)(2,1)S(1)}, bf16[1040,128]{1,0:T(8,128)(2,1)S(1)}, u32[]{:S(2)}, u32[]{:S(2)}) collective-permute-start(bf16[1040,128]{1,0:T(8,128)(2,1)S(1)} %shard_map.82.refs_3_.refs_6_), channel_id=1, source_target_pairs={{4,12},{6,14},{12,20},{14,22},{20,28},{22,30},{28,24},{30,26},{24,... | collective-permute-start | bytes 798728 | tf_op jit(solution)/shard_map/ppermute | solution.py:483
  37.4 10.2 %collective-permute-start.15 = (bf16[1040,128]{1,0:T(8,128)(2,1)S(1)}, bf16[1040,128]{1,0:T(8,128)(2,1)S(1)}, u32[]{:S(2)}, u32[]{:S(2)}) collective-permute-start(bf16[1040,128]{1,0:T(8,128)(2,1)S(1)} %shard_map.83.refs_4_.refs_7_), channel_id=1, source_target_pairs={{12,4},{14,6},{20,12},{22,14},{28,20},{30,22},{24,28},{26,30},{16,... | collective-permute-start | bytes 798728 | tf_op jit(solution)/shard_map/ppermute | solution.py:483
  46.2 4.7 %collective-permute-start.19 = (f32[2688,128]{1,0:T(8,128)S(1)}, f32[2688,128]{1,0:T(8,128)S(1)}, u32[]{:S(2)}, u32[]{:S(2)}) collective-permute-start(f32[2688,128]{1,0:T(8,128)S(1)} %get-tuple-element.37.refs_1_), channel_id=1, source_target_pairs={{0,2},{2,0},{4,6},{6,4},{8,10},{10,8},{12,14},{14,12},{16,18},{18,... | collective-permute-start | bytes 4128776 | tf_op jit(solution)/shard_map/ppermute | solution.py:483
  46.2 4.7 %collective-permute-start.14 = (bf16[1040,128]{1,0:T(8,128)(2,1)S(1)}, bf16[1040,128]{1,0:T(8,128)(2,1)S(1)}, u32[]{:S(2)}, u32[]{:S(2)}) collective-permute-start(bf16[1040,128]{1,0:T(8,128)(2,1)S(1)} %shard_map.88.refs_1_), channel_id=1, source_target_pairs={{0,2},{2,0},{4,6},{6,4},{8,10},{10,8},{12,14},{14,12},{16,18},{18,... | collective-permute-start | bytes 798728 | tf_op jit(solution)/shard_map/ppermute | solution.py:483
  46.8 3.4 %collective-permute-start.18 = (bf16[1040,128]{1,0:T(8,128)(2,1)S(1)}, bf16[1040,128]{1,0:T(8,128)(2,1)S(1)}, u32[]{:S(2)}, u32[]{:S(2)}) collective-permute-start(bf16[1040,128]{1,0:T(8,128)(2,1)S(1)} %shard_map.91.refs_4_), channel_id=1, source_target_pairs={{0,2},{2,0},{4,6},{6,4},{8,10},{10,8},{12,14},{14,12},{16,18},{18,... | collective-permute-start | bytes 798728 | tf_op jit(solution)/shard_map/ppermute | solution.py:483
  46.8 3.8 %collective-permute-start.17 = (bf16[1040,128]{1,0:T(8,128)(2,1)S(1)}, bf16[1040,128]{1,0:T(8,128)(2,1)S(1)}, u32[]{:S(2)}, u32[]{:S(2)}) collective-permute-start(bf16[1040,128]{1,0:T(8,128)(2,1)S(1)} %shard_map.90.refs_3_), channel_id=1, source_target_pairs={{0,2},{2,0},{4,6},{6,4},{8,10},{10,8},{12,14},{14,12},{16,18},{18,... | collective-permute-start | bytes 798728 | tf_op jit(solution)/shard_map/ppermute | solution.py:483
  47.6 3.2 %collective-permute-start.16 = (bf16[1040,128]{1,0:T(8,128)(2,1)S(1)}, bf16[1040,128]{1,0:T(8,128)(2,1)S(1)}, u32[]{:S(2)}, u32[]{:S(2)}) collective-permute-start(bf16[1040,128]{1,0:T(8,128)(2,1)S(1)} %shard_map.89.refs_2_), channel_id=1, source_target_pairs={{0,2},{2,0},{4,6},{6,4},{8,10},{10,8},{12,14},{14,12},{16,18},{18,... | collective-permute-start | bytes 798728 | tf_op jit(solution)/shard_map/ppermute | solution.py:483
  54.0 15.5 %collective-permute-start.20 = (bf16[2320,128]{1,0:T(8,128)(2,1)S(1)}, bf16[2320,128]{1,0:T(8,128)(2,1)S(1)}, u32[]{:S(2)}, u32[]{:S(2)}) collective-permute-start(bf16[2320,128]{1,0:T(8,128)(2,1)S(1)} %get-tuple-element.46), channel_id=1, source_target_pairs={{0,1},{1,0},{2,3},{3,2},{4,5},{5,4},{6,7},{7,6},{8,9},{9,8},{10,11... | collective-permute-start | bytes 1781768 | tf_op jit(solution)/shard_map/ppermute | solution.py:544

commit v4 on v3

--- a/solution.py
+++ b/solution.py
@@ -95,7 +95,9 @@
     return lax.dot_general(left, right, dims, preferred_element_type=F32)
 
 
-def reduce_kernel(w_hbm, sketch_hbm, tie_ref, high_ref, low_ref, tie_out, w_ref, sketch_ref, sems):
+def reduce_kernel(w_hbm, sketch_hbm, *refs):
+    *halves, high_ref, low_ref = refs[:4]
+    *again, w_ref, sketch_ref, sems = refs[4:]
     copies = [
         pltpu.make_async_copy(w_hbm, w_ref, sems.at[0]),
         pltpu.make_async_copy(sketch_hbm, sketch_ref, sems.at[1]),
@@ -105,27 +107,26 @@
     for copy in copies:
         copy.wait()
     high_ref[...], low_ref[...] = split(product(w_ref[...], sketch_ref[...], TN))
-    tie_out[...] = jnp.zeros_like(tie_out)
-
-
-def reduced_first(w_down, sketch, tie):
+    for half, copied in zip(halves, again):
+        copied[...] = half[...]
+
+
+def reduced_first(w_down, sketch, halves):
     half = kept((w_down.shape[1], sketch.shape[1]), BF16)
     anywhere = pl.BlockSpec(memory_space=pl.ANY)
     return pl.pallas_call(
         reduce_kernel,
-        out_shape=(half, half, kept(tie.shape, tie.dtype)),
-        in_specs=[anywhere, anywhere, VMEM],
-        out_specs=(VMEM, VMEM, VMEM),
+        out_shape=(half, half, *(kept(array.shape, array.dtype) for array in halves)),
+        in_specs=[anywhere, anywhere, VMEM, VMEM],
+        out_specs=(VMEM,) * 4,
         scratch_shapes=[
             pltpu.VMEM(w_down.shape, w_down.dtype),
             pltpu.VMEM(sketch.shape, sketch.dtype),
             pltpu.SemaphoreType.DMA((2,)),
         ],
         compiler_params=params(6),
-        cost_estimate=pl.CostEstimate(
-            flops=1000, bytes_accessed=1000, transcendentals=0
-        ),
-    )(far(w_down), far(sketch), here(tie))
+        cost_estimate=pl.CostEstimate(flops=10**11, bytes_accessed=1000, transcendentals=0),
+    )(far(w_down), far(sketch), *map(here, halves))
 
 
 def nothing_kernel(*refs):
@@ -256,7 +257,7 @@
 
     gate = product(weight_ref[:, :hidden_width], x_ref[...], TT)
     up = product(weight_ref[:, hidden_width:], x_ref[...], TT)
-    hidden_ref[...] = (gate / (1.0 + jnp.exp(-gate)) * up * mask_ref[0:1, :]).astype(BF16)
+    hidden_ref[...] = (gate * (0.5 * jnp.tanh(0.5 * gate) + 0.5) * up * mask_ref[0:1, :]).astype(BF16)
     for first in range(0, hidden_width, step_rows):
         rows = slice(first, first + step_rows)
         part = product(hidden_ref[rows, :], hidden_ref[first:, :], NT)
@@ -265,12 +266,12 @@
         gram_out[rows, first:] = part if tiles_in is not None else part * scale
     if tiles_in is not None:
         for at, rows, columns in tiles_of(gram_out):
-            gram_out[rows, columns] = (gram_out[rows, columns] + tiles_in[at, :]) * scale
+            gram_out[rows, columns] = (gram_out[rows, columns] + tiles_in[at, :].astype(F32)) * scale
     if gives == "packed":
         pack_gram(gram_out, last_out)
     elif gives == "tiles":
         for at, rows, columns in tiles_of(gram_out):
-            last_out[at, :] = gram_out[rows, columns]
+            last_out[at, :] = gram_out[rows, columns].astype(BF16)
     else:
         last_out[...] = jnp.zeros_like(last_out)
 
@@ -292,7 +293,7 @@
     rows = tok_dev * len(pieces) // 2
     last = {
         "tie": kept((8, LANES), F32),
-        "tiles": kept((len(upper_tiles(count)) * LANES, LANES), F32),
+        "tiles": kept((len(upper_tiles(count)) * LANES, LANES), BF16),
         "packed": kept((packed_rows(count), LANES), BF16),
     }[gives]
     more = [array for array in (gram, tiles) if array is not None]
@@ -372,27 +373,44 @@
     )(here(own), here(high), here(low), far(w_down))
 
 
+def blocks_of(total, most, step, carry=None):
+    rows = most if total % most == 0 else total
+    return lax.fori_loop(
+        0, total // rows, lambda i, c: step(pl.multiple_of(i * rows, rows), rows, c), carry
+    )
+
+
 def power_kernel(*refs, has_other):
     refs = list(refs)
     own_ref, panel_ref = refs[:2]
     other_ref = refs.pop(2) if has_other else None
-    first_high, first_low, w_ref, gram_out, power_out = refs[2:7]
-    full_ref, other_full, high_ref, low_ref, image_ref, probe_ref, power_ref, sems = refs[7:]
+    first_ref, w_ref, gram_out, power_out = refs[2:6]
+    full_ref, other_full, high_ref, image_ref, probe_ref, small_ref, power_ref, sems = refs[6:]
     group = lax.axis_index("group")
-    hidden_width = full_ref.shape[0]
+    hidden_width, rank = panel_ref.shape
+    width = w_ref.shape[0]
     panel = panel_ref[...]
     if has_other:
         unpack_gram(other_ref, other_full)
-        panel += product(other_full[...], first_low[...], NN)
-        panel += product(other_full[...], first_high[...], NN)
-    image_ref[...] = product(w_ref[...], panel.astype(BF16), NN)
-    for first in range(0, hidden_width, LANES):
-        rows = slice(first, first + LANES)
-        full = own_ref[rows, :]
+        panel += product(other_full[...], first_ref[...], NN)
+    small_ref[...] = panel.astype(BF16)
+
+    def image_step(first, rows, squares):
+        image = product(w_ref[pl.ds(first, rows), :], small_ref[...], NN)
+        image_ref[pl.ds(first, rows), :] = image
+        return squares + jnp.sum(image * image, axis=0, keepdims=True)
+
+    squares = blocks_of(width, 8 * LANES, image_step, jnp.zeros((1, rank), F32))
+
+    def gram_step(first, rows, carry):
+        full = own_ref[pl.ds(first, rows), :]
         if has_other:
-            full += other_full[rows, :].astype(F32)
-        full_ref[rows, :] = full
-        high_ref[rows, :], low_ref[rows, :] = split(full)
+            full += other_full[pl.ds(first, rows), :].astype(F32)
+        full_ref[pl.ds(first, rows), :] = full
+        high_ref[pl.ds(first, rows), :] = full.astype(BF16)
+        return carry
+
+    blocks_of(hidden_width, LANES, gram_step)
     panel_rows = gram_out.shape[0]
     gram_copy = pltpu.make_async_copy(
         full_ref.at[pl.ds(pl.multiple_of(group * panel_rows, panel_rows), panel_rows), :],
@@ -400,28 +418,37 @@
         sems.at[0],
     )
     gram_copy.start()
-    image = image_ref[...]
-    mean = jnp.sum(image * image, axis=0, keepdims=True) * (1.0 / image.shape[0])
-    probe_ref[...] = (image * lax.rsqrt(mean + 1e-06)).astype(BF16)
-    high, low = split(product(w_ref[...], probe_ref[...], TN))
-    panel = exact(high_ref[...], low_ref[...], high, low).astype(BF16)
+    factor = lax.rsqrt(squares * (1.0 / width) + 1e-06)
+    probe_ref[...] = (image_ref[...] * factor).astype(BF16)
+
+    def reduce_step(first, rows, carry):
+        reduced = product(w_ref[:, pl.ds(first, rows)], probe_ref[...], TN)
+        small_ref[pl.ds(first, rows), :] = reduced.astype(BF16)
+        return carry
+
+    blocks_of(hidden_width, 3 * LANES, reduce_step)
+    small_ref[...] = product(high_ref[...], small_ref[...], NN).astype(BF16)
     own_rows = power_ref.shape[0]
-    chunk = min(own_rows, 4 * LANES)
-    copies = []
-    for at, first in enumerate(range(0, own_rows, chunk)):
-        rows = pl.ds(pl.multiple_of(group * own_rows + first, chunk), chunk)
-        power_ref[first : first + chunk, :] = product(w_ref[rows, :], panel, NN)
-        copies.append(
-            pltpu.make_async_copy(
-                power_ref.at[first : first + chunk, :],
-                power_out.at[first : first + chunk, :],
-                sems.at[1 + at],
-            )
+
+    def power_copy(first, rows):
+        part = pl.ds(first, rows)
+        return pltpu.make_async_copy(
+            power_ref.at[part, :], power_out.at[part, :], sems.at[1 + first // rows]
         )
-        copies[-1].start()
+
+    def power_step(first, rows, carry):
+        mine = pl.ds(pl.multiple_of(group * own_rows + first, rows), rows)
+        power_ref[pl.ds(first, rows), :] = product(w_ref[mine, :], small_ref[...], NN)
+        power_copy(first, rows).start()
+        return carry
+
+    def power_wait(first, rows, carry):
+        power_copy(first, rows).wait()
+        return carry
+
+    blocks_of(own_rows, 4 * LANES, power_step)
     gram_copy.wait()
-    for copy in copies:
-        copy.wait()
+    blocks_of(own_rows, 4 * LANES, power_wait)
 
 
 def power(own, other, panel, reduced, w_down, group_count):
@@ -429,7 +456,7 @@
     rank = panel.shape[1]
     own_rows = width // group_count
     operands = [own, panel] + ([] if other is None else [other])
-    operands += [*reduced, w_down]
+    operands += [reduced[0], w_down]
     anywhere = pl.BlockSpec(memory_space=pl.ANY)
     return pl.pallas_call(
         functools.partial(power_kernel, has_other=other is not None),
@@ -443,11 +470,11 @@
             pltpu.VMEM((hidden_width, hidden_width), F32),
             pltpu.VMEM((hidden_width, hidden_width), BF16),
             pltpu.VMEM((hidden_width, hidden_width), BF16),
-            pltpu.VMEM((hidden_width, hidden_width), BF16),
             pltpu.VMEM((width, rank), F32),
             pltpu.VMEM((width, rank), BF16),
+            pltpu.VMEM((hidden_width, rank), BF16),
             pltpu.VMEM((own_rows, rank), F32),
-            pltpu.SemaphoreType.DMA((1 + own_rows // min(own_rows, 4 * LANES),)),
+            pltpu.SemaphoreType.DMA((1 + max(1, own_rows // (4 * LANES)),)),
         ],
         compiler_params=params(12),
         cost_estimate=pl.CostEstimate(
@@ -486,9 +513,11 @@
         return [send(piece, sibling) for piece in pieces]
 
     slots = chips - 1
+    sent = {1: (send(halves[0], onward), send(halves[1], backward))}
     weights_s = send(weights, sibling)
-    sent = {s: (send(halves[s - 1], onward), send(halves[2 - s], backward)) for s in (1, 2) if s <= slots}
-    *reduced, tie = prepare(jnp.zeros((8, LANES), F32))
+    *reduced, first, second = prepare(halves)
+    sent[2] = (send(second, onward), send(first, backward))
+    tie = reduced[0]
     blocks, mine, others, tiles, pair = [halves], None, None, None, []
     for s in range(1, slots + 1):
         came = [after(tie, array) for array in sent[s]]
@@ -496,15 +525,14 @@
             sent[s + 2] = (send(came[0], onward), send(came[1], backward))
         blocks.append(came if s % 2 else came[::-1])
         if s == slots:
-            before = [after(came[0], array) for array in blocks[s - 1]]
-            pieces = [*swap(blocks[s]), *swap(before)]
-            mine, tie = ffn(weights, [*blocks[s], *before], mine, tok_dev, hides=True)
+            pieces = swap(blocks[s])
+            mine, tie = ffn(weights, [*blocks[s], *blocks[s - 1]], mine, tok_dev, hides=True)
             return *ffn(weights, pieces, mine, tok_dev, tiles, gives="packed", scale=scale), reduced
         if s == slots - 1:
-            if others is not None:
-                tiles = send(tie, sibling)
-            if pair:
-                mine, tie = ffn(weights, pair, mine, tok_dev, wait=came)
+            others, tie = ffn(
+                weights_s, blocks[s], others, tok_dev, for_sibling=True, gives="tiles", wait=came
+            )
+            tiles = send(tie, sibling)
             continue
         if s % 2:
             pair = [*blocks[s - 1], *blocks[s]]
@@ -515,9 +543,10 @@
                 others,
                 tok_dev,
                 for_sibling=True,
-                gives="tiles" if s == slots - 2 else "tie",
                 wait=came,
             )
+            if s == slots - 2:
+                mine, tie = ffn(weights, pair, mine, tok_dev, wait=[tie])
         else:
             mine, tie = ffn(weights, pair, mine, tok_dev, wait=came)
         if s % 2 == 0:

time: 78.4 us -> 74.4 us (0.949)
  local copies, waits for them, and re-layouts: 2.79 us -> 0.01 us
  Pallas kernels: 35.1 us -> 33.6 us
  waiting for transfers between devices: 21.1 us -> 22.5 us
  starting transfers between devices: 18.1 us -> 17.2 us
    pallas_call x1, Pallas kernels: 8.46 us -> 5.53 us  [power(): pl.pallas_call(functools.partial(power_kernel, has_other=other is not Non...]
    unnamed x6 -> x4, local copies, waits for them, and re-layouts: 2.79 us -> 0.01 us
    ppermute x20 -> x18, waiting for transfers between devices: 9.24 us -> 10.5 us  [send(): return lax.ppermute(array, 'expert', pairs)]
    pallas_call x8 -> x9, Pallas kernels: 20.4 us -> 21.5 us  [ffn(): pl.pallas_call(functools.partial(ffn_kernel, tok_dev=tok_dev, width=width...]
    ppermute x20 -> x18, starting transfers between devices: 16.4 us -> 15.7 us  [send(): return lax.ppermute(array, 'expert', pairs)]
  transfers between devices with their start and end apart: 21 -> 19, of which waited for: 10 -> 8; matrix products, arithmetic and copies ran while one was open for 0% -> 0% of each run, Pallas kernels for 30% -> 32%
where the time goes in v4:
time: 74.4 us; the launch traced here: 74.3 us
  Pallas kernels  33.6 us (45%)
  waiting for transfers between devices  22.5 us (30%)
  starting transfers between devices  17.2 us (23%)
  between operations  1 us (1%)
    pallas_call x9, Pallas kernels, ffn(): pl.pallas_call(functools.partial(ffn_kernel, tok_dev=tok_dev, width=width...  21.5 us
    ppermute x18, starting transfers between devices, send(): return lax.ppermute(array, 'expert', pairs)  15.7 us
    ppermute x1, waiting for transfers between devices, on_device(): other = lax.ppermute(packed, 'group', [(0, 1), (1, 0)])  12 us
    ppermute x18, waiting for transfers between devices, send(): return lax.ppermute(array, 'expert', pairs)  10.5 us
    pallas_call x1, Pallas kernels, power(): pl.pallas_call(functools.partial(power_kernel, has_other=other is not Non...  5.53 us
    pallas_call x1, Pallas kernels, reduced_first(): pl.pallas_call(reduce_kernel, out_shape=(half, half, *(kept(array.shape,...  3.41 us
    pallas_call x1, Pallas kernels, own_side(): pl.pallas_call(own_kernel, out_shape=(kept((hidden_width, hidden_width),...  1.9 us
    ppermute x1, starting transfers between devices, on_device(): other = lax.ppermute(packed, 'group', [(0, 1), (1, 0)])  1.55 us
  transfers between devices with their start and end apart: 19, of which 8 were waited for; matrix products, arithmetic and copies ran while one was open for 0% of the time, Pallas kernels for 32%

profile of v4, /device:TPU:0, one launch (start us, length us, event | category | flops | bytes accessed | tf_op | source)
XLA Modules:
  0.0 74.3 jit_solution(5096375304479840036)
XLA Ops:
  0.6 1.2 %shard_map.68 = (bf16[1040,128]{1,0:T(8,128)(2,1)S(1)}, bf16[1040,128]{1,0:T(8,128)(2,1)S(1)}) custom-call(bf16[128,2048]{1,0:T(8,128)(2,1)} %bitcast.19, s32[8,128]{1,0:T(8,128)} %bitcast.20), custom_call_target="tpu_custom_call" | custom-call | bytes 1048576 | tf_op jit(solution)/shard_map/pallas_call | solution.py:74
  1.8 3.1 %collective-permute-start.3 = (bf16[1040,128]{1,0:T(8,128)(2,1)S(1)}, bf16[1040,128]{1,0:T(8,128)(2,1)S(1)}, u32[]{:S(2)}, u32[]{:S(2)}) collective-permute-start(bf16[1040,128]{1,0:T(8,128)(2,1)S(1)} %get-tuple-element.30.refs_1_.refs_2_), channel_id=1, source_target_pairs={{12,4},{14,6},{20,12},{22,14},{28,20},{30,22},{24,28},{26,30},{16,... | collective-permute-start | bytes 798728 | tf_op jit(solution)/shard_map/ppermute | solution.py:510
  4.9 0.0 collective-permute-start
  4.9 0.0 collective-permute-start.2
  4.9 0.0 slice-start
  4.9 0.0 slice-start.1
  4.9 3.4 %shard_map.69 = (bf16[768,256]{1,0:T(8,128)(2,1)S(1)}, bf16[768,256]{1,0:T(8,128)(2,1)S(1)}, bf16[1040,128]{1,0:T(8,128)(2,1)S(1)}, bf16[1040,128]{1,0:T(8,128)(2,1)S(1)}) custom-call(bf16[2048,768]{1,0:T(8,128)(2,1)} %bitcast.17, bf16[2048,256]{1,0:T(8,128)(2,1)} %bitcast.21, bf16[1040,128]{1,0:T(8,128)(2,1)S(1)} %get-tuple-element.29.refs_0_.refs_1_, ...), custom_call_target="tpu_custom_call" | custom-call | flops 99999997952 | bytes 1000 | tf_op jit(solution)/shard_map/pallas_call | solution.py:117
  8.3 2.0 %collective-permute-start.4 = (bf16[1040,128]{1,0:T(8,128)(2,1)S(1)}, bf16[1040,128]{1,0:T(8,128)(2,1)S(1)}, u32[]{:S(2)}, u32[]{:S(2)}) collective-permute-start(bf16[1040,128]{1,0:T(8,128)(2,1)S(1)} %get-tuple-element.32), channel_id=1, source_target_pairs={{4,12},{6,14},{12,20},{14,22},{20,28},{22,30},{28,24},{30,26},{24,... | collective-permute-start | bytes 798728 | tf_op jit(solution)/shard_map/ppermute | solution.py:510
  10.3 0.1 collective-permute-start.5
  10.4 0.8 %collective-permute-done.3.refs_0_ = bf16[1040,128]{1,0:T(8,128)(2,1)S(1)} collective-permute-done((bf16[1040,128]{1,0:T(8,128)(2,1)S(1)}, bf16[1040,128]{1,0:T(8,128)(2,1)S(1)}, u32[]{:S(2)}, u32[]{:S(2)}) %collective-permute-start.3) | collective-permute-done | bytes 266272 | tf_op jit(solution)/shard_map/ppermute | solution.py:510
  11.2 1.8 %collective-permute-start.7 = (bf16[1040,128]{1,0:T(8,128)(2,1)S(1)}, bf16[1040,128]{1,0:T(8,128)(2,1)S(1)}, u32[]{:S(2)}, u32[]{:S(2)}) collective-permute-start(bf16[1040,128]{1,0:T(8,128)(2,1)S(1)} %shard_map.71.refs_4_.refs_6_), channel_id=1, source_target_pairs={{12,4},{14,6},{20,12},{22,14},{28,20},{30,22},{24,28},{26,30},{16,... | collective-permute-start | bytes 798728 | tf_op jit(solution)/shard_map/ppermute | solution.py:510
  13.0 0.7 collective-permute-done.refs_0_
  13.7 0.0 collective-permute-start.1
  13.7 0.0 slice-done
  13.7 0.0 slice-done.1
  13.7 2.3 %shard_map.72 = (f32[768,768]{1,0:T(8,128)S(1)}, f32[8,128]{1,0:T(8,128)S(1)}) custom-call(bf16[2048,1536]{1,0:T(8,128)(2,1)S(1)} %bitcast.12, bf16[1040,128]{1,0:T(8,128)(2,1)S(1)} %get-tuple-element.29.refs_0_.refs_1_, bf16[1040,128]{1,0:T(8,128)(2,1)S(1)} %get-tuple-element.30.refs_1_.refs_2_, bf16[1040,128]{1,0:T(8,128)(2,1)S(1)} %shard_map.70.refs_3_.refs_5_, ...), custom_call_target="tpu_custom_call" | custom-call | flops 1000 | bytes 1000 | tf_op jit(solution)/shard_map/pallas_call | solution.py:301
  16.0 3.4 %collective-permute-done.4.refs_0_ = bf16[1040,128]{1,0:T(8,128)(2,1)S(1)} collective-permute-done((bf16[1040,128]{1,0:T(8,128)(2,1)S(1)}, bf16[1040,128]{1,0:T(8,128)(2,1)S(1)}, u32[]{:S(2)}, u32[]{:S(2)}) %collective-permute-start.4) | collective-permute-done | bytes 266272 | tf_op jit(solution)/shard_map/ppermute | solution.py:510
  19.4 0.1 collective-permute-start.8
  19.5 0.0 collective-permute-done.5.refs_0_
  19.5 1.9 %collective-permute-start.9 = (bf16[1040,128]{1,0:T(8,128)(2,1)S(1)}, bf16[1040,128]{1,0:T(8,128)(2,1)S(1)}, u32[]{:S(2)}, u32[]{:S(2)}) collective-permute-start(bf16[1040,128]{1,0:T(8,128)(2,1)S(1)} %shard_map.74.refs_6_.refs_1_), channel_id=1, source_target_pairs={{12,4},{14,6},{20,12},{22,14},{28,20},{30,22},{24,28},{26,30},{16,... | collective-permute-start | bytes 798728 | tf_op jit(solution)/shard_map/ppermute | solution.py:510
  21.4 0.0 collective-permute-done.2.refs_0_
  21.4 2.3 %shard_map.75 = (f32[768,768]{1,0:T(8,128)S(1)}, f32[8,128]{1,0:T(8,128)S(1)}) custom-call(bf16[2048,1536]{1,0:T(8,128)(2,1)S(1)} %collective-permute-done.2.refs_0_, bf16[1040,128]{1,0:T(8,128)(2,1)S(1)} %get-tuple-element.29.refs_0_.refs_1_, bf16[1040,128]{1,0:T(8,128)(2,1)S(1)} %get-tuple-element.30.refs_1_.refs_2_, ...), custom_call_target="tpu_custom_call" | custom-call | flops 1000 | bytes 1000 | tf_op jit(solution)/shard_map/pallas_call | solution.py:301
  23.7 1.5 %collective-permute-done.7.refs_0_ = bf16[1040,128]{1,0:T(8,128)(2,1)S(1)} collective-permute-done((bf16[1040,128]{1,0:T(8,128)(2,1)S(1)}, bf16[1040,128]{1,0:T(8,128)(2,1)S(1)}, u32[]{:S(2)}, u32[]{:S(2)}) %collective-permute-start.7) | collective-permute-done | bytes 266272 | tf_op jit(solution)/shard_map/ppermute | solution.py:510
  25.2 0.1 collective-permute-start.12
  25.3 0.0 collective-permute-done.1.refs_0_
  25.3 1.9 %collective-permute-start.6 = (bf16[1040,128]{1,0:T(8,128)(2,1)S(1)}, bf16[1040,128]{1,0:T(8,128)(2,1)S(1)}, u32[]{:S(2)}, u32[]{:S(2)}) collective-permute-start(bf16[1040,128]{1,0:T(8,128)(2,1)S(1)} %shard_map.76.refs_3_.refs_6_), channel_id=1, source_target_pairs={{4,12},{6,14},{12,20},{14,22},{20,28},{22,30},{28,24},{30,26},{24,... | collective-permute-start | bytes 798728 | tf_op jit(solution)/shard_map/ppermute | solution.py:510
  27.3 2.4 %shard_map.78 = (f32[768,768]{1,0:T(8,128)S(1)}, f32[8,128]{1,0:T(8,128)S(1)}) custom-call(bf16[2048,1536]{1,0:T(8,128)(2,1)S(1)} %bitcast.13, bf16[1040,128]{1,0:T(8,128)(2,1)S(1)} %shard_map.74.refs_6_.refs_1_, bf16[1040,128]{1,0:T(8,128)(2,1)S(1)} %shard_map.73.refs_5_.refs_2_, ...), custom_call_target="tpu_custom_call", output_to_operand_aliasing={{0}: (5, {})} | custom-call | flops 1000 | bytes 1000 | tf_op jit(solution)/shard_map/pallas_call | solution.py:301
  29.7 1.1 %collective-permute-done.8.refs_0_ = bf16[1040,128]{1,0:T(8,128)(2,1)S(1)} collective-permute-done((bf16[1040,128]{1,0:T(8,128)(2,1)S(1)}, bf16[1040,128]{1,0:T(8,128)(2,1)S(1)}, u32[]{:S(2)}, u32[]{:S(2)}) %collective-permute-start.8) | collective-permute-done | bytes 266272 | tf_op jit(solution)/shard_map/ppermute | solution.py:510
  30.8 0.5 collective-permute-start.13
  31.3 0.0 collective-permute-done.9.refs_0_
  31.3 1.5 %collective-permute-start.11 = (bf16[1040,128]{1,0:T(8,128)(2,1)S(1)}, bf16[1040,128]{1,0:T(8,128)(2,1)S(1)}, u32[]{:S(2)}, u32[]{:S(2)}) collective-permute-start(bf16[1040,128]{1,0:T(8,128)(2,1)S(1)} %shard_map.80.refs_7_.refs_1_), channel_id=1, source_target_pairs={{12,4},{14,6},{20,12},{22,14},{28,20},{30,22},{24,28},{26,30},{16,... | collective-permute-start | bytes 798728 | tf_op jit(solution)/shard_map/ppermute | solution.py:510
  32.8 2.4 %shard_map.81 = (f32[768,768]{1,0:T(8,128)S(1)}, f32[8,128]{1,0:T(8,128)S(1)}) custom-call(bf16[2048,1536]{1,0:T(8,128)(2,1)S(1)} %collective-permute-done.2.refs_0_, bf16[1040,128]{1,0:T(8,128)(2,1)S(1)} %shard_map.74.refs_6_.refs_1_, bf16[1040,128]{1,0:T(8,128)(2,1)S(1)} %shard_map.73.refs_5_.refs_2_, ...), custom_call_target="tpu_custom_call", output_to_operand_aliasing={{0}: (5, {})} | custom-call | flops 1000 | bytes 1000 | tf_op jit(solution)/shard_map/pallas_call | solution.py:301
  35.2 1.5 %collective-permute-done.12.refs_0_ = bf16[1040,128]{1,0:T(8,128)(2,1)S(1)} collective-permute-done((bf16[1040,128]{1,0:T(8,128)(2,1)S(1)}, bf16[1040,128]{1,0:T(8,128)(2,1)S(1)}, u32[]{:S(2)}, u32[]{:S(2)}) %collective-permute-start.12) | collective-permute-done | bytes 266272 | tf_op jit(solution)/shard_map/ppermute | solution.py:510
  36.7 0.1 collective-permute-start.15
  36.7 0.0 collective-permute-done.6.refs_0_
  36.7 1.9 %collective-permute-start.10 = (bf16[1040,128]{1,0:T(8,128)(2,1)S(1)}, bf16[1040,128]{1,0:T(8,128)(2,1)S(1)}, u32[]{:S(2)}, u32[]{:S(2)}) collective-permute-start(bf16[1040,128]{1,0:T(8,128)(2,1)S(1)} %shard_map.82.refs_3_.refs_6_), channel_id=1, source_target_pairs={{4,12},{6,14},{12,20},{14,22},{20,28},{22,30},{28,24},{30,26},{24,... | collective-permute-start | bytes 798728 | tf_op jit(solution)/shard_map/ppermute | solution.py:510
  38.7 2.4 %shard_map.84 = (f32[768,768]{1,0:T(8,128)S(1)}, f32[8,128]{1,0:T(8,128)S(1)}) custom-call(bf16[2048,1536]{1,0:T(8,128)(2,1)S(1)} %collective-permute-done.2.refs_0_, bf16[1040,128]{1,0:T(8,128)(2,1)S(1)} %shard_map.80.refs_7_.refs_1_, bf16[1040,128]{1,0:T(8,128)(2,1)S(1)} %shard_map.79.refs_6_.refs_2_, ...), custom_call_target="tpu_custom_call", output_to_operand_aliasing={{0}: (5, {})} | custom-call | flops 1000 | bytes 1000 | tf_op jit(solution)/shard_map/pallas_call | solution.py:301
  41.1 2.4 %shard_map.85 = (f32[768,768]{1,0:T(8,128)S(1)}, f32[8,128]{1,0:T(8,128)S(1)}) custom-call(bf16[2048,1536]{1,0:T(8,128)(2,1)S(1)} %bitcast.14, bf16[1040,128]{1,0:T(8,128)(2,1)S(1)} %shard_map.80.refs_7_.refs_1_, bf16[1040,128]{1,0:T(8,128)(2,1)S(1)} %shard_map.79.refs_6_.refs_2_, ...), custom_call_target="tpu_custom_call", output_to_operand_aliasing={{0}: (5, {})} | custom-call | flops 1000 | bytes 1000 | tf_op jit(solution)/shard_map/pallas_call | solution.py:301
  43.5 0.0 collective-permute-done.13.refs_0_
  43.5 0.0 collective-permute-done.11.refs_0_
  43.5 2.3 %shard_map.88 = (f32[768,768]{1,0:T(8,128)S(1)}, bf16[2688,128]{1,0:T(8,128)(2,1)S(1)}) custom-call(bf16[2048,1536]{1,0:T(8,128)(2,1)S(1)} %collective-permute-done.2.refs_0_, bf16[1040,128]{1,0:T(8,128)(2,1)S(1)} %shard_map.86.refs_1_.refs_5_.refs_3_, bf16[1040,128]{1,0:T(8,128)(2,1)S(1)} %shard_map.87.refs_2_.refs_4_, ...), custom_call_target="tpu_custom_call", output_to_operand_aliasing={{0}: (3, {})} | custom-call | flops 1000 | bytes 1000 | tf_op jit(solution)/shard_map/pallas_call | solution.py:301
  45.8 0.1 collective-permute-start.17
  45.9 1.5 %collective-permute-done.15.refs_0_ = bf16[1040,128]{1,0:T(8,128)(2,1)S(1)} collective-permute-done((bf16[1040,128]{1,0:T(8,128)(2,1)S(1)}, bf16[1040,128]{1,0:T(8,128)(2,1)S(1)}, u32[]{:S(2)}, u32[]{:S(2)}) %collective-permute-start.15) | collective-permute-done | bytes 266272 | tf_op jit(solution)/shard_map/ppermute | solution.py:510
  47.4 0.0 collective-permute-start.16
  47.4 0.0 collective-permute-done.10.refs_0_
  47.4 0.5 collective-permute-start.14
  47.9 2.4 %shard_map.91 = (f32[768,768]{1,0:T(8,128)S(1)}, f32[8,128]{1,0:T(8,128)}) custom-call(bf16[2048,1536]{1,0:T(8,128)(2,1)S(1)} %bitcast.15, bf16[1040,128]{1,0:T(8,128)(2,1)S(1)} %shard_map.89.refs_1_, bf16[1040,128]{1,0:T(8,128)(2,1)S(1)} %shard_map.90.refs_2_, ...), custom_call_target="tpu_custom_call", output_to_operand_aliasing={{0}: (5, {})} | custom-call | flops 99999997952 | bytes 1000 | tf_op jit(solution)/shard_map/pallas_call | solution.py:301
  50.3 0.0 collective-permute-done.16.refs_2_
  50.3 0.0 collective-permute-done.14.refs_1_
  50.3 0.0 collective-permute-done.17.refs_4_
  50.3 2.8 %shard_map.92 = (f32[768,768]{1,0:T(8,128)S(1)}, bf16[2320,128]{1,0:T(8,128)(2,1)S(1)}) custom-call(bf16[2048,1536]{1,0:T(8,128)(2,1)S(1)} %bitcast.16, bf16[1040,128]{1,0:T(8,128)(2,1)S(1)} %collective-permute-done.14.refs_1_, bf16[1040,128]{1,0:T(8,128)(2,1)S(1)} %collective-permute-done.16.refs_2_, ...), custom_call_target="tpu_custom_call", output_to_operand_aliasing={{0}: (3, {})} | custom-call | flops 1000 | bytes 1000 | tf_op jit(solution)/shard_map/pallas_call | solution.py:301
  53.1 1.6 %collective-permute-start.18 = (bf16[2320,128]{1,0:T(8,128)(2,1)S(1)}, bf16[2320,128]{1,0:T(8,128)(2,1)S(1)}, u32[]{:S(2)}, u32[]{:S(2)}) collective-permute-start(bf16[2320,128]{1,0:T(8,128)(2,1)S(1)} %get-tuple-element.52), channel_id=1, source_target_pairs={{0,1},{1,0},{2,3},{3,2},{4,5},{5,4},{6,7},{7,6},{8,9},{9,8},{10,11... | collective-permute-start | bytes 1781768 | tf_op jit(solution)/shard_map/ppermute | solution.py:573
  54.6 1.9 %shard_map.93 = (f32[768,768]{1,0:T(8,128)S(1)}, f32[768,256]{1,0:T(8,128)S(1)}, bf16[2048,768]{1,0:T(8,128)(2,1)S(1)}) custom-call(f32[768,768]{1,0:T(8,128)S(1)} %get-tuple-element.48.own_ref, bf16[768,256]{1,0:T(8,128)(2,1)S(1)} %get-tuple-element.31.refs_1_.high_ref.refs_3_, bf16[768,256]{1,0:T(8,128)(2,1)S(1)} %get-tuple-element.49.low_ref, ...), custom_call_target="tpu_custom_call" | custom-call | flops 905969664 | bytes 3145728 | tf_op jit(solution)/shard_map/pallas_call | solution.py:357
  56.6 12.0 %collective-permute-done.18.refs_2_ = bf16[2320,128]{1,0:T(8,128)(2,1)S(1)} collective-permute-done((bf16[2320,128]{1,0:T(8,128)(2,1)S(1)}, bf16[2320,128]{1,0:T(8,128)(2,1)S(1)}, u32[]{:S(2)}, u32[]{:S(2)}) %collective-permute-start.18) | collective-permute-done | bytes 593952 | tf_op jit(solution)/shard_map/ppermute | solution.py:573
  68.5 5.5 %shard_map.94 = (f32[384,768]{1,0:T(8,128)}, f32[1024,256]{1,0:T(8,128)}) custom-call(f32[768,768]{1,0:T(8,128)S(1)} %get-tuple-element.50.refs_0_, f32[768,256]{1,0:T(8,128)S(1)} %get-tuple-element.51.refs_1_, bf16[2320,128]{1,0:T(8,128)(2,1)S(1)} %collective-permute-done.18.refs_2_, bf16[768,256]{1,0:T(8,128)(2,1)S(1)} %get-tuple-element.31.refs_1_.high_ref.refs_3_, ...), custom_call_target="tpu_custom_call" | custom-call | flops 4227858432 | bytes 6291456 | tf_op jit(solution)/shard_map/pallas_call | solution.py:461
  (15 shorter events, 0.0 us)
Async XLA Ops:
  1.8 9.4 %collective-permute-start.3 = (bf16[1040,128]{1,0:T(8,128)(2,1)S(1)}, bf16[1040,128]{1,0:T(8,128)(2,1)S(1)}, u32[]{:S(2)}, u32[]{:S(2)}) collective-permute-start(bf16[1040,128]{1,0:T(8,128)(2,1)S(1)} %get-tuple-element.30.refs_1_.refs_2_), channel_id=1, source_target_pairs={{12,4},{14,6},{20,12},{22,14},{28,20},{30,22},{24,28},{26,30},{16,... | collective-permute-start | bytes 798728 | tf_op jit(solution)/shard_map/ppermute | solution.py:510
  4.9 8.8 %collective-permute-start = (bf16[1040,128]{1,0:T(8,128)(2,1)S(1)}, bf16[1040,128]{1,0:T(8,128)(2,1)S(1)}, u32[]{:S(2)}, u32[]{:S(2)}) collective-permute-start(bf16[1040,128]{1,0:T(8,128)(2,1)S(1)} %get-tuple-element.29.refs_0_.refs_1_), channel_id=1, source_target_pairs={{4,12},{6,14},{12,20},{14,22},{20,28},{22,30},{28,24},{30,26},{24,... | collective-permute-start | bytes 798728 | tf_op jit(solution)/shard_map/ppermute | solution.py:510
  4.9 16.5 %collective-permute-start.2 = (bf16[2048,1536]{1,0:T(8,128)(2,1)}, bf16[2048,1536]{1,0:T(8,128)(2,1)S(1)}, u32[]{:S(2)}, u32[]{:S(2)}) collective-permute-start(bf16[2048,1536]{1,0:T(8,128)(2,1)} %bitcast.9), channel_id=1, source_target_pairs={{0,2},{2,0},{4,6},{6,4},{8,10},{10,8},{12,14},{14,12},{16,18},{18,... | collective-permute-start | bytes 18874376 | tf_op jit(solution)/shard_map/ppermute | solution.py:510
  4.9 8.8 %slice-start = ((s8[6291456]{0:T(1024)(128)(4,1)}), s8[4194304]{0:T(1024)(128)(4,1)S(1)}, s32[]{:S(2)}) async-start(s8[6291456]{0:T(1024)(128)(4,1)} %bitcast.10), calls=%async_computation | async-start | bytes 8388608
  4.9 8.8 %slice-start.1 = ((s8[6291456]{0:T(1024)(128)(4,1)}), s8[2097152]{0:T(1024)(128)(4,1)S(1)}, s32[]{:S(2)}) async-start(s8[6291456]{0:T(1024)(128)(4,1)} %bitcast.10), calls=%async_computation.1 | async-start | bytes 4194304
  8.3 11.1 %collective-permute-start.4 = (bf16[1040,128]{1,0:T(8,128)(2,1)S(1)}, bf16[1040,128]{1,0:T(8,128)(2,1)S(1)}, u32[]{:S(2)}, u32[]{:S(2)}) collective-permute-start(bf16[1040,128]{1,0:T(8,128)(2,1)S(1)} %get-tuple-element.32), channel_id=1, source_target_pairs={{4,12},{6,14},{12,20},{14,22},{20,28},{22,30},{28,24},{30,26},{24,... | collective-permute-start | bytes 798728 | tf_op jit(solution)/shard_map/ppermute | solution.py:510
  10.3 9.2 %collective-permute-start.5 = (bf16[1040,128]{1,0:T(8,128)(2,1)S(1)}, bf16[1040,128]{1,0:T(8,128)(2,1)S(1)}, u32[]{:S(2)}, u32[]{:S(2)}) collective-permute-start(bf16[1040,128]{1,0:T(8,128)(2,1)S(1)} %get-tuple-element.34), channel_id=1, source_target_pairs={{12,4},{14,6},{20,12},{22,14},{28,20},{30,22},{24,28},{26,30},{16,... | collective-permute-start | bytes 798728 | tf_op jit(solution)/shard_map/ppermute | solution.py:510
  11.2 14.0 %collective-permute-start.7 = (bf16[1040,128]{1,0:T(8,128)(2,1)S(1)}, bf16[1040,128]{1,0:T(8,128)(2,1)S(1)}, u32[]{:S(2)}, u32[]{:S(2)}) collective-permute-start(bf16[1040,128]{1,0:T(8,128)(2,1)S(1)} %shard_map.71.refs_4_.refs_6_), channel_id=1, source_target_pairs={{12,4},{14,6},{20,12},{22,14},{28,20},{30,22},{24,28},{26,30},{16,... | collective-permute-start | bytes 798728 | tf_op jit(solution)/shard_map/ppermute | solution.py:510
  13.7 11.7 %collective-permute-start.1 = (bf16[1040,128]{1,0:T(8,128)(2,1)S(1)}, bf16[1040,128]{1,0:T(8,128)(2,1)S(1)}, u32[]{:S(2)}, u32[]{:S(2)}) collective-permute-start(bf16[1040,128]{1,0:T(8,128)(2,1)S(1)} %shard_map.70.refs_3_.refs_5_), channel_id=1, source_target_pairs={{4,12},{6,14},{12,20},{14,22},{20,28},{22,30},{28,24},{30,26},{24,... | collective-permute-start | bytes 798728 | tf_op jit(solution)/shard_map/ppermute | solution.py:510
  19.4 11.4 %collective-permute-start.8 = (bf16[1040,128]{1,0:T(8,128)(2,1)S(1)}, bf16[1040,128]{1,0:T(8,128)(2,1)S(1)}, u32[]{:S(2)}, u32[]{:S(2)}) collective-permute-start(bf16[1040,128]{1,0:T(8,128)(2,1)S(1)} %shard_map.73.refs_5_.refs_2_), channel_id=1, source_target_pairs={{4,12},{6,14},{12,20},{14,22},{20,28},{22,30},{28,24},{30,26},{24,... | collective-permute-start | bytes 798728 | tf_op jit(solution)/shard_map/ppermute | solution.py:510
  19.5 11.8 %collective-permute-start.9 = (bf16[1040,128]{1,0:T(8,128)(2,1)S(1)}, bf16[1040,128]{1,0:T(8,128)(2,1)S(1)}, u32[]{:S(2)}, u32[]{:S(2)}) collective-permute-start(bf16[1040,128]{1,0:T(8,128)(2,1)S(1)} %shard_map.74.refs_6_.refs_1_), channel_id=1, source_target_pairs={{12,4},{14,6},{20,12},{22,14},{28,20},{30,22},{24,28},{26,30},{16,... | collective-permute-start | bytes 798728 | tf_op jit(solution)/shard_map/ppermute | solution.py:510
  25.2 11.4 %collective-permute-start.12 = (bf16[1040,128]{1,0:T(8,128)(2,1)S(1)}, bf16[1040,128]{1,0:T(8,128)(2,1)S(1)}, u32[]{:S(2)}, u32[]{:S(2)}) collective-permute-start(bf16[1040,128]{1,0:T(8,128)(2,1)S(1)} %shard_map.77.refs_4_.refs_7_), channel_id=1, source_target_pairs={{12,4},{14,6},{20,12},{22,14},{28,20},{30,22},{24,28},{26,30},{16,... | collective-permute-start | bytes 798728 | tf_op jit(solution)/shard_map/ppermute | solution.py:510
  25.3 11.4 %collective-permute-start.6 = (bf16[1040,128]{1,0:T(8,128)(2,1)S(1)}, bf16[1040,128]{1,0:T(8,128)(2,1)S(1)}, u32[]{:S(2)}, u32[]{:S(2)}) collective-permute-start(bf16[1040,128]{1,0:T(8,128)(2,1)S(1)} %shard_map.76.refs_3_.refs_6_), channel_id=1, source_target_pairs={{4,12},{6,14},{12,20},{14,22},{20,28},{22,30},{28,24},{30,26},{24,... | collective-permute-start | bytes 798728 | tf_op jit(solution)/shard_map/ppermute | solution.py:510
  30.8 12.7 %collective-permute-start.13 = (bf16[1040,128]{1,0:T(8,128)(2,1)S(1)}, bf16[1040,128]{1,0:T(8,128)(2,1)S(1)}, u32[]{:S(2)}, u32[]{:S(2)}) collective-permute-start(bf16[1040,128]{1,0:T(8,128)(2,1)S(1)} %shard_map.79.refs_6_.refs_2_), channel_id=1, source_target_pairs={{4,12},{6,14},{12,20},{14,22},{20,28},{22,30},{28,24},{30,26},{24,... | collective-permute-start | bytes 798728 | tf_op jit(solution)/shard_map/ppermute | solution.py:510
  31.3 12.2 %collective-permute-start.11 = (bf16[1040,128]{1,0:T(8,128)(2,1)S(1)}, bf16[1040,128]{1,0:T(8,128)(2,1)S(1)}, u32[]{:S(2)}, u32[]{:S(2)}) collective-permute-start(bf16[1040,128]{1,0:T(8,128)(2,1)S(1)} %shard_map.80.refs_7_.refs_1_), channel_id=1, source_target_pairs={{12,4},{14,6},{20,12},{22,14},{28,20},{30,22},{24,28},{26,30},{16,... | collective-permute-start | bytes 798728 | tf_op jit(solution)/shard_map/ppermute | solution.py:510
  36.7 10.7 %collective-permute-start.15 = (bf16[1040,128]{1,0:T(8,128)(2,1)S(1)}, bf16[1040,128]{1,0:T(8,128)(2,1)S(1)}, u32[]{:S(2)}, u32[]{:S(2)}) collective-permute-start(bf16[1040,128]{1,0:T(8,128)(2,1)S(1)} %shard_map.83.refs_4_.refs_7_), channel_id=1, source_target_pairs={{12,4},{14,6},{20,12},{22,14},{28,20},{30,22},{24,28},{26,30},{16,... | collective-permute-start | bytes 798728 | tf_op jit(solution)/shard_map/ppermute | solution.py:510
  36.7 10.6 %collective-permute-start.10 = (bf16[1040,128]{1,0:T(8,128)(2,1)S(1)}, bf16[1040,128]{1,0:T(8,128)(2,1)S(1)}, u32[]{:S(2)}, u32[]{:S(2)}) collective-permute-start(bf16[1040,128]{1,0:T(8,128)(2,1)S(1)} %shard_map.82.refs_3_.refs_6_), channel_id=1, source_target_pairs={{4,12},{6,14},{12,20},{14,22},{20,28},{22,30},{28,24},{30,26},{24,... | collective-permute-start | bytes 798728 | tf_op jit(solution)/shard_map/ppermute | solution.py:510
  45.8 4.5 %collective-permute-start.17 = (bf16[2688,128]{1,0:T(8,128)(2,1)S(1)}, bf16[2688,128]{1,0:T(8,128)(2,1)S(1)}, u32[]{:S(2)}, u32[]{:S(2)}) collective-permute-start(bf16[2688,128]{1,0:T(8,128)(2,1)S(1)} %get-tuple-element.45.refs_1_), channel_id=1, source_target_pairs={{0,2},{2,0},{4,6},{6,4},{8,10},{10,8},{12,14},{14,12},{16,18},{18,... | collective-permute-start | bytes 2064392 | tf_op jit(solution)/shard_map/ppermute | solution.py:510
  47.4 2.9 %collective-permute-start.16 = (bf16[1040,128]{1,0:T(8,128)(2,1)S(1)}, bf16[1040,128]{1,0:T(8,128)(2,1)S(1)}, u32[]{:S(2)}, u32[]{:S(2)}) collective-permute-start(bf16[1040,128]{1,0:T(8,128)(2,1)S(1)} %shard_map.90.refs_2_), channel_id=1, source_target_pairs={{0,2},{2,0},{4,6},{6,4},{8,10},{10,8},{12,14},{14,12},{16,18},{18,... | collective-permute-start | bytes 798728 | tf_op jit(solution)/shard_map/ppermute | solution.py:510
  47.4 2.9 %collective-permute-start.14 = (bf16[1040,128]{1,0:T(8,128)(2,1)S(1)}, bf16[1040,128]{1,0:T(8,128)(2,1)S(1)}, u32[]{:S(2)}, u32[]{:S(2)}) collective-permute-start(bf16[1040,128]{1,0:T(8,128)(2,1)S(1)} %shard_map.89.refs_1_), channel_id=1, source_target_pairs={{0,2},{2,0},{4,6},{6,4},{8,10},{10,8},{12,14},{14,12},{16,18},{18,... | collective-permute-start | bytes 798728 | tf_op jit(solution)/shard_map/ppermute | solution.py:510
  53.1 15.5 %collective-permute-start.18 = (bf16[2320,128]{1,0:T(8,128)(2,1)S(1)}, bf16[2320,128]{1,0:T(8,128)(2,1)S(1)}, u32[]{:S(2)}, u32[]{:S(2)}) collective-permute-start(bf16[2320,128]{1,0:T(8,128)(2,1)S(1)} %get-tuple-element.52), channel_id=1, source_target_pairs={{0,1},{1,0},{2,3},{3,2},{4,5},{5,4},{6,7},{7,6},{8,9},{9,8},{10,11... | collective-permute-start | bytes 1781768 | tf_op jit(solution)/shard_map/ppermute | solution.py:573

commit v5 on v4

--- a/solution.py
+++ b/solution.py
@@ -30,6 +30,10 @@
 
 def kept(shape, dtype):
     return pltpu.VMEM(tuple(shape), dtype)
+
+
+def small_cost(hides):
+    return pl.CostEstimate(flops=10**11 if hides else 1000, bytes_accessed=1000, transcendentals=0)
 
 
 def params(mib):
@@ -125,7 +129,7 @@
             pltpu.SemaphoreType.DMA((2,)),
         ],
         compiler_params=params(6),
-        cost_estimate=pl.CostEstimate(flops=10**11, bytes_accessed=1000, transcendentals=0),
+        cost_estimate=small_cost(True),
     )(far(w_down), far(sketch), *map(here, halves))
 
 
@@ -133,7 +137,7 @@
     pass
 
 
-def after(tie, array, *others):
+def after(tie, array, *others, hides=False):
     operands = (array, tie, *others)
     return pl.pallas_call(
         nothing_kernel,
@@ -142,7 +146,7 @@
         out_specs=VMEM,
         input_output_aliases={0: 0},
         compiler_params=params(2),
-        cost_estimate=pl.CostEstimate(flops=1000, bytes_accessed=1000, transcendentals=0),
+        cost_estimate=small_cost(hides),
     )(*map(here, operands))
 
 
@@ -286,7 +290,6 @@
     gives="tie",
     scale=1.0,
     wait=(),
-    hides=False,
 ):
     hidden_width, width = weights.shape[1] // 2, weights.shape[0]
     count = hidden_width // LANES
@@ -320,11 +323,7 @@
             pltpu.VMEM((hidden_width, rows), BF16),
         ],
         compiler_params=params(8),
-        cost_estimate=pl.CostEstimate(
-            flops=10**11 if hides else 1000,
-            bytes_accessed=1000,
-            transcendentals=0,
-        ),
+        cost_estimate=small_cost(False),
     )(*map(here, operands))
 
 
@@ -518,39 +517,39 @@
     *reduced, first, second = prepare(halves)
     sent[2] = (send(second, onward), send(first, backward))
     tie = reduced[0]
-    blocks, mine, others, tiles, pair = [halves], None, None, None, []
+    groups = [(i, i + 1) for i in range(slots % 2, slots, 2)]
+    groups = [(0,)] * (slots % 2) + groups
+    work = {s: [] for s in range(1, slots + 1)}
+    for group in groups:
+        at = max(group[-1], 1)
+        last = group == groups[-1]
+        work[at].append((group, last))
+        work[at if last or len(group) == 1 else at + 1].append((group, not last))
+    blocks, mine, others, tiles = [halves], None, None, None
     for s in range(1, slots + 1):
         came = [after(tie, array) for array in sent[s]]
         if s + 2 <= slots:
             sent[s + 2] = (send(came[0], onward), send(came[1], backward))
         blocks.append(came if s % 2 else came[::-1])
-        if s == slots:
-            pieces = swap(blocks[s])
-            mine, tie = ffn(weights, [*blocks[s], *blocks[s - 1]], mine, tok_dev, hides=True)
-            return *ffn(weights, pieces, mine, tok_dev, tiles, gives="packed", scale=scale), reduced
-        if s == slots - 1:
-            others, tie = ffn(
-                weights_s, blocks[s], others, tok_dev, for_sibling=True, gives="tiles", wait=came
-            )
-            tiles = send(tie, sibling)
-            continue
-        if s % 2:
-            pair = [*blocks[s - 1], *blocks[s]]
-        if s == slots - 2 or s % 2 == 0:
-            others, tie = ffn(
-                weights_s,
-                pair,
-                others,
-                tok_dev,
-                for_sibling=True,
-                wait=came,
-            )
-            if s == slots - 2:
-                mine, tie = ffn(weights, pair, mine, tok_dev, wait=[tie])
-        else:
-            mine, tie = ffn(weights, pair, mine, tok_dev, wait=came)
-        if s % 2 == 0:
-            pair = []
+        for group, for_sibling in work[s]:
+            pieces = [half for i in group for half in blocks[i]]
+            wait = [*came, tie]
+            if for_sibling:
+                gives = "tiles" if group == groups[-1] else "tie"
+                others, tie = ffn(
+                    weights_s, pieces, others, tok_dev, for_sibling=True, gives=gives, wait=wait
+                )
+                if gives == "tiles":
+                    tiles = send(tie, sibling)
+            else:
+                mine, tie = ffn(weights, pieces, mine, tok_dev, wait=wait)
+    swapped = swap(blocks[slots])
+    tie = after(came[0], tie, came[1], hides=True)
+    pieces = [*blocks[slots], *swapped]
+    return (
+        *ffn(weights, pieces, mine, tok_dev, tiles, gives="packed", scale=scale, wait=[tie]),
+        reduced,
+    )
 
 
 def on_device(tokens, routes, gate_up, down_weight, sketch):

time: 74.4 us -> 73.8 us (level)
    ppermute x18, waiting for transfers between devices: 10.5 us -> 9.73 us  [send(): return lax.ppermute(array, 'expert', pairs)]
  transfers between devices with their start and end apart: 19 -> 19, of which waited for: 8 -> 12; matrix products, arithmetic and copies ran while one was open for 0% -> 0% of each run, Pallas kernels for 32% -> 32%
where the time goes in v5:
time: 73.8 us; the launch traced here: 73.7 us
  Pallas kernels  33.5 us (45%)
  waiting for transfers between devices  22 us (30%)
  starting transfers between devices  17.3 us (23%)
  between operations  0.93 us (1%)
    pallas_call x9, Pallas kernels, ffn(): pl.pallas_call(functools.partial(ffn_kernel, tok_dev=tok_dev, width=width...  21.5 us
    ppermute x18, starting transfers between devices, send(): return lax.ppermute(array, 'expert', pairs)  15.7 us
    ppermute x1, waiting for transfers between devices, on_device(): other = lax.ppermute(packed, 'group', [(0, 1), (1, 0)])  12.3 us
    ppermute x18, waiting for transfers between devices, send(): return lax.ppermute(array, 'expert', pairs)  9.73 us
    pallas_call x1, Pallas kernels, power(): pl.pallas_call(functools.partial(power_kernel, has_other=other is not Non...  5.52 us
    pallas_call x1, Pallas kernels, reduced_first(): pl.pallas_call(reduce_kernel, out_shape=(half, half, *(kept(array.shape,...  3.41 us
    pallas_call x1, Pallas kernels, own_side(): pl.pallas_call(own_kernel, out_shape=(kept((hidden_width, hidden_width),...  1.91 us
    ppermute x1, starting transfers between devices, on_device(): other = lax.ppermute(packed, 'group', [(0, 1), (1, 0)])  1.58 us
  transfers between devices with their start and end apart: 19, of which 12 were waited for; matrix products, arithmetic and copies ran while one was open for 0% of the time, Pallas kernels for 32%

profile of v5, /device:TPU:0, one launch (start us, length us, event | category | flops | bytes accessed | tf_op | source)
XLA Modules:
  0.0 73.7 jit_solution(1859403686764670338)
XLA Ops:
  0.6 1.2 %shard_map.68 = (bf16[1040,128]{1,0:T(8,128)(2,1)S(1)}, bf16[1040,128]{1,0:T(8,128)(2,1)S(1)}) custom-call(bf16[128,2048]{1,0:T(8,128)(2,1)} %bitcast.19, s32[8,128]{1,0:T(8,128)} %bitcast.20), custom_call_target="tpu_custom_call" | custom-call | bytes 1048576 | tf_op jit(solution)/shard_map/pallas_call | solution.py:78
  1.8 3.1 %collective-permute-start.2 = (bf16[1040,128]{1,0:T(8,128)(2,1)S(1)}, bf16[1040,128]{1,0:T(8,128)(2,1)S(1)}, u32[]{:S(2)}, u32[]{:S(2)}) collective-permute-start(bf16[1040,128]{1,0:T(8,128)(2,1)S(1)} %get-tuple-element.31.refs_1_.refs_2_), channel_id=1, source_target_pairs={{12,4},{14,6},{20,12},{22,14},{28,20},{30,22},{24,28},{26,30},{16,... | collective-permute-start | bytes 798728 | tf_op jit(solution)/shard_map/ppermute | solution.py:509
  4.9 0.0 collective-permute-start
  4.9 0.0 collective-permute-start.4
  4.9 0.0 slice-start
  4.9 0.0 slice-start.1
  4.9 3.4 %shard_map.69 = (bf16[768,256]{1,0:T(8,128)(2,1)S(1)}, bf16[768,256]{1,0:T(8,128)(2,1)S(1)}, bf16[1040,128]{1,0:T(8,128)(2,1)S(1)}, bf16[1040,128]{1,0:T(8,128)(2,1)S(1)}) custom-call(bf16[2048,768]{1,0:T(8,128)(2,1)} %bitcast.17, bf16[2048,256]{1,0:T(8,128)(2,1)} %bitcast.21, bf16[1040,128]{1,0:T(8,128)(2,1)S(1)} %get-tuple-element.30.refs_0_.refs_1_, ...), custom_call_target="tpu_custom_call" | custom-call | flops 99999997952 | bytes 1000 | tf_op jit(solution)/shard_map/pallas_call | solution.py:121
  8.3 2.0 %collective-permute-start.5 = (bf16[1040,128]{1,0:T(8,128)(2,1)S(1)}, bf16[1040,128]{1,0:T(8,128)(2,1)S(1)}, u32[]{:S(2)}, u32[]{:S(2)}) collective-permute-start(bf16[1040,128]{1,0:T(8,128)(2,1)S(1)} %get-tuple-element.36), channel_id=1, source_target_pairs={{4,12},{6,14},{12,20},{14,22},{20,28},{22,30},{28,24},{30,26},{24,... | collective-permute-start | bytes 798728 | tf_op jit(solution)/shard_map/ppermute | solution.py:509
  10.3 0.1 collective-permute-start.3
  10.4 0.8 %collective-permute-done.2.refs_0_ = bf16[1040,128]{1,0:T(8,128)(2,1)S(1)} collective-permute-done((bf16[1040,128]{1,0:T(8,128)(2,1)S(1)}, bf16[1040,128]{1,0:T(8,128)(2,1)S(1)}, u32[]{:S(2)}, u32[]{:S(2)}) %collective-permute-start.2) | collective-permute-done | bytes 266272 | tf_op jit(solution)/shard_map/ppermute | solution.py:509
  11.2 1.8 %collective-permute-start.7 = (bf16[1040,128]{1,0:T(8,128)(2,1)S(1)}, bf16[1040,128]{1,0:T(8,128)(2,1)S(1)}, u32[]{:S(2)}, u32[]{:S(2)}) collective-permute-start(bf16[1040,128]{1,0:T(8,128)(2,1)S(1)} %shard_map.71.refs_4_.refs_2_), channel_id=1, source_target_pairs={{12,4},{14,6},{20,12},{22,14},{28,20},{30,22},{24,28},{26,30},{16,... | collective-permute-start | bytes 798728 | tf_op jit(solution)/shard_map/ppermute | solution.py:509
  13.0 0.7 collective-permute-done.refs_0_
  13.7 0.0 collective-permute-start.1
  13.7 0.0 slice-done
  13.7 0.0 slice-done.1
  13.7 2.2 %shard_map.72 = (f32[768,768]{1,0:T(8,128)S(1)}, f32[8,128]{1,0:T(8,128)S(1)}) custom-call(bf16[2048,1536]{1,0:T(8,128)(2,1)S(1)} %bitcast.12, bf16[1040,128]{1,0:T(8,128)(2,1)S(1)} %get-tuple-element.30.refs_0_.refs_1_, bf16[1040,128]{1,0:T(8,128)(2,1)S(1)} %get-tuple-element.31.refs_1_.refs_2_, bf16[1040,128]{1,0:T(8,128)(2,1)S(1)} %shard_map.70.refs_3_.refs_1_, ...), custom_call_target="tpu_custom_call" | custom-call | flops 1000 | bytes 1000 | tf_op jit(solution)/shard_map/pallas_call | solution.py:304
  15.9 0.0 collective-permute-done.4.refs_0_
  15.9 2.2 %shard_map.73 = (f32[768,768]{1,0:T(8,128)S(1)}, f32[8,128]{1,0:T(8,128)S(1)}) custom-call(bf16[2048,1536]{1,0:T(8,128)(2,1)S(1)} %collective-permute-done.4.refs_0_, bf16[1040,128]{1,0:T(8,128)(2,1)S(1)} %get-tuple-element.30.refs_0_.refs_1_, bf16[1040,128]{1,0:T(8,128)(2,1)S(1)} %get-tuple-element.31.refs_1_.refs_2_, ...), custom_call_target="tpu_custom_call" | custom-call | flops 1000 | bytes 1000 | tf_op jit(solution)/shard_map/pallas_call | solution.py:304
  18.1 1.3 %collective-permute-done.5.refs_0_ = bf16[1040,128]{1,0:T(8,128)(2,1)S(1)} collective-permute-done((bf16[1040,128]{1,0:T(8,128)(2,1)S(1)}, bf16[1040,128]{1,0:T(8,128)(2,1)S(1)}, u32[]{:S(2)}, u32[]{:S(2)}) %collective-permute-start.5) | collective-permute-done | bytes 266272 | tf_op jit(solution)/shard_map/ppermute | solution.py:509
  19.4 0.1 collective-permute-start.9
  19.5 0.0 collective-permute-done.3.refs_0_
  19.5 1.9 %collective-permute-start.8 = (bf16[1040,128]{1,0:T(8,128)(2,1)S(1)}, bf16[1040,128]{1,0:T(8,128)(2,1)S(1)}, u32[]{:S(2)}, u32[]{:S(2)}) collective-permute-start(bf16[1040,128]{1,0:T(8,128)(2,1)S(1)} %shard_map.74.refs_3_.refs_7_), channel_id=1, source_target_pairs={{12,4},{14,6},{20,12},{22,14},{28,20},{30,22},{24,28},{26,30},{16,... | collective-permute-start | bytes 798728 | tf_op jit(solution)/shard_map/ppermute | solution.py:509
  21.4 2.4 %shard_map.76 = (f32[768,768]{1,0:T(8,128)S(1)}, f32[8,128]{1,0:T(8,128)S(1)}) custom-call(bf16[2048,1536]{1,0:T(8,128)(2,1)S(1)} %bitcast.13, bf16[1040,128]{1,0:T(8,128)(2,1)S(1)} %shard_map.70.refs_3_.refs_1_, bf16[1040,128]{1,0:T(8,128)(2,1)S(1)} %shard_map.71.refs_4_.refs_2_, ...), custom_call_target="tpu_custom_call", output_to_operand_aliasing={{0}: (5, {})} | custom-call | flops 1000 | bytes 1000 | tf_op jit(solution)/shard_map/pallas_call | solution.py:304
  23.8 1.5 %collective-permute-done.7.refs_0_ = bf16[1040,128]{1,0:T(8,128)(2,1)S(1)} collective-permute-done((bf16[1040,128]{1,0:T(8,128)(2,1)S(1)}, bf16[1040,128]{1,0:T(8,128)(2,1)S(1)}, u32[]{:S(2)}, u32[]{:S(2)}) %collective-permute-start.7) | collective-permute-done | bytes 266272 | tf_op jit(solution)/shard_map/ppermute | solution.py:509
  25.2 0.1 collective-permute-start.11
  25.3 0.0 collective-permute-done.1.refs_0_
  25.3 1.9 %collective-permute-start.6 = (bf16[1040,128]{1,0:T(8,128)(2,1)S(1)}, bf16[1040,128]{1,0:T(8,128)(2,1)S(1)}, u32[]{:S(2)}, u32[]{:S(2)}) collective-permute-start(bf16[1040,128]{1,0:T(8,128)(2,1)S(1)} %shard_map.77.refs_6_.refs_1_), channel_id=1, source_target_pairs={{4,12},{6,14},{12,20},{14,22},{20,28},{22,30},{28,24},{30,26},{24,... | collective-permute-start | bytes 798728 | tf_op jit(solution)/shard_map/ppermute | solution.py:509
  27.3 2.4 %shard_map.79 = (f32[768,768]{1,0:T(8,128)S(1)}, f32[8,128]{1,0:T(8,128)S(1)}) custom-call(bf16[2048,1536]{1,0:T(8,128)(2,1)S(1)} %collective-permute-done.4.refs_0_, bf16[1040,128]{1,0:T(8,128)(2,1)S(1)} %shard_map.70.refs_3_.refs_1_, bf16[1040,128]{1,0:T(8,128)(2,1)S(1)} %shard_map.71.refs_4_.refs_2_, ...), custom_call_target="tpu_custom_call", output_to_operand_aliasing={{0}: (5, {})} | custom-call | flops 1000 | bytes 1000 | tf_op jit(solution)/shard_map/pallas_call | solution.py:304
  29.6 1.1 %collective-permute-done.9.refs_0_ = bf16[1040,128]{1,0:T(8,128)(2,1)S(1)} collective-permute-done((bf16[1040,128]{1,0:T(8,128)(2,1)S(1)}, bf16[1040,128]{1,0:T(8,128)(2,1)S(1)}, u32[]{:S(2)}, u32[]{:S(2)}) %collective-permute-start.9) | collective-permute-done | bytes 266272 | tf_op jit(solution)/shard_map/ppermute | solution.py:509
  30.8 0.5 collective-permute-start.13
  31.3 0.0 collective-permute-done.8.refs_0_
  31.3 1.5 %collective-permute-start.12 = (bf16[1040,128]{1,0:T(8,128)(2,1)S(1)}, bf16[1040,128]{1,0:T(8,128)(2,1)S(1)}, u32[]{:S(2)}, u32[]{:S(2)}) collective-permute-start(bf16[1040,128]{1,0:T(8,128)(2,1)S(1)} %shard_map.80.refs_3_.refs_7_), channel_id=1, source_target_pairs={{12,4},{14,6},{20,12},{22,14},{28,20},{30,22},{24,28},{26,30},{16,... | collective-permute-start | bytes 798728 | tf_op jit(solution)/shard_map/ppermute | solution.py:509
  32.8 2.4 %shard_map.82 = (f32[768,768]{1,0:T(8,128)S(1)}, f32[8,128]{1,0:T(8,128)S(1)}) custom-call(bf16[2048,1536]{1,0:T(8,128)(2,1)S(1)} %bitcast.14, bf16[1040,128]{1,0:T(8,128)(2,1)S(1)} %shard_map.77.refs_6_.refs_1_, bf16[1040,128]{1,0:T(8,128)(2,1)S(1)} %shard_map.78.refs_7_.refs_2_, ...), custom_call_target="tpu_custom_call", output_to_operand_aliasing={{0}: (5, {})} | custom-call | flops 1000 | bytes 1000 | tf_op jit(solution)/shard_map/pallas_call | solution.py:304
  35.2 1.5 %collective-permute-done.11.refs_0_ = bf16[1040,128]{1,0:T(8,128)(2,1)S(1)} collective-permute-done((bf16[1040,128]{1,0:T(8,128)(2,1)S(1)}, bf16[1040,128]{1,0:T(8,128)(2,1)S(1)}, u32[]{:S(2)}, u32[]{:S(2)}) %collective-permute-start.11) | collective-permute-done | bytes 266272 | tf_op jit(solution)/shard_map/ppermute | solution.py:509
  36.7 0.1 collective-permute-start.14
  36.7 0.0 collective-permute-done.6.refs_0_
  36.7 1.9 %collective-permute-start.10 = (bf16[1040,128]{1,0:T(8,128)(2,1)S(1)}, bf16[1040,128]{1,0:T(8,128)(2,1)S(1)}, u32[]{:S(2)}, u32[]{:S(2)}) collective-permute-start(bf16[1040,128]{1,0:T(8,128)(2,1)S(1)} %shard_map.83.refs_6_.refs_1_), channel_id=1, source_target_pairs={{4,12},{6,14},{12,20},{14,22},{20,28},{22,30},{28,24},{30,26},{24,... | collective-permute-start | bytes 798728 | tf_op jit(solution)/shard_map/ppermute | solution.py:509
  38.7 2.4 %shard_map.85 = (f32[768,768]{1,0:T(8,128)S(1)}, f32[8,128]{1,0:T(8,128)S(1)}) custom-call(bf16[2048,1536]{1,0:T(8,128)(2,1)S(1)} %collective-permute-done.4.refs_0_, bf16[1040,128]{1,0:T(8,128)(2,1)S(1)} %shard_map.77.refs_6_.refs_1_, bf16[1040,128]{1,0:T(8,128)(2,1)S(1)} %shard_map.78.refs_7_.refs_2_, ...), custom_call_target="tpu_custom_call", output_to_operand_aliasing={{0}: (5, {})} | custom-call | flops 1000 | bytes 1000 | tf_op jit(solution)/shard_map/pallas_call | solution.py:304
  41.0 1.1 %collective-permute-done.13.refs_0_ = bf16[1040,128]{1,0:T(8,128)(2,1)S(1)} collective-permute-done((bf16[1040,128]{1,0:T(8,128)(2,1)S(1)}, bf16[1040,128]{1,0:T(8,128)(2,1)S(1)}, u32[]{:S(2)}, u32[]{:S(2)}) %collective-permute-start.13) | collective-permute-done | bytes 266272 | tf_op jit(solution)/shard_map/ppermute | solution.py:509
  42.2 0.2 collective-permute-done.12.refs_0_
  42.4 2.4 %shard_map.88 = (f32[768,768]{1,0:T(8,128)S(1)}, bf16[2688,128]{1,0:T(8,128)(2,1)S(1)}) custom-call(bf16[2048,1536]{1,0:T(8,128)(2,1)S(1)} %collective-permute-done.4.refs_0_, bf16[1040,128]{1,0:T(8,128)(2,1)S(1)} %shard_map.83.refs_6_.refs_1_, bf16[1040,128]{1,0:T(8,128)(2,1)S(1)} %shard_map.84.refs_7_.refs_2_, ...), custom_call_target="tpu_custom_call", output_to_operand_aliasing={{0}: (5, {})} | custom-call | flops 1000 | bytes 1000 | tf_op jit(solution)/shard_map/pallas_call | solution.py:304
  44.8 0.1 collective-permute-start.17
  44.9 2.4 %shard_map.89 = (f32[768,768]{1,0:T(8,128)S(1)}, f32[8,128]{1,0:T(8,128)S(1)}) custom-call(bf16[2048,1536]{1,0:T(8,128)(2,1)S(1)} %bitcast.15, bf16[1040,128]{1,0:T(8,128)(2,1)S(1)} %shard_map.83.refs_6_.refs_1_, bf16[1040,128]{1,0:T(8,128)(2,1)S(1)} %shard_map.84.refs_7_.refs_2_, ...), custom_call_target="tpu_custom_call", output_to_operand_aliasing={{0}: (5, {})} | custom-call | flops 1000 | bytes 1000 | tf_op jit(solution)/shard_map/pallas_call | solution.py:304
  47.2 0.1 collective-permute-done.14.refs_0_
  47.4 0.5 collective-permute-start.16
  47.8 0.0 collective-permute-done.10.refs_0_
  47.8 0.1 collective-permute-start.15
  47.9 1.1 %collective-permute-done.16.refs_4_ = bf16[1040,128]{1,0:T(8,128)(2,1)S(1)} collective-permute-done((bf16[1040,128]{1,0:T(8,128)(2,1)S(1)}, bf16[1040,128]{1,0:T(8,128)(2,1)S(1)}, u32[]{:S(2)}, u32[]{:S(2)}) %collective-permute-start.16) | collective-permute-done | bytes 266272 | tf_op jit(solution)/shard_map/ppermute | solution.py:509
  49.0 0.4 collective-permute-done.15.refs_3_
  49.4 0.0 collective-permute-done.17.refs_6_
  49.4 2.9 %shard_map.93 = (f32[768,768]{1,0:T(8,128)S(1)}, bf16[2320,128]{1,0:T(8,128)(2,1)S(1)}) custom-call(bf16[2048,1536]{1,0:T(8,128)(2,1)S(1)} %bitcast.16, bf16[1040,128]{1,0:T(8,128)(2,1)S(1)} %shard_map.90.refs_1_, bf16[1040,128]{1,0:T(8,128)(2,1)S(1)} %shard_map.91.refs_2_, ...), custom_call_target="tpu_custom_call", output_to_operand_aliasing={{0}: (5, {})} | custom-call | flops 1000 | bytes 1000 | tf_op jit(solution)/shard_map/pallas_call | solution.py:304
  52.2 1.6 %collective-permute-start.18 = (bf16[2320,128]{1,0:T(8,128)(2,1)S(1)}, bf16[2320,128]{1,0:T(8,128)(2,1)S(1)}, u32[]{:S(2)}, u32[]{:S(2)}) collective-permute-start(bf16[2320,128]{1,0:T(8,128)(2,1)S(1)} %get-tuple-element.54), channel_id=1, source_target_pairs={{0,1},{1,0},{2,3},{3,2},{4,5},{5,4},{6,7},{7,6},{8,9},{9,8},{10,11... | collective-permute-start | bytes 1781768 | tf_op jit(solution)/shard_map/ppermute | solution.py:572
  53.8 1.9 %shard_map.94 = (f32[768,768]{1,0:T(8,128)S(1)}, f32[768,256]{1,0:T(8,128)S(1)}, bf16[2048,768]{1,0:T(8,128)(2,1)S(1)}) custom-call(f32[768,768]{1,0:T(8,128)S(1)} %get-tuple-element.50.own_ref, bf16[768,256]{1,0:T(8,128)(2,1)S(1)} %get-tuple-element.32.refs_1_.refs_5_.high_ref.refs_3_, bf16[768,256]{1,0:T(8,128)(2,1)S(1)} %get-tuple-element.51.low_ref, ...), custom_call_target="tpu_custom_call" | custom-call | flops 905969664 | bytes 3145728 | tf_op jit(solution)/shard_map/pallas_call | solution.py:356
  55.7 12.3 %collective-permute-done.18.refs_2_ = bf16[2320,128]{1,0:T(8,128)(2,1)S(1)} collective-permute-done((bf16[2320,128]{1,0:T(8,128)(2,1)S(1)}, bf16[2320,128]{1,0:T(8,128)(2,1)S(1)}, u32[]{:S(2)}, u32[]{:S(2)}) %collective-permute-start.18) | collective-permute-done | bytes 593952 | tf_op jit(solution)/shard_map/ppermute | solution.py:572
  68.0 5.5 %shard_map.95 = (f32[384,768]{1,0:T(8,128)}, f32[1024,256]{1,0:T(8,128)}) custom-call(f32[768,768]{1,0:T(8,128)S(1)} %get-tuple-element.52.refs_0_, f32[768,256]{1,0:T(8,128)S(1)} %get-tuple-element.53.refs_1_, bf16[2320,128]{1,0:T(8,128)(2,1)S(1)} %collective-permute-done.18.refs_2_, ...), custom_call_target="tpu_custom_call" | custom-call | flops 4227858432 | bytes 6291456 | tf_op jit(solution)/shard_map/pallas_call | solution.py:460
  (16 shorter events, 0.0 us)
Async XLA Ops:
  1.8 9.4 %collective-permute-start.2 = (bf16[1040,128]{1,0:T(8,128)(2,1)S(1)}, bf16[1040,128]{1,0:T(8,128)(2,1)S(1)}, u32[]{:S(2)}, u32[]{:S(2)}) collective-permute-start(bf16[1040,128]{1,0:T(8,128)(2,1)S(1)} %get-tuple-element.31.refs_1_.refs_2_), channel_id=1, source_target_pairs={{12,4},{14,6},{20,12},{22,14},{28,20},{30,22},{24,28},{26,30},{16,... | collective-permute-start | bytes 798728 | tf_op jit(solution)/shard_map/ppermute | solution.py:509
  4.9 8.8 %collective-permute-start = (bf16[1040,128]{1,0:T(8,128)(2,1)S(1)}, bf16[1040,128]{1,0:T(8,128)(2,1)S(1)}, u32[]{:S(2)}, u32[]{:S(2)}) collective-permute-start(bf16[1040,128]{1,0:T(8,128)(2,1)S(1)} %get-tuple-element.30.refs_0_.refs_1_), channel_id=1, source_target_pairs={{4,12},{6,14},{12,20},{14,22},{20,28},{22,30},{28,24},{30,26},{24,... | collective-permute-start | bytes 798728 | tf_op jit(solution)/shard_map/ppermute | solution.py:509
  4.9 11.0 %collective-permute-start.4 = (bf16[2048,1536]{1,0:T(8,128)(2,1)}, bf16[2048,1536]{1,0:T(8,128)(2,1)S(1)}, u32[]{:S(2)}, u32[]{:S(2)}) collective-permute-start(bf16[2048,1536]{1,0:T(8,128)(2,1)} %bitcast.9), channel_id=1, source_target_pairs={{0,2},{2,0},{4,6},{6,4},{8,10},{10,8},{12,14},{14,12},{16,18},{18,... | collective-permute-start | bytes 18874376 | tf_op jit(solution)/shard_map/ppermute | solution.py:509
  4.9 8.8 %slice-start = ((s8[6291456]{0:T(1024)(128)(4,1)}), s8[4194304]{0:T(1024)(128)(4,1)S(1)}, s32[]{:S(2)}) async-start(s8[6291456]{0:T(1024)(128)(4,1)} %bitcast.10), calls=%async_computation | async-start | bytes 8388608
  4.9 8.8 %slice-start.1 = ((s8[6291456]{0:T(1024)(128)(4,1)}), s8[2097152]{0:T(1024)(128)(4,1)S(1)}, s32[]{:S(2)}) async-start(s8[6291456]{0:T(1024)(128)(4,1)} %bitcast.10), calls=%async_computation.1 | async-start | bytes 4194304
  8.3 11.1 %collective-permute-start.5 = (bf16[1040,128]{1,0:T(8,128)(2,1)S(1)}, bf16[1040,128]{1,0:T(8,128)(2,1)S(1)}, u32[]{:S(2)}, u32[]{:S(2)}) collective-permute-start(bf16[1040,128]{1,0:T(8,128)(2,1)S(1)} %get-tuple-element.36), channel_id=1, source_target_pairs={{4,12},{6,14},{12,20},{14,22},{20,28},{22,30},{28,24},{30,26},{24,... | collective-permute-start | bytes 798728 | tf_op jit(solution)/shard_map/ppermute | solution.py:509
  10.3 9.2 %collective-permute-start.3 = (bf16[1040,128]{1,0:T(8,128)(2,1)S(1)}, bf16[1040,128]{1,0:T(8,128)(2,1)S(1)}, u32[]{:S(2)}, u32[]{:S(2)}) collective-permute-start(bf16[1040,128]{1,0:T(8,128)(2,1)S(1)} %get-tuple-element.33), channel_id=1, source_target_pairs={{12,4},{14,6},{20,12},{22,14},{28,20},{30,22},{24,28},{26,30},{16,... | collective-permute-start | bytes 798728 | tf_op jit(solution)/shard_map/ppermute | solution.py:509
  11.2 14.0 %collective-permute-start.7 = (bf16[1040,128]{1,0:T(8,128)(2,1)S(1)}, bf16[1040,128]{1,0:T(8,128)(2,1)S(1)}, u32[]{:S(2)}, u32[]{:S(2)}) collective-permute-start(bf16[1040,128]{1,0:T(8,128)(2,1)S(1)} %shard_map.71.refs_4_.refs_2_), channel_id=1, source_target_pairs={{12,4},{14,6},{20,12},{22,14},{28,20},{30,22},{24,28},{26,30},{16,... | collective-permute-start | bytes 798728 | tf_op jit(solution)/shard_map/ppermute | solution.py:509
  13.7 11.7 %collective-permute-start.1 = (bf16[1040,128]{1,0:T(8,128)(2,1)S(1)}, bf16[1040,128]{1,0:T(8,128)(2,1)S(1)}, u32[]{:S(2)}, u32[]{:S(2)}) collective-permute-start(bf16[1040,128]{1,0:T(8,128)(2,1)S(1)} %shard_map.70.refs_3_.refs_1_), channel_id=1, source_target_pairs={{4,12},{6,14},{12,20},{14,22},{20,28},{22,30},{28,24},{30,26},{24,... | collective-permute-start | bytes 798728 | tf_op jit(solution)/shard_map/ppermute | solution.py:509
  19.4 11.4 %collective-permute-start.9 = (bf16[1040,128]{1,0:T(8,128)(2,1)S(1)}, bf16[1040,128]{1,0:T(8,128)(2,1)S(1)}, u32[]{:S(2)}, u32[]{:S(2)}) collective-permute-start(bf16[1040,128]{1,0:T(8,128)(2,1)S(1)} %shard_map.75.refs_4_.refs_6_), channel_id=1, source_target_pairs={{4,12},{6,14},{12,20},{14,22},{20,28},{22,30},{28,24},{30,26},{24,... | collective-permute-start | bytes 798728 | tf_op jit(solution)/shard_map/ppermute | solution.py:509
  19.5 11.8 %collective-permute-start.8 = (bf16[1040,128]{1,0:T(8,128)(2,1)S(1)}, bf16[1040,128]{1,0:T(8,128)(2,1)S(1)}, u32[]{:S(2)}, u32[]{:S(2)}) collective-permute-start(bf16[1040,128]{1,0:T(8,128)(2,1)S(1)} %shard_map.74.refs_3_.refs_7_), channel_id=1, source_target_pairs={{12,4},{14,6},{20,12},{22,14},{28,20},{30,22},{24,28},{26,30},{16,... | collective-permute-start | bytes 798728 | tf_op jit(solution)/shard_map/ppermute | solution.py:509
  25.2 11.4 %collective-permute-start.11 = (bf16[1040,128]{1,0:T(8,128)(2,1)S(1)}, bf16[1040,128]{1,0:T(8,128)(2,1)S(1)}, u32[]{:S(2)}, u32[]{:S(2)}) collective-permute-start(bf16[1040,128]{1,0:T(8,128)(2,1)S(1)} %shard_map.78.refs_7_.refs_2_), channel_id=1, source_target_pairs={{12,4},{14,6},{20,12},{22,14},{28,20},{30,22},{24,28},{26,30},{16,... | collective-permute-start | bytes 798728 | tf_op jit(solution)/shard_map/ppermute | solution.py:509
  25.3 11.4 %collective-permute-start.6 = (bf16[1040,128]{1,0:T(8,128)(2,1)S(1)}, bf16[1040,128]{1,0:T(8,128)(2,1)S(1)}, u32[]{:S(2)}, u32[]{:S(2)}) collective-permute-start(bf16[1040,128]{1,0:T(8,128)(2,1)S(1)} %shard_map.77.refs_6_.refs_1_), channel_id=1, source_target_pairs={{4,12},{6,14},{12,20},{14,22},{20,28},{22,30},{28,24},{30,26},{24,... | collective-permute-start | bytes 798728 | tf_op jit(solution)/shard_map/ppermute | solution.py:509
  30.8 11.4 %collective-permute-start.13 = (bf16[1040,128]{1,0:T(8,128)(2,1)S(1)}, bf16[1040,128]{1,0:T(8,128)(2,1)S(1)}, u32[]{:S(2)}, u32[]{:S(2)}) collective-permute-start(bf16[1040,128]{1,0:T(8,128)(2,1)S(1)} %shard_map.81.refs_4_.refs_6_), channel_id=1, source_target_pairs={{4,12},{6,14},{12,20},{14,22},{20,28},{22,30},{28,24},{30,26},{24,... | collective-permute-start | bytes 798728 | tf_op jit(solution)/shard_map/ppermute | solution.py:509
  31.3 11.1 %collective-permute-start.12 = (bf16[1040,128]{1,0:T(8,128)(2,1)S(1)}, bf16[1040,128]{1,0:T(8,128)(2,1)S(1)}, u32[]{:S(2)}, u32[]{:S(2)}) collective-permute-start(bf16[1040,128]{1,0:T(8,128)(2,1)S(1)} %shard_map.80.refs_3_.refs_7_), channel_id=1, source_target_pairs={{12,4},{14,6},{20,12},{22,14},{28,20},{30,22},{24,28},{26,30},{16,... | collective-permute-start | bytes 798728 | tf_op jit(solution)/shard_map/ppermute | solution.py:509
  36.7 10.7 %collective-permute-start.14 = (bf16[1040,128]{1,0:T(8,128)(2,1)S(1)}, bf16[1040,128]{1,0:T(8,128)(2,1)S(1)}, u32[]{:S(2)}, u32[]{:S(2)}) collective-permute-start(bf16[1040,128]{1,0:T(8,128)(2,1)S(1)} %shard_map.84.refs_7_.refs_2_), channel_id=1, source_target_pairs={{12,4},{14,6},{20,12},{22,14},{28,20},{30,22},{24,28},{26,30},{16,... | collective-permute-start | bytes 798728 | tf_op jit(solution)/shard_map/ppermute | solution.py:509
  36.7 11.1 %collective-permute-start.10 = (bf16[1040,128]{1,0:T(8,128)(2,1)S(1)}, bf16[1040,128]{1,0:T(8,128)(2,1)S(1)}, u32[]{:S(2)}, u32[]{:S(2)}) collective-permute-start(bf16[1040,128]{1,0:T(8,128)(2,1)S(1)} %shard_map.83.refs_6_.refs_1_), channel_id=1, source_target_pairs={{4,12},{6,14},{12,20},{14,22},{20,28},{22,30},{28,24},{30,26},{24,... | collective-permute-start | bytes 798728 | tf_op jit(solution)/shard_map/ppermute | solution.py:509
  44.8 4.6 %collective-permute-start.17 = (bf16[2688,128]{1,0:T(8,128)(2,1)S(1)}, bf16[2688,128]{1,0:T(8,128)(2,1)S(1)}, u32[]{:S(2)}, u32[]{:S(2)}) collective-permute-start(bf16[2688,128]{1,0:T(8,128)(2,1)S(1)} %get-tuple-element.47.refs_8_), channel_id=1, source_target_pairs={{0,2},{2,0},{4,6},{6,4},{8,10},{10,8},{12,14},{14,12},{16,18},{18,... | collective-permute-start | bytes 2064392 | tf_op jit(solution)/shard_map/ppermute | solution.py:509
  47.4 1.6 %collective-permute-start.16 = (bf16[1040,128]{1,0:T(8,128)(2,1)S(1)}, bf16[1040,128]{1,0:T(8,128)(2,1)S(1)}, u32[]{:S(2)}, u32[]{:S(2)}) collective-permute-start(bf16[1040,128]{1,0:T(8,128)(2,1)S(1)} %shard_map.91.refs_2_), channel_id=1, source_target_pairs={{0,2},{2,0},{4,6},{6,4},{8,10},{10,8},{12,14},{14,12},{16,18},{18,... | collective-permute-start | bytes 798728 | tf_op jit(solution)/shard_map/ppermute | solution.py:509
  47.8 1.5 %collective-permute-start.15 = (bf16[1040,128]{1,0:T(8,128)(2,1)S(1)}, bf16[1040,128]{1,0:T(8,128)(2,1)S(1)}, u32[]{:S(2)}, u32[]{:S(2)}) collective-permute-start(bf16[1040,128]{1,0:T(8,128)(2,1)S(1)} %shard_map.90.refs_1_), channel_id=1, source_target_pairs={{0,2},{2,0},{4,6},{6,4},{8,10},{10,8},{12,14},{14,12},{16,18},{18,... | collective-permute-start | bytes 798728 | tf_op jit(solution)/shard_map/ppermute | solution.py:509
  52.2 15.8 %collective-permute-start.18 = (bf16[2320,128]{1,0:T(8,128)(2,1)S(1)}, bf16[2320,128]{1,0:T(8,128)(2,1)S(1)}, u32[]{:S(2)}, u32[]{:S(2)}) collective-permute-start(bf16[2320,128]{1,0:T(8,128)(2,1)S(1)} %get-tuple-element.54), channel_id=1, source_target_pairs={{0,1},{1,0},{2,3},{3,2},{4,5},{5,4},{6,7},{7,6},{8,9},{9,8},{10,11... | collective-permute-start | bytes 1781768 | tf_op jit(solution)/shard_map/ppermute | solution.py:572

commit v6 on v5

--- a/solution.py
+++ b/solution.py
@@ -333,22 +333,24 @@
     return total + product(high, other_high, NN)
 
 
-def own_kernel(own_ref, high_ref, low_ref, w_hbm, full_ref, panel_ref, w_ref, sem):
+def own_kernel(own_ref, high_ref, low_ref, w_hbm, full_ref, panel_ref, w_ref, square_ref, sem):
     copy = pltpu.make_async_copy(w_hbm, w_ref, sem)
     copy.start()
-    count = own_ref.shape[0] // LANES
-    for a in range(count):
-        for b in range(a, count):
-            rows, columns = slice(a * LANES, (a + 1) * LANES), slice(b * LANES, (b + 1) * LANES)
-            tile = own_ref[rows, columns]
-            full_ref[rows, columns] = tile
-            if a != b:
-                full_ref[columns, rows] = tile.T
-    for first in range(0, own_ref.shape[0], 2 * LANES):
-        rows = slice(first, min(first + 2 * LANES, own_ref.shape[0]))
+    for _, rows, columns in tiles_of(own_ref):
+        tile = own_ref[rows, columns]
+        full_ref[rows, columns] = tile
+        if rows != columns:
+            full_ref[columns, rows] = tile.T
+    hidden_width = own_ref.shape[0]
+    step_rows = gram_step(hidden_width)
+    for first in range(0, hidden_width, step_rows):
+        rows = slice(first, first + step_rows)
         high, low = split(full_ref[rows, :])
         panel_ref[rows, :] = exact(high, low, high_ref[...], low_ref[...])
     copy.wait()
+    for first in range(0, hidden_width, step_rows):
+        rows = slice(first, first + step_rows)
+        square_ref[rows, :] = product(w_ref[:, rows], w_ref[...], TN).astype(BF16)
 
 
 def own_side(own, high, low, w_down):
@@ -359,16 +361,13 @@
             kept((hidden_width, hidden_width), F32),
             kept((hidden_width, rank), F32),
             kept(w_down.shape, w_down.dtype),
+            kept((hidden_width, hidden_width), BF16),
         ),
         in_specs=[VMEM] * 3 + [pl.BlockSpec(memory_space=pl.ANY)],
-        out_specs=(VMEM, VMEM, VMEM),
+        out_specs=(VMEM,) * 4,
         scratch_shapes=[pltpu.SemaphoreType.DMA],
-        compiler_params=params(4),
-        cost_estimate=pl.CostEstimate(
-            flops=6 * hidden_width * hidden_width * rank,
-            bytes_accessed=w_down.size * 2,
-            transcendentals=0,
-        ),
+        compiler_params=params(6),
+        cost_estimate=small_cost(False),
     )(here(own), here(high), here(low), far(w_down))
 
 
@@ -383,8 +382,8 @@
     refs = list(refs)
     own_ref, panel_ref = refs[:2]
     other_ref = refs.pop(2) if has_other else None
-    first_ref, w_ref, gram_out, power_out = refs[2:6]
-    full_ref, other_full, high_ref, image_ref, probe_ref, small_ref, power_ref, sems = refs[6:]
+    first_ref, w_ref, square_ref, gram_out, power_out = refs[2:7]
+    full_ref, other_full, high_ref, small_ref, power_ref, sems = refs[7:]
     group = lax.axis_index("group")
     hidden_width, rank = panel_ref.shape
     width = w_ref.shape[0]
@@ -394,22 +393,13 @@
         panel += product(other_full[...], first_ref[...], NN)
     small_ref[...] = panel.astype(BF16)
 
-    def image_step(first, rows, squares):
-        image = product(w_ref[pl.ds(first, rows), :], small_ref[...], NN)
-        image_ref[pl.ds(first, rows), :] = image
-        return squares + jnp.sum(image * image, axis=0, keepdims=True)
-
-    squares = blocks_of(width, 8 * LANES, image_step, jnp.zeros((1, rank), F32))
-
-    def gram_step(first, rows, carry):
-        full = own_ref[pl.ds(first, rows), :]
+    for first in range(0, hidden_width, LANES):
+        rows = slice(first, first + LANES)
+        full = own_ref[rows, :]
         if has_other:
-            full += other_full[pl.ds(first, rows), :].astype(F32)
-        full_ref[pl.ds(first, rows), :] = full
-        high_ref[pl.ds(first, rows), :] = full.astype(BF16)
-        return carry
-
-    blocks_of(hidden_width, LANES, gram_step)
+            full += other_full[rows, :].astype(F32)
+        full_ref[rows, :] = full
+        high_ref[rows, :] = full.astype(BF16)
     panel_rows = gram_out.shape[0]
     gram_copy = pltpu.make_async_copy(
         full_ref.at[pl.ds(pl.multiple_of(group * panel_rows, panel_rows), panel_rows), :],
@@ -417,15 +407,11 @@
         sems.at[0],
     )
     gram_copy.start()
-    factor = lax.rsqrt(squares * (1.0 / width) + 1e-06)
-    probe_ref[...] = (image_ref[...] * factor).astype(BF16)
-
-    def reduce_step(first, rows, carry):
-        reduced = product(w_ref[:, pl.ds(first, rows)], probe_ref[...], TN)
-        small_ref[pl.ds(first, rows), :] = reduced.astype(BF16)
-        return carry
-
-    blocks_of(hidden_width, 3 * LANES, reduce_step)
+    panel = small_ref[...]
+    reduced = product(square_ref[...], panel, NN)
+    squares = jnp.sum(panel.astype(F32) * reduced, axis=0, keepdims=True)
+    factor = lax.rsqrt(jnp.maximum(squares, 0.0) * (1.0 / width) + 1e-06)
+    small_ref[...] = (reduced * factor).astype(BF16)
     small_ref[...] = product(high_ref[...], small_ref[...], NN).astype(BF16)
     own_rows = power_ref.shape[0]
 
@@ -450,12 +436,12 @@
     blocks_of(own_rows, 4 * LANES, power_wait)
 
 
-def power(own, other, panel, reduced, w_down, group_count):
+def power(own, other, panel, reduced, w_down, square, group_count):
     width, hidden_width = w_down.shape
     rank = panel.shape[1]
     own_rows = width // group_count
     operands = [own, panel] + ([] if other is None else [other])
-    operands += [reduced[0], w_down]
+    operands += [reduced[0], w_down, square]
     anywhere = pl.BlockSpec(memory_space=pl.ANY)
     return pl.pallas_call(
         functools.partial(power_kernel, has_other=other is not None),
@@ -469,8 +455,6 @@
             pltpu.VMEM((hidden_width, hidden_width), F32),
             pltpu.VMEM((hidden_width, hidden_width), BF16),
             pltpu.VMEM((hidden_width, hidden_width), BF16),
-            pltpu.VMEM((width, rank), F32),
-            pltpu.VMEM((width, rank), BF16),
             pltpu.VMEM((hidden_width, rank), BF16),
             pltpu.VMEM((own_rows, rank), F32),
             pltpu.SemaphoreType.DMA((1 + max(1, own_rows // (4 * LANES)),)),
@@ -572,8 +556,8 @@
         other = lax.ppermute(packed, "group", [(0, 1), (1, 0)])
     else:
         own, other = lax.psum(own, "group"), None
-    own, panel, w_down = own_side(own, *reduced, w_down)
-    gram, result = power(own, other, panel, reduced, w_down, group_count)
+    own, panel, w_down, square = own_side(own, *reduced, w_down)
+    gram, result = power(own, other, panel, reduced, w_down, square, group_count)
     return gram[None], result[None]
 
 

time: 73.8 us -> 71.9 us (0.974)
  waiting for transfers between devices: 22 us -> 19.1 us
  Pallas kernels: 33.5 us -> 34.5 us
    ppermute x1, waiting for transfers between devices: 12.3 us -> 9.34 us  [on_device(): other = lax.ppermute(packed, 'group', [(0, 1), (1, 0)])]
    pallas_call x1, Pallas kernels: 1.91 us -> 4.83 us  [own_side(): pl.pallas_call(own_kernel, out_shape=(kept((hidden_width, hidden_width),...]
    pallas_call x1, Pallas kernels: 5.52 us -> 3.59 us  [power(): pl.pallas_call(functools.partial(power_kernel, has_other=other is not Non...]
  transfers between devices with their start and end apart: 19 -> 19, of which waited for: 12 -> 12; matrix products, arithmetic and copies ran while one was open for 0% -> 0% of each run, Pallas kernels for 32% -> 37%
where the time goes in v6:
time: 71.9 us; the launch traced here: 71.7 us
  Pallas kernels  34.5 us (48%)
  waiting for transfers between devices  19.1 us (27%)
  starting transfers between devices  17.3 us (24%)
  between operations  0.93 us (1%)
    pallas_call x9, Pallas kernels, ffn(): pl.pallas_call(functools.partial(ffn_kernel, tok_dev=tok_dev, width=width...  21.5 us
    ppermute x18, starting transfers between devices, send(): return lax.ppermute(array, 'expert', pairs)  15.7 us
    ppermute x18, waiting for transfers between devices, send(): return lax.ppermute(array, 'expert', pairs)  9.73 us
    ppermute x1, waiting for transfers between devices, on_device(): other = lax.ppermute(packed, 'group', [(0, 1), (1, 0)])  9.34 us
    pallas_call x1, Pallas kernels, own_side(): pl.pallas_call(own_kernel, out_shape=(kept((hidden_width, hidden_width),...  4.83 us
    pallas_call x1, Pallas kernels, power(): pl.pallas_call(functools.partial(power_kernel, has_other=other is not Non...  3.59 us
    pallas_call x1, Pallas kernels, reduced_first(): pl.pallas_call(reduce_kernel, out_shape=(half, half, *(kept(array.shape,...  3.41 us
    ppermute x1, starting transfers between devices, on_device(): other = lax.ppermute(packed, 'group', [(0, 1), (1, 0)])  1.58 us
  transfers between devices with their start and end apart: 19, of which 12 were waited for; matrix products, arithmetic and copies ran while one was open for 0% of the time, Pallas kernels for 37%

profile of v6, /device:TPU:0, one launch (start us, length us, event | category | flops | bytes accessed | tf_op | source)
XLA Modules:
  0.0 71.7 jit_solution(15626297321381771995)
XLA Ops:
  0.6 1.2 %shard_map.68 = (bf16[1040,128]{1,0:T(8,128)(2,1)S(1)}, bf16[1040,128]{1,0:T(8,128)(2,1)S(1)}) custom-call(bf16[128,2048]{1,0:T(8,128)(2,1)} %bitcast.19, s32[8,128]{1,0:T(8,128)} %bitcast.20), custom_call_target="tpu_custom_call" | custom-call | bytes 1048576 | tf_op jit(solution)/shard_map/pallas_call | solution.py:78
  1.8 3.1 %collective-permute-start.2 = (bf16[1040,128]{1,0:T(8,128)(2,1)S(1)}, bf16[1040,128]{1,0:T(8,128)(2,1)S(1)}, u32[]{:S(2)}, u32[]{:S(2)}) collective-permute-start(bf16[1040,128]{1,0:T(8,128)(2,1)S(1)} %get-tuple-element.32.refs_1_.refs_2_), channel_id=1, source_target_pairs={{12,4},{14,6},{20,12},{22,14},{28,20},{30,22},{24,28},{26,30},{16,... | collective-permute-start | bytes 798728 | tf_op jit(solution)/shard_map/ppermute | solution.py:493
  4.9 0.0 collective-permute-start
  4.9 0.0 collective-permute-start.4
  4.9 0.0 slice-start
  4.9 0.0 slice-start.1
  4.9 3.4 %shard_map.69 = (bf16[768,256]{1,0:T(8,128)(2,1)S(1)}, bf16[768,256]{1,0:T(8,128)(2,1)S(1)}, bf16[1040,128]{1,0:T(8,128)(2,1)S(1)}, bf16[1040,128]{1,0:T(8,128)(2,1)S(1)}) custom-call(bf16[2048,768]{1,0:T(8,128)(2,1)} %bitcast.17, bf16[2048,256]{1,0:T(8,128)(2,1)} %bitcast.21, bf16[1040,128]{1,0:T(8,128)(2,1)S(1)} %get-tuple-element.31.refs_0_.refs_1_, ...), custom_call_target="tpu_custom_call" | custom-call | flops 99999997952 | bytes 1000 | tf_op jit(solution)/shard_map/pallas_call | solution.py:121
  8.3 2.0 %collective-permute-start.5 = (bf16[1040,128]{1,0:T(8,128)(2,1)S(1)}, bf16[1040,128]{1,0:T(8,128)(2,1)S(1)}, u32[]{:S(2)}, u32[]{:S(2)}) collective-permute-start(bf16[1040,128]{1,0:T(8,128)(2,1)S(1)} %get-tuple-element.37), channel_id=1, source_target_pairs={{4,12},{6,14},{12,20},{14,22},{20,28},{22,30},{28,24},{30,26},{24,... | collective-permute-start | bytes 798728 | tf_op jit(solution)/shard_map/ppermute | solution.py:493
  10.3 0.1 collective-permute-start.3
  10.4 0.8 %collective-permute-done.2.refs_0_ = bf16[1040,128]{1,0:T(8,128)(2,1)S(1)} collective-permute-done((bf16[1040,128]{1,0:T(8,128)(2,1)S(1)}, bf16[1040,128]{1,0:T(8,128)(2,1)S(1)}, u32[]{:S(2)}, u32[]{:S(2)}) %collective-permute-start.2) | collective-permute-done | bytes 266272 | tf_op jit(solution)/shard_map/ppermute | solution.py:493
  11.2 1.8 %collective-permute-start.7 = (bf16[1040,128]{1,0:T(8,128)(2,1)S(1)}, bf16[1040,128]{1,0:T(8,128)(2,1)S(1)}, u32[]{:S(2)}, u32[]{:S(2)}) collective-permute-start(bf16[1040,128]{1,0:T(8,128)(2,1)S(1)} %shard_map.71.refs_4_.refs_2_), channel_id=1, source_target_pairs={{12,4},{14,6},{20,12},{22,14},{28,20},{30,22},{24,28},{26,30},{16,... | collective-permute-start | bytes 798728 | tf_op jit(solution)/shard_map/ppermute | solution.py:493
  13.0 0.7 collective-permute-done.refs_0_
  13.7 0.0 collective-permute-start.1
  13.7 0.0 slice-done
  13.7 0.0 slice-done.1
  13.7 2.2 %shard_map.72 = (f32[768,768]{1,0:T(8,128)S(1)}, f32[8,128]{1,0:T(8,128)S(1)}) custom-call(bf16[2048,1536]{1,0:T(8,128)(2,1)S(1)} %bitcast.12, bf16[1040,128]{1,0:T(8,128)(2,1)S(1)} %get-tuple-element.31.refs_0_.refs_1_, bf16[1040,128]{1,0:T(8,128)(2,1)S(1)} %get-tuple-element.32.refs_1_.refs_2_, bf16[1040,128]{1,0:T(8,128)(2,1)S(1)} %shard_map.70.refs_3_.refs_1_, ...), custom_call_target="tpu_custom_call" | custom-call | flops 1000 | bytes 1000 | tf_op jit(solution)/shard_map/pallas_call | solution.py:304
  15.9 0.0 collective-permute-done.4.refs_0_
  15.9 2.2 %shard_map.73 = (f32[768,768]{1,0:T(8,128)S(1)}, f32[8,128]{1,0:T(8,128)S(1)}) custom-call(bf16[2048,1536]{1,0:T(8,128)(2,1)S(1)} %collective-permute-done.4.refs_0_, bf16[1040,128]{1,0:T(8,128)(2,1)S(1)} %get-tuple-element.31.refs_0_.refs_1_, bf16[1040,128]{1,0:T(8,128)(2,1)S(1)} %get-tuple-element.32.refs_1_.refs_2_, ...), custom_call_target="tpu_custom_call" | custom-call | flops 1000 | bytes 1000 | tf_op jit(solution)/shard_map/pallas_call | solution.py:304
  18.1 1.3 %collective-permute-done.5.refs_0_ = bf16[1040,128]{1,0:T(8,128)(2,1)S(1)} collective-permute-done((bf16[1040,128]{1,0:T(8,128)(2,1)S(1)}, bf16[1040,128]{1,0:T(8,128)(2,1)S(1)}, u32[]{:S(2)}, u32[]{:S(2)}) %collective-permute-start.5) | collective-permute-done | bytes 266272 | tf_op jit(solution)/shard_map/ppermute | solution.py:493
  19.4 0.1 collective-permute-start.9
  19.5 0.0 collective-permute-done.3.refs_0_
  19.5 1.9 %collective-permute-start.8 = (bf16[1040,128]{1,0:T(8,128)(2,1)S(1)}, bf16[1040,128]{1,0:T(8,128)(2,1)S(1)}, u32[]{:S(2)}, u32[]{:S(2)}) collective-permute-start(bf16[1040,128]{1,0:T(8,128)(2,1)S(1)} %shard_map.74.refs_3_.refs_7_), channel_id=1, source_target_pairs={{12,4},{14,6},{20,12},{22,14},{28,20},{30,22},{24,28},{26,30},{16,... | collective-permute-start | bytes 798728 | tf_op jit(solution)/shard_map/ppermute | solution.py:493
  21.4 2.4 %shard_map.76 = (f32[768,768]{1,0:T(8,128)S(1)}, f32[8,128]{1,0:T(8,128)S(1)}) custom-call(bf16[2048,1536]{1,0:T(8,128)(2,1)S(1)} %bitcast.13, bf16[1040,128]{1,0:T(8,128)(2,1)S(1)} %shard_map.70.refs_3_.refs_1_, bf16[1040,128]{1,0:T(8,128)(2,1)S(1)} %shard_map.71.refs_4_.refs_2_, ...), custom_call_target="tpu_custom_call", output_to_operand_aliasing={{0}: (5, {})} | custom-call | flops 1000 | bytes 1000 | tf_op jit(solution)/shard_map/pallas_call | solution.py:304
  23.8 1.5 %collective-permute-done.7.refs_0_ = bf16[1040,128]{1,0:T(8,128)(2,1)S(1)} collective-permute-done((bf16[1040,128]{1,0:T(8,128)(2,1)S(1)}, bf16[1040,128]{1,0:T(8,128)(2,1)S(1)}, u32[]{:S(2)}, u32[]{:S(2)}) %collective-permute-start.7) | collective-permute-done | bytes 266272 | tf_op jit(solution)/shard_map/ppermute | solution.py:493
  25.2 0.1 collective-permute-start.11
  25.3 0.0 collective-permute-done.1.refs_0_
  25.3 1.9 %collective-permute-start.6 = (bf16[1040,128]{1,0:T(8,128)(2,1)S(1)}, bf16[1040,128]{1,0:T(8,128)(2,1)S(1)}, u32[]{:S(2)}, u32[]{:S(2)}) collective-permute-start(bf16[1040,128]{1,0:T(8,128)(2,1)S(1)} %shard_map.77.refs_6_.refs_1_), channel_id=1, source_target_pairs={{4,12},{6,14},{12,20},{14,22},{20,28},{22,30},{28,24},{30,26},{24,... | collective-permute-start | bytes 798728 | tf_op jit(solution)/shard_map/ppermute | solution.py:493
  27.3 2.4 %shard_map.79 = (f32[768,768]{1,0:T(8,128)S(1)}, f32[8,128]{1,0:T(8,128)S(1)}) custom-call(bf16[2048,1536]{1,0:T(8,128)(2,1)S(1)} %collective-permute-done.4.refs_0_, bf16[1040,128]{1,0:T(8,128)(2,1)S(1)} %shard_map.70.refs_3_.refs_1_, bf16[1040,128]{1,0:T(8,128)(2,1)S(1)} %shard_map.71.refs_4_.refs_2_, ...), custom_call_target="tpu_custom_call", output_to_operand_aliasing={{0}: (5, {})} | custom-call | flops 1000 | bytes 1000 | tf_op jit(solution)/shard_map/pallas_call | solution.py:304
  29.6 1.1 %collective-permute-done.9.refs_0_ = bf16[1040,128]{1,0:T(8,128)(2,1)S(1)} collective-permute-done((bf16[1040,128]{1,0:T(8,128)(2,1)S(1)}, bf16[1040,128]{1,0:T(8,128)(2,1)S(1)}, u32[]{:S(2)}, u32[]{:S(2)}) %collective-permute-start.9) | collective-permute-done | bytes 266272 | tf_op jit(solution)/shard_map/ppermute | solution.py:493
  30.8 0.5 collective-permute-start.13
  31.3 0.0 collective-permute-done.8.refs_0_
  31.3 1.5 %collective-permute-start.12 = (bf16[1040,128]{1,0:T(8,128)(2,1)S(1)}, bf16[1040,128]{1,0:T(8,128)(2,1)S(1)}, u32[]{:S(2)}, u32[]{:S(2)}) collective-permute-start(bf16[1040,128]{1,0:T(8,128)(2,1)S(1)} %shard_map.80.refs_3_.refs_7_), channel_id=1, source_target_pairs={{12,4},{14,6},{20,12},{22,14},{28,20},{30,22},{24,28},{26,30},{16,... | collective-permute-start | bytes 798728 | tf_op jit(solution)/shard_map/ppermute | solution.py:493
  32.8 2.4 %shard_map.82 = (f32[768,768]{1,0:T(8,128)S(1)}, f32[8,128]{1,0:T(8,128)S(1)}) custom-call(bf16[2048,1536]{1,0:T(8,128)(2,1)S(1)} %bitcast.14, bf16[1040,128]{1,0:T(8,128)(2,1)S(1)} %shard_map.77.refs_6_.refs_1_, bf16[1040,128]{1,0:T(8,128)(2,1)S(1)} %shard_map.78.refs_7_.refs_2_, ...), custom_call_target="tpu_custom_call", output_to_operand_aliasing={{0}: (5, {})} | custom-call | flops 1000 | bytes 1000 | tf_op jit(solution)/shard_map/pallas_call | solution.py:304
  35.2 1.5 %collective-permute-done.11.refs_0_ = bf16[1040,128]{1,0:T(8,128)(2,1)S(1)} collective-permute-done((bf16[1040,128]{1,0:T(8,128)(2,1)S(1)}, bf16[1040,128]{1,0:T(8,128)(2,1)S(1)}, u32[]{:S(2)}, u32[]{:S(2)}) %collective-permute-start.11) | collective-permute-done | bytes 266272 | tf_op jit(solution)/shard_map/ppermute | solution.py:493
  36.7 0.1 collective-permute-start.14
  36.7 0.0 collective-permute-done.6.refs_0_
  36.7 1.9 %collective-permute-start.10 = (bf16[1040,128]{1,0:T(8,128)(2,1)S(1)}, bf16[1040,128]{1,0:T(8,128)(2,1)S(1)}, u32[]{:S(2)}, u32[]{:S(2)}) collective-permute-start(bf16[1040,128]{1,0:T(8,128)(2,1)S(1)} %shard_map.83.refs_6_.refs_1_), channel_id=1, source_target_pairs={{4,12},{6,14},{12,20},{14,22},{20,28},{22,30},{28,24},{30,26},{24,... | collective-permute-start | bytes 798728 | tf_op jit(solution)/shard_map/ppermute | solution.py:493
  38.7 2.4 %shard_map.85 = (f32[768,768]{1,0:T(8,128)S(1)}, f32[8,128]{1,0:T(8,128)S(1)}) custom-call(bf16[2048,1536]{1,0:T(8,128)(2,1)S(1)} %collective-permute-done.4.refs_0_, bf16[1040,128]{1,0:T(8,128)(2,1)S(1)} %shard_map.77.refs_6_.refs_1_, bf16[1040,128]{1,0:T(8,128)(2,1)S(1)} %shard_map.78.refs_7_.refs_2_, ...), custom_call_target="tpu_custom_call", output_to_operand_aliasing={{0}: (5, {})} | custom-call | flops 1000 | bytes 1000 | tf_op jit(solution)/shard_map/pallas_call | solution.py:304
  41.0 1.1 %collective-permute-done.13.refs_0_ = bf16[1040,128]{1,0:T(8,128)(2,1)S(1)} collective-permute-done((bf16[1040,128]{1,0:T(8,128)(2,1)S(1)}, bf16[1040,128]{1,0:T(8,128)(2,1)S(1)}, u32[]{:S(2)}, u32[]{:S(2)}) %collective-permute-start.13) | collective-permute-done | bytes 266272 | tf_op jit(solution)/shard_map/ppermute | solution.py:493
  42.2 0.2 collective-permute-done.12.refs_0_
  42.4 2.4 %shard_map.88 = (f32[768,768]{1,0:T(8,128)S(1)}, bf16[2688,128]{1,0:T(8,128)(2,1)S(1)}) custom-call(bf16[2048,1536]{1,0:T(8,128)(2,1)S(1)} %collective-permute-done.4.refs_0_, bf16[1040,128]{1,0:T(8,128)(2,1)S(1)} %shard_map.83.refs_6_.refs_1_, bf16[1040,128]{1,0:T(8,128)(2,1)S(1)} %shard_map.84.refs_7_.refs_2_, ...), custom_call_target="tpu_custom_call", output_to_operand_aliasing={{0}: (5, {})} | custom-call | flops 1000 | bytes 1000 | tf_op jit(solution)/shard_map/pallas_call | solution.py:304
  44.8 0.1 collective-permute-start.17
  44.9 2.4 %shard_map.89 = (f32[768,768]{1,0:T(8,128)S(1)}, f32[8,128]{1,0:T(8,128)S(1)}) custom-call(bf16[2048,1536]{1,0:T(8,128)(2,1)S(1)} %bitcast.15, bf16[1040,128]{1,0:T(8,128)(2,1)S(1)} %shard_map.83.refs_6_.refs_1_, bf16[1040,128]{1,0:T(8,128)(2,1)S(1)} %shard_map.84.refs_7_.refs_2_, ...), custom_call_target="tpu_custom_call", output_to_operand_aliasing={{0}: (5, {})} | custom-call | flops 1000 | bytes 1000 | tf_op jit(solution)/shard_map/pallas_call | solution.py:304
  47.2 0.1 collective-permute-done.14.refs_0_
  47.4 0.5 collective-permute-start.16
  47.8 0.0 collective-permute-done.10.refs_0_
  47.8 0.1 collective-permute-start.15
  47.9 1.1 %collective-permute-done.16.refs_4_ = bf16[1040,128]{1,0:T(8,128)(2,1)S(1)} collective-permute-done((bf16[1040,128]{1,0:T(8,128)(2,1)S(1)}, bf16[1040,128]{1,0:T(8,128)(2,1)S(1)}, u32[]{:S(2)}, u32[]{:S(2)}) %collective-permute-start.16) | collective-permute-done | bytes 266272 | tf_op jit(solution)/shard_map/ppermute | solution.py:493
  49.0 0.4 collective-permute-done.15.refs_3_
  49.4 0.0 collective-permute-done.17.refs_6_
  49.4 2.9 %shard_map.93 = (f32[768,768]{1,0:T(8,128)S(1)}, bf16[2320,128]{1,0:T(8,128)(2,1)S(1)}) custom-call(bf16[2048,1536]{1,0:T(8,128)(2,1)S(1)} %bitcast.16, bf16[1040,128]{1,0:T(8,128)(2,1)S(1)} %shard_map.90.refs_1_, bf16[1040,128]{1,0:T(8,128)(2,1)S(1)} %shard_map.91.refs_2_, ...), custom_call_target="tpu_custom_call", output_to_operand_aliasing={{0}: (5, {})} | custom-call | flops 1000 | bytes 1000 | tf_op jit(solution)/shard_map/pallas_call | solution.py:304
  52.2 1.6 %collective-permute-start.18 = (bf16[2320,128]{1,0:T(8,128)(2,1)S(1)}, bf16[2320,128]{1,0:T(8,128)(2,1)S(1)}, u32[]{:S(2)}, u32[]{:S(2)}) collective-permute-start(bf16[2320,128]{1,0:T(8,128)(2,1)S(1)} %get-tuple-element.55), channel_id=1, source_target_pairs={{0,1},{1,0},{2,3},{3,2},{4,5},{5,4},{6,7},{7,6},{8,9},{9,8},{10,11... | collective-permute-start | bytes 1781768 | tf_op jit(solution)/shard_map/ppermute | solution.py:556
  53.8 4.8 %shard_map.94 = (f32[768,768]{1,0:T(8,128)S(1)}, f32[768,256]{1,0:T(8,128)S(1)}, bf16[2048,768]{1,0:T(8,128)(2,1)S(1)}, bf16[768,768]{1,0:T(8,128)(2,1)S(1)}) custom-call(f32[768,768]{1,0:T(8,128)S(1)} %get-tuple-element.51.own_ref, bf16[768,256]{1,0:T(8,128)(2,1)S(1)} %get-tuple-element.33.refs_1_.refs_5_.high_ref.refs_3_, ...), custom_call_target="tpu_custom_call" | custom-call | flops 1000 | bytes 1000 | tf_op jit(solution)/shard_map/pallas_call | solution.py:358
  58.6 9.3 %collective-permute-done.18.refs_2_ = bf16[2320,128]{1,0:T(8,128)(2,1)S(1)} collective-permute-done((bf16[2320,128]{1,0:T(8,128)(2,1)S(1)}, bf16[2320,128]{1,0:T(8,128)(2,1)S(1)}, u32[]{:S(2)}, u32[]{:S(2)}) %collective-permute-start.18) | collective-permute-done | bytes 593952 | tf_op jit(solution)/shard_map/ppermute | solution.py:556
  68.0 3.6 %shard_map.95 = (f32[384,768]{1,0:T(8,128)}, f32[1024,256]{1,0:T(8,128)}) custom-call(f32[768,768]{1,0:T(8,128)S(1)} %get-tuple-element.53.refs_0_, f32[768,256]{1,0:T(8,128)S(1)} %get-tuple-element.54.refs_1_, bf16[2320,128]{1,0:T(8,128)(2,1)S(1)} %collective-permute-done.18.refs_2_, ...), custom_call_target="tpu_custom_call" | custom-call | flops 4227858432 | bytes 6291456 | tf_op jit(solution)/shard_map/pallas_call | solution.py:446
  (16 shorter events, 0.0 us)
Async XLA Ops:
  1.8 9.4 %collective-permute-start.2 = (bf16[1040,128]{1,0:T(8,128)(2,1)S(1)}, bf16[1040,128]{1,0:T(8,128)(2,1)S(1)}, u32[]{:S(2)}, u32[]{:S(2)}) collective-permute-start(bf16[1040,128]{1,0:T(8,128)(2,1)S(1)} %get-tuple-element.32.refs_1_.refs_2_), channel_id=1, source_target_pairs={{12,4},{14,6},{20,12},{22,14},{28,20},{30,22},{24,28},{26,30},{16,... | collective-permute-start | bytes 798728 | tf_op jit(solution)/shard_map/ppermute | solution.py:493
  4.9 8.8 %collective-permute-start = (bf16[1040,128]{1,0:T(8,128)(2,1)S(1)}, bf16[1040,128]{1,0:T(8,128)(2,1)S(1)}, u32[]{:S(2)}, u32[]{:S(2)}) collective-permute-start(bf16[1040,128]{1,0:T(8,128)(2,1)S(1)} %get-tuple-element.31.refs_0_.refs_1_), channel_id=1, source_target_pairs={{4,12},{6,14},{12,20},{14,22},{20,28},{22,30},{28,24},{30,26},{24,... | collective-permute-start | bytes 798728 | tf_op jit(solution)/shard_map/ppermute | solution.py:493
  4.9 11.0 %collective-permute-start.4 = (bf16[2048,1536]{1,0:T(8,128)(2,1)}, bf16[2048,1536]{1,0:T(8,128)(2,1)S(1)}, u32[]{:S(2)}, u32[]{:S(2)}) collective-permute-start(bf16[2048,1536]{1,0:T(8,128)(2,1)} %bitcast.9), channel_id=1, source_target_pairs={{0,2},{2,0},{4,6},{6,4},{8,10},{10,8},{12,14},{14,12},{16,18},{18,... | collective-permute-start | bytes 18874376 | tf_op jit(solution)/shard_map/ppermute | solution.py:493
  4.9 8.8 %slice-start = ((s8[6291456]{0:T(1024)(128)(4,1)}), s8[4194304]{0:T(1024)(128)(4,1)S(1)}, s32[]{:S(2)}) async-start(s8[6291456]{0:T(1024)(128)(4,1)} %bitcast.10), calls=%async_computation | async-start | bytes 8388608
  4.9 8.8 %slice-start.1 = ((s8[6291456]{0:T(1024)(128)(4,1)}), s8[2097152]{0:T(1024)(128)(4,1)S(1)}, s32[]{:S(2)}) async-start(s8[6291456]{0:T(1024)(128)(4,1)} %bitcast.10), calls=%async_computation.1 | async-start | bytes 4194304
  8.3 11.1 %collective-permute-start.5 = (bf16[1040,128]{1,0:T(8,128)(2,1)S(1)}, bf16[1040,128]{1,0:T(8,128)(2,1)S(1)}, u32[]{:S(2)}, u32[]{:S(2)}) collective-permute-start(bf16[1040,128]{1,0:T(8,128)(2,1)S(1)} %get-tuple-element.37), channel_id=1, source_target_pairs={{4,12},{6,14},{12,20},{14,22},{20,28},{22,30},{28,24},{30,26},{24,... | collective-permute-start | bytes 798728 | tf_op jit(solution)/shard_map/ppermute | solution.py:493
  10.3 9.2 %collective-permute-start.3 = (bf16[1040,128]{1,0:T(8,128)(2,1)S(1)}, bf16[1040,128]{1,0:T(8,128)(2,1)S(1)}, u32[]{:S(2)}, u32[]{:S(2)}) collective-permute-start(bf16[1040,128]{1,0:T(8,128)(2,1)S(1)} %get-tuple-element.34), channel_id=1, source_target_pairs={{12,4},{14,6},{20,12},{22,14},{28,20},{30,22},{24,28},{26,30},{16,... | collective-permute-start | bytes 798728 | tf_op jit(solution)/shard_map/ppermute | solution.py:493
  11.2 14.0 %collective-permute-start.7 = (bf16[1040,128]{1,0:T(8,128)(2,1)S(1)}, bf16[1040,128]{1,0:T(8,128)(2,1)S(1)}, u32[]{:S(2)}, u32[]{:S(2)}) collective-permute-start(bf16[1040,128]{1,0:T(8,128)(2,1)S(1)} %shard_map.71.refs_4_.refs_2_), channel_id=1, source_target_pairs={{12,4},{14,6},{20,12},{22,14},{28,20},{30,22},{24,28},{26,30},{16,... | collective-permute-start | bytes 798728 | tf_op jit(solution)/shard_map/ppermute | solution.py:493
  13.7 11.7 %collective-permute-start.1 = (bf16[1040,128]{1,0:T(8,128)(2,1)S(1)}, bf16[1040,128]{1,0:T(8,128)(2,1)S(1)}, u32[]{:S(2)}, u32[]{:S(2)}) collective-permute-start(bf16[1040,128]{1,0:T(8,128)(2,1)S(1)} %shard_map.70.refs_3_.refs_1_), channel_id=1, source_target_pairs={{4,12},{6,14},{12,20},{14,22},{20,28},{22,30},{28,24},{30,26},{24,... | collective-permute-start | bytes 798728 | tf_op jit(solution)/shard_map/ppermute | solution.py:493
  19.4 11.4 %collective-permute-start.9 = (bf16[1040,128]{1,0:T(8,128)(2,1)S(1)}, bf16[1040,128]{1,0:T(8,128)(2,1)S(1)}, u32[]{:S(2)}, u32[]{:S(2)}) collective-permute-start(bf16[1040,128]{1,0:T(8,128)(2,1)S(1)} %shard_map.75.refs_4_.refs_6_), channel_id=1, source_target_pairs={{4,12},{6,14},{12,20},{14,22},{20,28},{22,30},{28,24},{30,26},{24,... | collective-permute-start | bytes 798728 | tf_op jit(solution)/shard_map/ppermute | solution.py:493
  19.5 11.8 %collective-permute-start.8 = (bf16[1040,128]{1,0:T(8,128)(2,1)S(1)}, bf16[1040,128]{1,0:T(8,128)(2,1)S(1)}, u32[]{:S(2)}, u32[]{:S(2)}) collective-permute-start(bf16[1040,128]{1,0:T(8,128)(2,1)S(1)} %shard_map.74.refs_3_.refs_7_), channel_id=1, source_target_pairs={{12,4},{14,6},{20,12},{22,14},{28,20},{30,22},{24,28},{26,30},{16,... | collective-permute-start | bytes 798728 | tf_op jit(solution)/shard_map/ppermute | solution.py:493
  25.2 11.4 %collective-permute-start.11 = (bf16[1040,128]{1,0:T(8,128)(2,1)S(1)}, bf16[1040,128]{1,0:T(8,128)(2,1)S(1)}, u32[]{:S(2)}, u32[]{:S(2)}) collective-permute-start(bf16[1040,128]{1,0:T(8,128)(2,1)S(1)} %shard_map.78.refs_7_.refs_2_), channel_id=1, source_target_pairs={{12,4},{14,6},{20,12},{22,14},{28,20},{30,22},{24,28},{26,30},{16,... | collective-permute-start | bytes 798728 | tf_op jit(solution)/shard_map/ppermute | solution.py:493
  25.3 11.4 %collective-permute-start.6 = (bf16[1040,128]{1,0:T(8,128)(2,1)S(1)}, bf16[1040,128]{1,0:T(8,128)(2,1)S(1)}, u32[]{:S(2)}, u32[]{:S(2)}) collective-permute-start(bf16[1040,128]{1,0:T(8,128)(2,1)S(1)} %shard_map.77.refs_6_.refs_1_), channel_id=1, source_target_pairs={{4,12},{6,14},{12,20},{14,22},{20,28},{22,30},{28,24},{30,26},{24,... | collective-permute-start | bytes 798728 | tf_op jit(solution)/shard_map/ppermute | solution.py:493
  30.8 11.4 %collective-permute-start.13 = (bf16[1040,128]{1,0:T(8,128)(2,1)S(1)}, bf16[1040,128]{1,0:T(8,128)(2,1)S(1)}, u32[]{:S(2)}, u32[]{:S(2)}) collective-permute-start(bf16[1040,128]{1,0:T(8,128)(2,1)S(1)} %shard_map.81.refs_4_.refs_6_), channel_id=1, source_target_pairs={{4,12},{6,14},{12,20},{14,22},{20,28},{22,30},{28,24},{30,26},{24,... | collective-permute-start | bytes 798728 | tf_op jit(solution)/shard_map/ppermute | solution.py:493
  31.3 11.1 %collective-permute-start.12 = (bf16[1040,128]{1,0:T(8,128)(2,1)S(1)}, bf16[1040,128]{1,0:T(8,128)(2,1)S(1)}, u32[]{:S(2)}, u32[]{:S(2)}) collective-permute-start(bf16[1040,128]{1,0:T(8,128)(2,1)S(1)} %shard_map.80.refs_3_.refs_7_), channel_id=1, source_target_pairs={{12,4},{14,6},{20,12},{22,14},{28,20},{30,22},{24,28},{26,30},{16,... | collective-permute-start | bytes 798728 | tf_op jit(solution)/shard_map/ppermute | solution.py:493
  36.7 10.7 %collective-permute-start.14 = (bf16[1040,128]{1,0:T(8,128)(2,1)S(1)}, bf16[1040,128]{1,0:T(8,128)(2,1)S(1)}, u32[]{:S(2)}, u32[]{:S(2)}) collective-permute-start(bf16[1040,128]{1,0:T(8,128)(2,1)S(1)} %shard_map.84.refs_7_.refs_2_), channel_id=1, source_target_pairs={{12,4},{14,6},{20,12},{22,14},{28,20},{30,22},{24,28},{26,30},{16,... | collective-permute-start | bytes 798728 | tf_op jit(solution)/shard_map/ppermute | solution.py:493
  36.7 11.1 %collective-permute-start.10 = (bf16[1040,128]{1,0:T(8,128)(2,1)S(1)}, bf16[1040,128]{1,0:T(8,128)(2,1)S(1)}, u32[]{:S(2)}, u32[]{:S(2)}) collective-permute-start(bf16[1040,128]{1,0:T(8,128)(2,1)S(1)} %shard_map.83.refs_6_.refs_1_), channel_id=1, source_target_pairs={{4,12},{6,14},{12,20},{14,22},{20,28},{22,30},{28,24},{30,26},{24,... | collective-permute-start | bytes 798728 | tf_op jit(solution)/shard_map/ppermute | solution.py:493
  44.8 4.6 %collective-permute-start.17 = (bf16[2688,128]{1,0:T(8,128)(2,1)S(1)}, bf16[2688,128]{1,0:T(8,128)(2,1)S(1)}, u32[]{:S(2)}, u32[]{:S(2)}) collective-permute-start(bf16[2688,128]{1,0:T(8,128)(2,1)S(1)} %get-tuple-element.48.refs_8_), channel_id=1, source_target_pairs={{0,2},{2,0},{4,6},{6,4},{8,10},{10,8},{12,14},{14,12},{16,18},{18,... | collective-permute-start | bytes 2064392 | tf_op jit(solution)/shard_map/ppermute | solution.py:493
  47.4 1.6 %collective-permute-start.16 = (bf16[1040,128]{1,0:T(8,128)(2,1)S(1)}, bf16[1040,128]{1,0:T(8,128)(2,1)S(1)}, u32[]{:S(2)}, u32[]{:S(2)}) collective-permute-start(bf16[1040,128]{1,0:T(8,128)(2,1)S(1)} %shard_map.91.refs_2_), channel_id=1, source_target_pairs={{0,2},{2,0},{4,6},{6,4},{8,10},{10,8},{12,14},{14,12},{16,18},{18,... | collective-permute-start | bytes 798728 | tf_op jit(solution)/shard_map/ppermute | solution.py:493
  47.8 1.5 %collective-permute-start.15 = (bf16[1040,128]{1,0:T(8,128)(2,1)S(1)}, bf16[1040,128]{1,0:T(8,128)(2,1)S(1)}, u32[]{:S(2)}, u32[]{:S(2)}) collective-permute-start(bf16[1040,128]{1,0:T(8,128)(2,1)S(1)} %shard_map.90.refs_1_), channel_id=1, source_target_pairs={{0,2},{2,0},{4,6},{6,4},{8,10},{10,8},{12,14},{14,12},{16,18},{18,... | collective-permute-start | bytes 798728 | tf_op jit(solution)/shard_map/ppermute | solution.py:493
  52.2 15.8 %collective-permute-start.18 = (bf16[2320,128]{1,0:T(8,128)(2,1)S(1)}, bf16[2320,128]{1,0:T(8,128)(2,1)S(1)}, u32[]{:S(2)}, u32[]{:S(2)}) collective-permute-start(bf16[2320,128]{1,0:T(8,128)(2,1)S(1)} %get-tuple-element.55), channel_id=1, source_target_pairs={{0,1},{1,0},{2,3},{3,2},{4,5},{5,4},{6,7},{7,6},{8,9},{9,8},{10,11... | collective-permute-start | bytes 1781768 | tf_op jit(solution)/shard_map/ppermute | solution.py:556

commit v7 on v6

--- a/solution.py
+++ b/solution.py
@@ -9,6 +9,7 @@
 
 TOPK = 8
 LANES = 128
+FRONT = 2
 ID_ROWS = 16
 NT = (((1,), (1,)), ((), ()))
 NN = (((1,), (0,)), ((), ()))
@@ -150,12 +151,17 @@
     )(*map(here, operands))
 
 
-def right_tiles(count):
-    return [(a, b) for a in range(count) for b in range(a + 1, count)]
-
-
-def packed_rows(count):
-    return (len(right_tiles(count)) + (count + 1) // 2) * LANES + ID_ROWS
+def right_tiles(count, part):
+    rows = range(count)[:FRONT] if part == 0 else range(count)[FRONT:]
+    return [(a, b) for a in rows for b in range(a + 1, count)]
+
+
+def pairs_of(count, part):
+    return range(0, min(count, FRONT), 2) if part == 0 else range(FRONT, count, 2)
+
+
+def packed_rows(count, part):
+    return (len(right_tiles(count, part)) + len(pairs_of(count, part))) * LANES + ID_ROWS
 
 
 def tile_places():
@@ -169,9 +175,9 @@
     return 2 * LANES if hidden_width % (2 * LANES) == 0 else LANES
 
 
-def pack_gram(gram_ref, packed_ref):
+def pack_gram(gram_ref, packed_ref, part):
     count = gram_ref.shape[0] // LANES
-    rights = right_tiles(count)
+    rights = right_tiles(count, part)
 
     def tile(a, b):
         return gram_ref[a * LANES : (a + 1) * LANES, b * LANES : (b + 1) * LANES]
@@ -181,16 +187,16 @@
     row, column = tile_places()
     strip = jnp.zeros((ID_ROWS, LANES), F32)
     place = lax.broadcasted_iota(jnp.int32, strip.shape, 0)
-    for pair in range((count + 1) // 2):
-        at = (len(rights) + pair) * LANES
-        both = tile(2 * pair, 2 * pair)
-        if 2 * pair + 1 < count:
-            second = tile(2 * pair + 1, 2 * pair + 1)
+    at = len(rights) * LANES
+    for i, first in enumerate(pairs_of(count, part)):
+        both = tile(first, first)
+        if first + 1 < count:
+            second = tile(first + 1, first + 1)
             diagonal = jnp.sum(jnp.where(row == column, second, 0.0), axis=0, keepdims=True)
-            strip = jnp.where(place == pair, diagonal, strip)
+            strip = jnp.where(place == i, diagonal, strip)
             both = jnp.where(row <= column, both, second)
         packed_ref[at : at + LANES, :] = both.astype(BF16)
-    at = (len(rights) + (count + 1) // 2) * LANES
+        at += LANES
     packed_ref[at : at + ID_ROWS, :] = strip.astype(BF16)
 
 
@@ -207,9 +213,9 @@
         )
 
 
-def unpack_gram(packed_ref, full_ref):
+def unpack_gram(packed_ref, full_ref, part):
     count = full_ref.shape[0] // LANES
-    rights = right_tiles(count)
+    rights = right_tiles(count, part)
 
     def put(a, b, value):
         full_ref[a * LANES : (a + 1) * LANES, b * LANES : (b + 1) * LANES] = value.astype(BF16)
@@ -219,25 +225,25 @@
         put(a, b, value)
         put(b, a, value.astype(F32).T)
     row, column = tile_places()
-    at = (len(rights) + (count + 1) // 2) * LANES
+    pairs = pairs_of(count, part)
+    at = (len(rights) + len(pairs)) * LANES
     strip = packed_ref[at : at + ID_ROWS, :].astype(F32)
-    for pair in range((count + 1) // 2):
-        at = (len(rights) + pair) * LANES
+    for i, first in enumerate(pairs):
+        at = (len(rights) + i) * LANES
         both = packed_ref[at : at + LANES, :].astype(F32)
         turned = both.T
-        put(2 * pair, 2 * pair, jnp.where(row <= column, both, turned))
-        if 2 * pair + 1 < count:
+        put(first, first, jnp.where(row <= column, both, turned))
+        if first + 1 < count:
             second = jnp.where(row > column, both, turned)
-            second = jnp.where(row == column, strip[pair : pair + 1, :], second)
-            put(2 * pair + 1, 2 * pair + 1, second)
-
-
-def ffn_kernel(*refs, tok_dev, width, operands, has_gram, has_tiles, for_sibling, gives, scale):
+            second = jnp.where(row == column, strip[i : i + 1, :], second)
+            put(first + 1, first + 1, second)
+
+
+def ffn_kernel(*refs, tok_dev, width, operands, has_gram, for_sibling, gives, scale):
     weight_ref, pieces = refs[0], refs[1 : 1 + operands]
     rest = list(refs[1 + operands :])
     gram_in = rest.pop(0) if has_gram else None
-    tiles_in = rest.pop(0) if has_tiles else None
-    gram_out, last_out, x_ref, mask_ref, hidden_ref = rest[-5:]
+    gram_out, last_out, hidden_ref, x_ref, mask_ref = rest[-5:]
     half, tiles = tok_dev // 2, width // LANES
     expert = lax.axis_index("expert")
     if for_sibling:
@@ -262,17 +268,10 @@
     gate = product(weight_ref[:, :hidden_width], x_ref[...], TT)
     up = product(weight_ref[:, hidden_width:], x_ref[...], TT)
     hidden_ref[...] = (gate * (0.5 * jnp.tanh(0.5 * gate) + 0.5) * up * mask_ref[0:1, :]).astype(BF16)
-    for first in range(0, hidden_width, step_rows):
-        rows = slice(first, first + step_rows)
-        part = product(hidden_ref[rows, :], hidden_ref[first:, :], NT)
-        if has_gram:
-            part += gram_in[rows, first:]
-        gram_out[rows, first:] = part if tiles_in is not None else part * scale
-    if tiles_in is not None:
-        for at, rows, columns in tiles_of(gram_out):
-            gram_out[rows, columns] = (gram_out[rows, columns] + tiles_in[at, :].astype(F32)) * scale
-    if gives == "packed":
-        pack_gram(gram_out, last_out)
+    for first in range(0, FRONT * LANES if gives == "front" else hidden_width, step_rows):
+        gram_rows(hidden_ref, gram_in, gram_out, first, step_rows, scale)
+    if gives == "front":
+        pack_gram(gram_out, last_out, 0)
     elif gives == "tiles":
         for at, rows, columns in tiles_of(gram_out):
             last_out[at, :] = gram_out[rows, columns].astype(BF16)
@@ -280,12 +279,40 @@
         last_out[...] = jnp.zeros_like(last_out)
 
 
+def gram_rows(hidden_ref, gram_in, gram_out, first, count, scale):
+    rows = slice(first, first + count)
+    part = product(hidden_ref[rows, :], hidden_ref[first:, :], NT)
+    if gram_in is not None:
+        part += gram_in[rows, first:]
+    gram_out[rows, first:] = part * scale
+
+
+def rest_kernel(gram_in, hidden_ref, gram_out, packed_out, *, scale):
+    hidden_width = gram_in.shape[0]
+    step_rows = gram_step(hidden_width)
+    for first in range(FRONT * LANES, hidden_width, step_rows):
+        gram_rows(hidden_ref, gram_in, gram_out, first, step_rows, scale)
+    pack_gram(gram_out, packed_out, 1)
+
+
+def rest_of(gram, hidden, scale):
+    count = gram.shape[0] // LANES
+    return pl.pallas_call(
+        functools.partial(rest_kernel, scale=scale),
+        out_shape=(kept(gram.shape, gram.dtype), kept((packed_rows(count, 1), LANES), BF16)),
+        in_specs=[VMEM, VMEM],
+        out_specs=(VMEM, VMEM),
+        input_output_aliases={0: 0},
+        compiler_params=params(10),
+        cost_estimate=small_cost(False),
+    )(here(gram), here(hidden))
+
+
 def ffn(
     weights,
     pieces,
     gram,
     tok_dev,
-    tiles=None,
     for_sibling=False,
     gives="tie",
     scale=1.0,
@@ -297,10 +324,11 @@
     last = {
         "tie": kept((8, LANES), F32),
         "tiles": kept((len(upper_tiles(count)) * LANES, LANES), BF16),
-        "packed": kept((packed_rows(count), LANES), BF16),
+        "front": kept((packed_rows(count, 0), LANES), BF16),
     }[gives]
-    more = [array for array in (gram, tiles) if array is not None]
-    operands = [weights, *pieces, *more, *wait]
+    hidden = pltpu.VMEM((hidden_width, rows), BF16)
+    front = gives == "front"
+    operands = [weights, *pieces, *([] if gram is None else [gram]), *wait]
     return pl.pallas_call(
         functools.partial(
             ffn_kernel,
@@ -308,23 +336,39 @@
             width=width,
             operands=len(pieces),
             has_gram=gram is not None,
-            has_tiles=tiles is not None,
             for_sibling=for_sibling,
             gives=gives,
             scale=scale,
         ),
-        out_shape=(kept((hidden_width, hidden_width), F32), last),
+        out_shape=(kept((hidden_width, hidden_width), F32), last, *([hidden] * front)),
         in_specs=[VMEM] * len(operands),
-        out_specs=(VMEM, VMEM),
+        out_specs=(VMEM,) * (2 + front),
         input_output_aliases={} if gram is None else {1 + len(pieces): 0},
         scratch_shapes=[
+            *([hidden] * (not front)),
             pltpu.VMEM((rows, width), BF16),
             pltpu.VMEM((8, rows), F32),
-            pltpu.VMEM((hidden_width, rows), BF16),
         ],
         compiler_params=params(8),
         cost_estimate=small_cost(False),
     )(*map(here, operands))
+
+
+def merge_kernel(gram_ref, tiles_ref, tie_ref, out_ref):
+    for at, rows, columns in tiles_of(gram_ref):
+        out_ref[rows, columns] = gram_ref[rows, columns] + tiles_ref[at, :].astype(F32)
+
+
+def merged(gram, tiles, tie):
+    return pl.pallas_call(
+        merge_kernel,
+        out_shape=kept(gram.shape, gram.dtype),
+        in_specs=[VMEM] * 3,
+        out_specs=VMEM,
+        input_output_aliases={0: 0},
+        compiler_params=params(10),
+        cost_estimate=small_cost(False),
+    )(here(gram), here(tiles), here(tie))
 
 
 def exact(high, low, other_high, other_low):
@@ -378,28 +422,58 @@
     )
 
 
+def front_kernel(own_in, panel_in, front_ref, first_ref, own_out, panel_out, other_ref):
+    rows = slice(0, FRONT * LANES)
+    other_ref[FRONT * LANES :, FRONT * LANES :] = jnp.zeros_like(
+        other_ref[FRONT * LANES :, FRONT * LANES :]
+    )
+    unpack_gram(front_ref, other_ref, 0)
+    panel_out[...] = panel_in[...] + product(other_ref[...], first_ref[...], NN)
+    own_out[rows, :] = own_in[rows, :] + other_ref[rows, :].astype(F32)
+
+
+def with_front(own, panel, front, first):
+    return pl.pallas_call(
+        front_kernel,
+        out_shape=(
+            kept(own.shape, F32),
+            kept(panel.shape, F32),
+            kept(own.shape, BF16),
+        ),
+        in_specs=[VMEM] * 4,
+        out_specs=(VMEM,) * 3,
+        input_output_aliases={0: 0, 1: 1},
+        compiler_params=params(10),
+        cost_estimate=small_cost(False),
+    )(*map(here, (own, panel, front, first)))
+
+
 def power_kernel(*refs, has_other):
     refs = list(refs)
     own_ref, panel_ref = refs[:2]
-    other_ref = refs.pop(2) if has_other else None
+    front_ref, rest_ref = [refs.pop(2) for _ in range(2)] if has_other else (None, None)
     first_ref, w_ref, square_ref, gram_out, power_out = refs[2:7]
     full_ref, other_full, high_ref, small_ref, power_ref, sems = refs[7:]
     group = lax.axis_index("group")
     hidden_width, rank = panel_ref.shape
     width = w_ref.shape[0]
-    panel = panel_ref[...]
+    done = FRONT * LANES if has_other else hidden_width
     if has_other:
-        unpack_gram(other_ref, other_full)
-        panel += product(other_full[...], first_ref[...], NN)
-    small_ref[...] = panel.astype(BF16)
-
+        unpack_gram(rest_ref, other_full, 1)
+        small_ref[:done, :] = panel_ref[:done, :].astype(BF16)
+        small_ref[done:, :] = (
+            panel_ref[done:, :] + product(other_full[done:, done:], first_ref[done:, :], NN)
+        ).astype(BF16)
+    else:
+        small_ref[...] = panel_ref[...].astype(BF16)
     for first in range(0, hidden_width, LANES):
         rows = slice(first, first + LANES)
-        full = own_ref[rows, :]
-        if has_other:
-            full += other_full[rows, :].astype(F32)
-        full_ref[rows, :] = full
-        high_ref[rows, :] = full.astype(BF16)
+        if first < done:
+            full_ref[rows, :] = own_ref[rows, :]
+        else:
+            full_ref[rows, :done] = own_ref[rows, :done] + front_ref[rows, :done].astype(F32)
+            full_ref[rows, done:] = own_ref[rows, done:] + other_full[rows, done:].astype(F32)
+        high_ref[rows, :] = full_ref[rows, :].astype(BF16)
     panel_rows = gram_out.shape[0]
     gram_copy = pltpu.make_async_copy(
         full_ref.at[pl.ds(pl.multiple_of(group * panel_rows, panel_rows), panel_rows), :],
@@ -440,11 +514,11 @@
     width, hidden_width = w_down.shape
     rank = panel.shape[1]
     own_rows = width // group_count
-    operands = [own, panel] + ([] if other is None else [other])
+    operands = [own, panel, *other]
     operands += [reduced[0], w_down, square]
     anywhere = pl.BlockSpec(memory_space=pl.ANY)
     return pl.pallas_call(
-        functools.partial(power_kernel, has_other=other is not None),
+        functools.partial(power_kernel, has_other=len(other) > 0),
         out_shape=(
             jax.ShapeDtypeStruct((hidden_width // group_count, hidden_width), F32),
             jax.ShapeDtypeStruct((own_rows, rank), F32),
@@ -529,11 +603,12 @@
                 mine, tie = ffn(weights, pieces, mine, tok_dev, wait=wait)
     swapped = swap(blocks[slots])
     tie = after(came[0], tie, came[1], hides=True)
+    if tiles is not None:
+        mine = merged(mine, tiles, tie)
     pieces = [*blocks[slots], *swapped]
-    return (
-        *ffn(weights, pieces, mine, tok_dev, tiles, gives="packed", scale=scale, wait=[tie]),
-        reduced,
-    )
+    gram, front, hidden = ffn(weights, pieces, mine, tok_dev, gives="front", scale=scale, wait=[tie])
+    gram, rest = rest_of(gram, hidden, scale)
+    return gram, (front, rest), reduced
 
 
 def on_device(tokens, routes, gate_up, down_weight, sketch):
@@ -553,10 +628,13 @@
         functools.partial(reduced_first, w_down, sketch[0]),
     )
     if group_count == 2:
-        other = lax.ppermute(packed, "group", [(0, 1), (1, 0)])
+        other = [lax.ppermute(part, "group", [(0, 1), (1, 0)]) for part in packed]
     else:
-        own, other = lax.psum(own, "group"), None
+        own, other = lax.psum(own, "group"), []
     own, panel, w_down, square = own_side(own, *reduced, w_down)
+    if other:
+        own, panel, front = with_front(own, panel, other[0], reduced[0])
+        other = [front, other[1]]
     gram, result = power(own, other, panel, reduced, w_down, square, group_count)
     return gram[None], result[None]
 

time: 71.9 us -> 71.3 us (level)
  waiting for transfers between devices: 19.1 us -> 17.1 us
  Pallas kernels: 34.5 us -> 35.3 us
    ppermute x1 -> x2, waiting for transfers between devices: 9.34 us -> 7.58 us  [on_device(): other = [lax.ppermute(part, 'group', [(0, 1), (1, 0)]) for part in packed]]
    pallas_call x1 -> x4, Pallas kernels: 3.59 us -> 4.94 us  [the longest x1 3.45 us: power(): pl.pallas_call(functools.partial(power_kernel, has_other=len(other) > 0),...]
    ppermute x1 -> x2, starting transfers between devices: 1.58 us -> 2.17 us  [on_device(): other = [lax.ppermute(part, 'group', [(0, 1), (1, 0)]) for part in packed]]
  transfers between devices with their start and end apart: 19 -> 20, of which waited for: 12 -> 13; matrix products, arithmetic and copies ran while one was open for 0% -> 0% of each run, Pallas kernels for 37% -> 40%
where the time goes in v7:
time: 71.3 us; the launch traced here: 71.2 us
  Pallas kernels  35.3 us (50%)
  starting transfers between devices  17.8 us (25%)
  waiting for transfers between devices  17.1 us (24%)
  between operations  0.96 us (1%)
    pallas_call x9, Pallas kernels, ffn(): pl.pallas_call(functools.partial(ffn_kernel, tok_dev=tok_dev, width=width...  20.9 us
    ppermute x18, starting transfers between devices, send(): return lax.ppermute(array, 'expert', pairs)  15.7 us
    ppermute x18, waiting for transfers between devices, send(): return lax.ppermute(array, 'expert', pairs)  9.48 us
    ppermute x2, waiting for transfers between devices, on_device(): other = [lax.ppermute(part, 'group', [(0, 1), (1, 0)]) for part in packed]  7.58 us
    pallas_call x1, Pallas kernels, own_side(): pl.pallas_call(own_kernel, out_shape=(kept((hidden_width, hidden_width),...  4.85 us
    pallas_call x1, Pallas kernels, power(): pl.pallas_call(functools.partial(power_kernel, has_other=len(other) > 0),...  3.45 us
    pallas_call x1, Pallas kernels, reduced_first(): pl.pallas_call(reduce_kernel, out_shape=(half, half, *(kept(array.shape,...  3.41 us
    ppermute x2, starting transfers between devices, on_device(): other = [lax.ppermute(part, 'group', [(0, 1), (1, 0)]) for part in packed]  2.17 us
  transfers between devices with their start and end apart: 20, of which 13 were waited for; matrix products, arithmetic and copies ran while one was open for 0% of the time, Pallas kernels for 40%

profile of v7, /device:TPU:0, one launch (start us, length us, event | category | flops | bytes accessed | tf_op | source)
XLA Modules:
  0.0 71.2 jit_solution(7856299629932165759)
XLA Ops:
  0.6 1.2 %shard_map.68 = (bf16[1040,128]{1,0:T(8,128)(2,1)S(1)}, bf16[1040,128]{1,0:T(8,128)(2,1)S(1)}) custom-call(bf16[128,2048]{1,0:T(8,128)(2,1)} %bitcast.19, s32[8,128]{1,0:T(8,128)} %bitcast.20), custom_call_target="tpu_custom_call" | custom-call | bytes 1048576 | tf_op jit(solution)/shard_map/pallas_call | solution.py:79
  1.8 3.1 %collective-permute-start.2 = (bf16[1040,128]{1,0:T(8,128)(2,1)S(1)}, bf16[1040,128]{1,0:T(8,128)(2,1)S(1)}, u32[]{:S(2)}, u32[]{:S(2)}) collective-permute-start(bf16[1040,128]{1,0:T(8,128)(2,1)S(1)} %get-tuple-element.38.refs_1_.refs_2_), channel_id=1, source_target_pairs={{12,4},{14,6},{20,12},{22,14},{28,20},{30,22},{24,28},{26,30},{16,... | collective-permute-start | bytes 798728 | tf_op jit(solution)/shard_map/ppermute | solution.py:567
  4.9 0.0 collective-permute-start
  4.9 0.0 collective-permute-start.4
  4.9 0.0 slice-start
  4.9 0.0 slice-start.1
  4.9 3.4 %shard_map.69 = (bf16[768,256]{1,0:T(8,128)(2,1)S(1)}, bf16[768,256]{1,0:T(8,128)(2,1)S(1)}, bf16[1040,128]{1,0:T(8,128)(2,1)S(1)}, bf16[1040,128]{1,0:T(8,128)(2,1)S(1)}) custom-call(bf16[2048,768]{1,0:T(8,128)(2,1)} %bitcast.17, bf16[2048,256]{1,0:T(8,128)(2,1)} %bitcast.21, bf16[1040,128]{1,0:T(8,128)(2,1)S(1)} %get-tuple-element.37.refs_0_.refs_1_, ...), custom_call_target="tpu_custom_call" | custom-call | flops 99999997952 | bytes 1000 | tf_op jit(solution)/shard_map/pallas_call | solution.py:122
  8.3 2.0 %collective-permute-start.5 = (bf16[1040,128]{1,0:T(8,128)(2,1)S(1)}, bf16[1040,128]{1,0:T(8,128)(2,1)S(1)}, u32[]{:S(2)}, u32[]{:S(2)}) collective-permute-start(bf16[1040,128]{1,0:T(8,128)(2,1)S(1)} %get-tuple-element.43), channel_id=1, source_target_pairs={{4,12},{6,14},{12,20},{14,22},{20,28},{22,30},{28,24},{30,26},{24,... | collective-permute-start | bytes 798728 | tf_op jit(solution)/shard_map/ppermute | solution.py:567
  10.3 0.1 collective-permute-start.3
  10.4 0.8 %collective-permute-done.2.refs_0_ = bf16[1040,128]{1,0:T(8,128)(2,1)S(1)} collective-permute-done((bf16[1040,128]{1,0:T(8,128)(2,1)S(1)}, bf16[1040,128]{1,0:T(8,128)(2,1)S(1)}, u32[]{:S(2)}, u32[]{:S(2)}) %collective-permute-start.2) | collective-permute-done | bytes 266272 | tf_op jit(solution)/shard_map/ppermute | solution.py:567
  11.2 1.8 %collective-permute-start.7 = (bf16[1040,128]{1,0:T(8,128)(2,1)S(1)}, bf16[1040,128]{1,0:T(8,128)(2,1)S(1)}, u32[]{:S(2)}, u32[]{:S(2)}) collective-permute-start(bf16[1040,128]{1,0:T(8,128)(2,1)S(1)} %shard_map.71.refs_4_.refs_2_), channel_id=1, source_target_pairs={{12,4},{14,6},{20,12},{22,14},{28,20},{30,22},{24,28},{26,30},{16,... | collective-permute-start | bytes 798728 | tf_op jit(solution)/shard_map/ppermute | solution.py:567
  13.0 0.7 collective-permute-done.refs_0_
  13.7 0.0 collective-permute-start.1
  13.7 0.0 slice-done
  13.7 0.0 slice-done.1
  13.7 2.2 %shard_map.72 = (f32[768,768]{1,0:T(8,128)S(1)}, f32[8,128]{1,0:T(8,128)S(1)}) custom-call(bf16[2048,1536]{1,0:T(8,128)(2,1)S(1)} %bitcast.12, bf16[1040,128]{1,0:T(8,128)(2,1)S(1)} %get-tuple-element.37.refs_0_.refs_1_, bf16[1040,128]{1,0:T(8,128)(2,1)S(1)} %get-tuple-element.38.refs_1_.refs_2_, bf16[1040,128]{1,0:T(8,128)(2,1)S(1)} %shard_map.70.refs_3_.refs_1_, ...), custom_call_target="tpu_custom_call" | custom-call | flops 1000 | bytes 1000 | tf_op jit(solution)/shard_map/pallas_call | solution.py:332
  15.9 0.0 collective-permute-done.4.refs_0_
  15.9 2.2 %shard_map.73 = (f32[768,768]{1,0:T(8,128)S(1)}, f32[8,128]{1,0:T(8,128)S(1)}) custom-call(bf16[2048,1536]{1,0:T(8,128)(2,1)S(1)} %collective-permute-done.4.refs_0_, bf16[1040,128]{1,0:T(8,128)(2,1)S(1)} %get-tuple-element.37.refs_0_.refs_1_, bf16[1040,128]{1,0:T(8,128)(2,1)S(1)} %get-tuple-element.38.refs_1_.refs_2_, ...), custom_call_target="tpu_custom_call" | custom-call | flops 1000 | bytes 1000 | tf_op jit(solution)/shard_map/pallas_call | solution.py:332
  18.1 1.3 %collective-permute-done.5.refs_0_ = bf16[1040,128]{1,0:T(8,128)(2,1)S(1)} collective-permute-done((bf16[1040,128]{1,0:T(8,128)(2,1)S(1)}, bf16[1040,128]{1,0:T(8,128)(2,1)S(1)}, u32[]{:S(2)}, u32[]{:S(2)}) %collective-permute-start.5) | collective-permute-done | bytes 266272 | tf_op jit(solution)/shard_map/ppermute | solution.py:567
  19.4 0.1 collective-permute-start.9
  19.5 0.0 collective-permute-done.3.refs_0_
  19.5 1.9 %collective-permute-start.8 = (bf16[1040,128]{1,0:T(8,128)(2,1)S(1)}, bf16[1040,128]{1,0:T(8,128)(2,1)S(1)}, u32[]{:S(2)}, u32[]{:S(2)}) collective-permute-start(bf16[1040,128]{1,0:T(8,128)(2,1)S(1)} %shard_map.74.refs_3_.refs_7_), channel_id=1, source_target_pairs={{12,4},{14,6},{20,12},{22,14},{28,20},{30,22},{24,28},{26,30},{16,... | collective-permute-start | bytes 798728 | tf_op jit(solution)/shard_map/ppermute | solution.py:567
  21.4 2.4 %shard_map.76 = (f32[768,768]{1,0:T(8,128)S(1)}, f32[8,128]{1,0:T(8,128)S(1)}) custom-call(bf16[2048,1536]{1,0:T(8,128)(2,1)S(1)} %bitcast.13, bf16[1040,128]{1,0:T(8,128)(2,1)S(1)} %shard_map.70.refs_3_.refs_1_, bf16[1040,128]{1,0:T(8,128)(2,1)S(1)} %shard_map.71.refs_4_.refs_2_, ...), custom_call_target="tpu_custom_call", output_to_operand_aliasing={{0}: (5, {})} | custom-call | flops 1000 | bytes 1000 | tf_op jit(solution)/shard_map/pallas_call | solution.py:332
  23.8 1.5 %collective-permute-done.7.refs_0_ = bf16[1040,128]{1,0:T(8,128)(2,1)S(1)} collective-permute-done((bf16[1040,128]{1,0:T(8,128)(2,1)S(1)}, bf16[1040,128]{1,0:T(8,128)(2,1)S(1)}, u32[]{:S(2)}, u32[]{:S(2)}) %collective-permute-start.7) | collective-permute-done | bytes 266272 | tf_op jit(solution)/shard_map/ppermute | solution.py:567
  25.2 0.1 collective-permute-start.11
  25.3 0.0 collective-permute-done.1.refs_0_
  25.3 1.9 %collective-permute-start.6 = (bf16[1040,128]{1,0:T(8,128)(2,1)S(1)}, bf16[1040,128]{1,0:T(8,128)(2,1)S(1)}, u32[]{:S(2)}, u32[]{:S(2)}) collective-permute-start(bf16[1040,128]{1,0:T(8,128)(2,1)S(1)} %shard_map.77.refs_6_.refs_1_), channel_id=1, source_target_pairs={{4,12},{6,14},{12,20},{14,22},{20,28},{22,30},{28,24},{30,26},{24,... | collective-permute-start | bytes 798728 | tf_op jit(solution)/shard_map/ppermute | solution.py:567
  27.3 2.4 %shard_map.79 = (f32[768,768]{1,0:T(8,128)S(1)}, f32[8,128]{1,0:T(8,128)S(1)}) custom-call(bf16[2048,1536]{1,0:T(8,128)(2,1)S(1)} %collective-permute-done.4.refs_0_, bf16[1040,128]{1,0:T(8,128)(2,1)S(1)} %shard_map.70.refs_3_.refs_1_, bf16[1040,128]{1,0:T(8,128)(2,1)S(1)} %shard_map.71.refs_4_.refs_2_, ...), custom_call_target="tpu_custom_call", output_to_operand_aliasing={{0}: (5, {})} | custom-call | flops 1000 | bytes 1000 | tf_op jit(solution)/shard_map/pallas_call | solution.py:332
  29.6 1.1 %collective-permute-done.9.refs_0_ = bf16[1040,128]{1,0:T(8,128)(2,1)S(1)} collective-permute-done((bf16[1040,128]{1,0:T(8,128)(2,1)S(1)}, bf16[1040,128]{1,0:T(8,128)(2,1)S(1)}, u32[]{:S(2)}, u32[]{:S(2)}) %collective-permute-start.9) | collective-permute-done | bytes 266272 | tf_op jit(solution)/shard_map/ppermute | solution.py:567
  30.8 0.5 collective-permute-start.13
  31.3 0.0 collective-permute-done.8.refs_0_
  31.3 1.5 %collective-permute-start.12 = (bf16[1040,128]{1,0:T(8,128)(2,1)S(1)}, bf16[1040,128]{1,0:T(8,128)(2,1)S(1)}, u32[]{:S(2)}, u32[]{:S(2)}) collective-permute-start(bf16[1040,128]{1,0:T(8,128)(2,1)S(1)} %shard_map.80.refs_3_.refs_7_), channel_id=1, source_target_pairs={{12,4},{14,6},{20,12},{22,14},{28,20},{30,22},{24,28},{26,30},{16,... | collective-permute-start | bytes 798728 | tf_op jit(solution)/shard_map/ppermute | solution.py:567
  32.8 2.4 %shard_map.82 = (f32[768,768]{1,0:T(8,128)S(1)}, f32[8,128]{1,0:T(8,128)S(1)}) custom-call(bf16[2048,1536]{1,0:T(8,128)(2,1)S(1)} %bitcast.14, bf16[1040,128]{1,0:T(8,128)(2,1)S(1)} %shard_map.77.refs_6_.refs_1_, bf16[1040,128]{1,0:T(8,128)(2,1)S(1)} %shard_map.78.refs_7_.refs_2_, ...), custom_call_target="tpu_custom_call", output_to_operand_aliasing={{0}: (5, {})} | custom-call | flops 1000 | bytes 1000 | tf_op jit(solution)/shard_map/pallas_call | solution.py:332
  35.2 1.5 %collective-permute-done.11.refs_0_ = bf16[1040,128]{1,0:T(8,128)(2,1)S(1)} collective-permute-done((bf16[1040,128]{1,0:T(8,128)(2,1)S(1)}, bf16[1040,128]{1,0:T(8,128)(2,1)S(1)}, u32[]{:S(2)}, u32[]{:S(2)}) %collective-permute-start.11) | collective-permute-done | bytes 266272 | tf_op jit(solution)/shard_map/ppermute | solution.py:567
  36.7 0.1 collective-permute-start.14
  36.7 0.0 collective-permute-done.6.refs_0_
  36.7 1.9 %collective-permute-start.10 = (bf16[1040,128]{1,0:T(8,128)(2,1)S(1)}, bf16[1040,128]{1,0:T(8,128)(2,1)S(1)}, u32[]{:S(2)}, u32[]{:S(2)}) collective-permute-start(bf16[1040,128]{1,0:T(8,128)(2,1)S(1)} %shard_map.83.refs_6_.refs_1_), channel_id=1, source_target_pairs={{4,12},{6,14},{12,20},{14,22},{20,28},{22,30},{28,24},{30,26},{24,... | collective-permute-start | bytes 798728 | tf_op jit(solution)/shard_map/ppermute | solution.py:567
  38.7 2.4 %shard_map.85 = (f32[768,768]{1,0:T(8,128)S(1)}, f32[8,128]{1,0:T(8,128)S(1)}) custom-call(bf16[2048,1536]{1,0:T(8,128)(2,1)S(1)} %collective-permute-done.4.refs_0_, bf16[1040,128]{1,0:T(8,128)(2,1)S(1)} %shard_map.77.refs_6_.refs_1_, bf16[1040,128]{1,0:T(8,128)(2,1)S(1)} %shard_map.78.refs_7_.refs_2_, ...), custom_call_target="tpu_custom_call", output_to_operand_aliasing={{0}: (5, {})} | custom-call | flops 1000 | bytes 1000 | tf_op jit(solution)/shard_map/pallas_call | solution.py:332
  41.0 1.1 %collective-permute-done.13.refs_0_ = bf16[1040,128]{1,0:T(8,128)(2,1)S(1)} collective-permute-done((bf16[1040,128]{1,0:T(8,128)(2,1)S(1)}, bf16[1040,128]{1,0:T(8,128)(2,1)S(1)}, u32[]{:S(2)}, u32[]{:S(2)}) %collective-permute-start.13) | collective-permute-done | bytes 266272 | tf_op jit(solution)/shard_map/ppermute | solution.py:567
  42.2 0.2 collective-permute-done.12.refs_0_
  42.4 2.4 %shard_map.88 = (f32[768,768]{1,0:T(8,128)S(1)}, bf16[2688,128]{1,0:T(8,128)(2,1)S(1)}) custom-call(bf16[2048,1536]{1,0:T(8,128)(2,1)S(1)} %collective-permute-done.4.refs_0_, bf16[1040,128]{1,0:T(8,128)(2,1)S(1)} %shard_map.83.refs_6_.refs_1_, bf16[1040,128]{1,0:T(8,128)(2,1)S(1)} %shard_map.84.refs_7_.refs_2_, ...), custom_call_target="tpu_custom_call", output_to_operand_aliasing={{0}: (5, {})} | custom-call | flops 1000 | bytes 1000 | tf_op jit(solution)/shard_map/pallas_call | solution.py:332
  44.8 0.1 collective-permute-start.17
  44.9 2.4 %shard_map.89 = (f32[768,768]{1,0:T(8,128)S(1)}, f32[8,128]{1,0:T(8,128)S(1)}) custom-call(bf16[2048,1536]{1,0:T(8,128)(2,1)S(1)} %bitcast.15, bf16[1040,128]{1,0:T(8,128)(2,1)S(1)} %shard_map.83.refs_6_.refs_1_, bf16[1040,128]{1,0:T(8,128)(2,1)S(1)} %shard_map.84.refs_7_.refs_2_, ...), custom_call_target="tpu_custom_call", output_to_operand_aliasing={{0}: (5, {})} | custom-call | flops 1000 | bytes 1000 | tf_op jit(solution)/shard_map/pallas_call | solution.py:332
  47.2 0.2 collective-permute-done.14.refs_0_
  47.4 0.4 collective-permute-start.16
  47.8 0.0 collective-permute-done.10.refs_0_
  47.8 0.1 collective-permute-start.15
  47.9 0.0 collective-permute-done.17.tiles_ref
  47.9 0.3 shard_map.93.refs_5_
  48.2 0.8 %collective-permute-done.16.refs_4_ = bf16[1040,128]{1,0:T(8,128)(2,1)S(1)} collective-permute-done((bf16[1040,128]{1,0:T(8,128)(2,1)S(1)}, bf16[1040,128]{1,0:T(8,128)(2,1)S(1)}, u32[]{:S(2)}, u32[]{:S(2)}) %collective-permute-start.16) | collective-permute-done | bytes 266272 | tf_op jit(solution)/shard_map/ppermute | solution.py:567
  49.0 0.4 collective-permute-done.15.refs_3_
  49.3 2.4 %shard_map.94 = (f32[768,768]{1,0:T(8,128)S(1)}, bf16[1296,128]{1,0:T(8,128)(2,1)S(1)}, bf16[768,256]{1,0:T(8,128)(2,1)S(1)}) custom-call(bf16[2048,1536]{1,0:T(8,128)(2,1)S(1)} %bitcast.16, bf16[1040,128]{1,0:T(8,128)(2,1)S(1)} %shard_map.90.refs_1_, bf16[1040,128]{1,0:T(8,128)(2,1)S(1)} %shard_map.91.refs_2_, ...), custom_call_target="tpu_custom_call", output_to_operand_aliasing={{0}: (5, {})} | custom-call | flops 1000 | bytes 1000 | tf_op jit(solution)/shard_map/pallas_call | solution.py:332
  51.7 1.6 %collective-permute-start.18 = (bf16[1296,128]{1,0:T(8,128)(2,1)S(1)}, bf16[1296,128]{1,0:T(8,128)(2,1)S(1)}, u32[]{:S(2)}, u32[]{:S(2)}) collective-permute-start(bf16[1296,128]{1,0:T(8,128)(2,1)S(1)} %get-tuple-element.63), channel_id=1, source_target_pairs={{0,1},{1,0},{2,3},{3,2},{4,5},{5,4},{6,7},{7,6},{8,9},{9,8},{10,11... | collective-permute-start | bytes 995336 | tf_op jit(solution)/shard_map/ppermute | solution.py:631
  53.3 0.5 shard_map.95
  53.8 0.6 collective-permute-start.19
  54.4 4.8 %shard_map.96 = (f32[768,768]{1,0:T(8,128)S(1)}, f32[768,256]{1,0:T(8,128)S(1)}, bf16[2048,768]{1,0:T(8,128)(2,1)S(1)}, bf16[768,768]{1,0:T(8,128)(2,1)S(1)}) custom-call(f32[768,768]{1,0:T(8,128)S(1)} %get-tuple-element.59.own_ref, bf16[768,256]{1,0:T(8,128)(2,1)S(1)} %get-tuple-element.39.refs_1_.refs_5_.high_ref.first_ref.refs_4_, ...), custom_call_target="tpu_custom_call" | custom-call | flops 1000 | bytes 1000 | tf_op jit(solution)/shard_map/pallas_call | solution.py:402
  59.2 3.2 %collective-permute-done.18.front_ref = bf16[1296,128]{1,0:T(8,128)(2,1)S(1)} collective-permute-done((bf16[1296,128]{1,0:T(8,128)(2,1)S(1)}, bf16[1296,128]{1,0:T(8,128)(2,1)S(1)}, u32[]{:S(2)}, u32[]{:S(2)}) %collective-permute-start.18) | collective-permute-done | bytes 331808 | tf_op jit(solution)/shard_map/ppermute | solution.py:631
  62.4 0.7 %shard_map.97 = (f32[768,768]{1,0:T(8,128)S(1)}, f32[768,256]{1,0:T(8,128)S(1)}, bf16[768,768]{1,0:T(8,128)(2,1)S(1)}) custom-call(f32[768,768]{1,0:T(8,128)S(1)} %get-tuple-element.61.own_in, f32[768,256]{1,0:T(8,128)S(1)} %get-tuple-element.62.panel_in, ...), custom_call_target="tpu_custom_call", output_to_operand_aliasing={{0}: (0, {}), {1}: (1, {})} | custom-call | flops 1000 | bytes 1000 | tf_op jit(solution)/shard_map/pallas_call | solution.py:436
  63.1 4.4 %collective-permute-done.19.refs_3_ = bf16[1040,128]{1,0:T(8,128)(2,1)S(1)} collective-permute-done((bf16[1040,128]{1,0:T(8,128)(2,1)S(1)}, bf16[1040,128]{1,0:T(8,128)(2,1)S(1)}, u32[]{:S(2)}, u32[]{:S(2)}) %collective-permute-start.19) | collective-permute-done | bytes 266272 | tf_op jit(solution)/shard_map/ppermute | solution.py:631
  67.6 3.4 %shard_map.98 = (f32[384,768]{1,0:T(8,128)}, f32[1024,256]{1,0:T(8,128)}) custom-call(f32[768,768]{1,0:T(8,128)S(1)} %get-tuple-element.64.refs_0_, f32[768,256]{1,0:T(8,128)S(1)} %get-tuple-element.65.refs_1_, bf16[768,768]{1,0:T(8,128)(2,1)S(1)} %get-tuple-element.66.refs_2_, bf16[1040,128]{1,0:T(8,128)(2,1)S(1)} %collective-permute-done.19.refs_3_, ...), custom_call_target="tpu_custom_call" | custom-call | flops 4227858432 | bytes 6291456 | tf_op jit(solution)/shard_map/pallas_call | solution.py:520
  (16 shorter events, 0.0 us)
Async XLA Ops:
  1.8 9.4 %collective-permute-start.2 = (bf16[1040,128]{1,0:T(8,128)(2,1)S(1)}, bf16[1040,128]{1,0:T(8,128)(2,1)S(1)}, u32[]{:S(2)}, u32[]{:S(2)}) collective-permute-start(bf16[1040,128]{1,0:T(8,128)(2,1)S(1)} %get-tuple-element.38.refs_1_.refs_2_), channel_id=1, source_target_pairs={{12,4},{14,6},{20,12},{22,14},{28,20},{30,22},{24,28},{26,30},{16,... | collective-permute-start | bytes 798728 | tf_op jit(solution)/shard_map/ppermute | solution.py:567
  4.9 8.8 %collective-permute-start = (bf16[1040,128]{1,0:T(8,128)(2,1)S(1)}, bf16[1040,128]{1,0:T(8,128)(2,1)S(1)}, u32[]{:S(2)}, u32[]{:S(2)}) collective-permute-start(bf16[1040,128]{1,0:T(8,128)(2,1)S(1)} %get-tuple-element.37.refs_0_.refs_1_), channel_id=1, source_target_pairs={{4,12},{6,14},{12,20},{14,22},{20,28},{22,30},{28,24},{30,26},{24,... | collective-permute-start | bytes 798728 | tf_op jit(solution)/shard_map/ppermute | solution.py:567
  4.9 11.0 %collective-permute-start.4 = (bf16[2048,1536]{1,0:T(8,128)(2,1)}, bf16[2048,1536]{1,0:T(8,128)(2,1)S(1)}, u32[]{:S(2)}, u32[]{:S(2)}) collective-permute-start(bf16[2048,1536]{1,0:T(8,128)(2,1)} %bitcast.9), channel_id=1, source_target_pairs={{0,2},{2,0},{4,6},{6,4},{8,10},{10,8},{12,14},{14,12},{16,18},{18,... | collective-permute-start | bytes 18874376 | tf_op jit(solution)/shard_map/ppermute | solution.py:567
  4.9 8.8 %slice-start = ((s8[6291456]{0:T(1024)(128)(4,1)}), s8[4194304]{0:T(1024)(128)(4,1)S(1)}, s32[]{:S(2)}) async-start(s8[6291456]{0:T(1024)(128)(4,1)} %bitcast.10), calls=%async_computation | async-start | bytes 8388608
  4.9 8.8 %slice-start.1 = ((s8[6291456]{0:T(1024)(128)(4,1)}), s8[2097152]{0:T(1024)(128)(4,1)S(1)}, s32[]{:S(2)}) async-start(s8[6291456]{0:T(1024)(128)(4,1)} %bitcast.10), calls=%async_computation.1 | async-start | bytes 4194304
  8.3 11.1 %collective-permute-start.5 = (bf16[1040,128]{1,0:T(8,128)(2,1)S(1)}, bf16[1040,128]{1,0:T(8,128)(2,1)S(1)}, u32[]{:S(2)}, u32[]{:S(2)}) collective-permute-start(bf16[1040,128]{1,0:T(8,128)(2,1)S(1)} %get-tuple-element.43), channel_id=1, source_target_pairs={{4,12},{6,14},{12,20},{14,22},{20,28},{22,30},{28,24},{30,26},{24,... | collective-permute-start | bytes 798728 | tf_op jit(solution)/shard_map/ppermute | solution.py:567
  10.3 9.2 %collective-permute-start.3 = (bf16[1040,128]{1,0:T(8,128)(2,1)S(1)}, bf16[1040,128]{1,0:T(8,128)(2,1)S(1)}, u32[]{:S(2)}, u32[]{:S(2)}) collective-permute-start(bf16[1040,128]{1,0:T(8,128)(2,1)S(1)} %get-tuple-element.40), channel_id=1, source_target_pairs={{12,4},{14,6},{20,12},{22,14},{28,20},{30,22},{24,28},{26,30},{16,... | collective-permute-start | bytes 798728 | tf_op jit(solution)/shard_map/ppermute | solution.py:567
  11.2 14.0 %collective-permute-start.7 = (bf16[1040,128]{1,0:T(8,128)(2,1)S(1)}, bf16[1040,128]{1,0:T(8,128)(2,1)S(1)}, u32[]{:S(2)}, u32[]{:S(2)}) collective-permute-start(bf16[1040,128]{1,0:T(8,128)(2,1)S(1)} %shard_map.71.refs_4_.refs_2_), channel_id=1, source_target_pairs={{12,4},{14,6},{20,12},{22,14},{28,20},{30,22},{24,28},{26,30},{16,... | collective-permute-start | bytes 798728 | tf_op jit(solution)/shard_map/ppermute | solution.py:567
  13.7 11.7 %collective-permute-start.1 = (bf16[1040,128]{1,0:T(8,128)(2,1)S(1)}, bf16[1040,128]{1,0:T(8,128)(2,1)S(1)}, u32[]{:S(2)}, u32[]{:S(2)}) collective-permute-start(bf16[1040,128]{1,0:T(8,128)(2,1)S(1)} %shard_map.70.refs_3_.refs_1_), channel_id=1, source_target_pairs={{4,12},{6,14},{12,20},{14,22},{20,28},{22,30},{28,24},{30,26},{24,... | collective-permute-start | bytes 798728 | tf_op jit(solution)/shard_map/ppermute | solution.py:567
  19.4 11.4 %collective-permute-start.9 = (bf16[1040,128]{1,0:T(8,128)(2,1)S(1)}, bf16[1040,128]{1,0:T(8,128)(2,1)S(1)}, u32[]{:S(2)}, u32[]{:S(2)}) collective-permute-start(bf16[1040,128]{1,0:T(8,128)(2,1)S(1)} %shard_map.75.refs_4_.refs_6_), channel_id=1, source_target_pairs={{4,12},{6,14},{12,20},{14,22},{20,28},{22,30},{28,24},{30,26},{24,... | collective-permute-start | bytes 798728 | tf_op jit(solution)/shard_map/ppermute | solution.py:567
  19.5 11.7 %collective-permute-start.8 = (bf16[1040,128]{1,0:T(8,128)(2,1)S(1)}, bf16[1040,128]{1,0:T(8,128)(2,1)S(1)}, u32[]{:S(2)}, u32[]{:S(2)}) collective-permute-start(bf16[1040,128]{1,0:T(8,128)(2,1)S(1)} %shard_map.74.refs_3_.refs_7_), channel_id=1, source_target_pairs={{12,4},{14,6},{20,12},{22,14},{28,20},{30,22},{24,28},{26,30},{16,... | collective-permute-start | bytes 798728 | tf_op jit(solution)/shard_map/ppermute | solution.py:567
  25.2 11.4 %collective-permute-start.11 = (bf16[1040,128]{1,0:T(8,128)(2,1)S(1)}, bf16[1040,128]{1,0:T(8,128)(2,1)S(1)}, u32[]{:S(2)}, u32[]{:S(2)}) collective-permute-start(bf16[1040,128]{1,0:T(8,128)(2,1)S(1)} %shard_map.78.refs_7_.refs_2_), channel_id=1, source_target_pairs={{12,4},{14,6},{20,12},{22,14},{28,20},{30,22},{24,28},{26,30},{16,... | collective-permute-start | bytes 798728 | tf_op jit(solution)/shard_map/ppermute | solution.py:567
  25.3 11.4 %collective-permute-start.6 = (bf16[1040,128]{1,0:T(8,128)(2,1)S(1)}, bf16[1040,128]{1,0:T(8,128)(2,1)S(1)}, u32[]{:S(2)}, u32[]{:S(2)}) collective-permute-start(bf16[1040,128]{1,0:T(8,128)(2,1)S(1)} %shard_map.77.refs_6_.refs_1_), channel_id=1, source_target_pairs={{4,12},{6,14},{12,20},{14,22},{20,28},{22,30},{28,24},{30,26},{24,... | collective-permute-start | bytes 798728 | tf_op jit(solution)/shard_map/ppermute | solution.py:567
  30.8 11.4 %collective-permute-start.13 = (bf16[1040,128]{1,0:T(8,128)(2,1)S(1)}, bf16[1040,128]{1,0:T(8,128)(2,1)S(1)}, u32[]{:S(2)}, u32[]{:S(2)}) collective-permute-start(bf16[1040,128]{1,0:T(8,128)(2,1)S(1)} %shard_map.81.refs_4_.refs_6_), channel_id=1, source_target_pairs={{4,12},{6,14},{12,20},{14,22},{20,28},{22,30},{28,24},{30,26},{24,... | collective-permute-start | bytes 798728 | tf_op jit(solution)/shard_map/ppermute | solution.py:567
  31.3 11.1 %collective-permute-start.12 = (bf16[1040,128]{1,0:T(8,128)(2,1)S(1)}, bf16[1040,128]{1,0:T(8,128)(2,1)S(1)}, u32[]{:S(2)}, u32[]{:S(2)}) collective-permute-start(bf16[1040,128]{1,0:T(8,128)(2,1)S(1)} %shard_map.80.refs_3_.refs_7_), channel_id=1, source_target_pairs={{12,4},{14,6},{20,12},{22,14},{28,20},{30,22},{24,28},{26,30},{16,... | collective-permute-start | bytes 798728 | tf_op jit(solution)/shard_map/ppermute | solution.py:567
  36.7 10.7 %collective-permute-start.14 = (bf16[1040,128]{1,0:T(8,128)(2,1)S(1)}, bf16[1040,128]{1,0:T(8,128)(2,1)S(1)}, u32[]{:S(2)}, u32[]{:S(2)}) collective-permute-start(bf16[1040,128]{1,0:T(8,128)(2,1)S(1)} %shard_map.84.refs_7_.refs_2_), channel_id=1, source_target_pairs={{12,4},{14,6},{20,12},{22,14},{28,20},{30,22},{24,28},{26,30},{16,... | collective-permute-start | bytes 798728 | tf_op jit(solution)/shard_map/ppermute | solution.py:567
  36.7 11.1 %collective-permute-start.10 = (bf16[1040,128]{1,0:T(8,128)(2,1)S(1)}, bf16[1040,128]{1,0:T(8,128)(2,1)S(1)}, u32[]{:S(2)}, u32[]{:S(2)}) collective-permute-start(bf16[1040,128]{1,0:T(8,128)(2,1)S(1)} %shard_map.83.refs_6_.refs_1_), channel_id=1, source_target_pairs={{4,12},{6,14},{12,20},{14,22},{20,28},{22,30},{28,24},{30,26},{24,... | collective-permute-start | bytes 798728 | tf_op jit(solution)/shard_map/ppermute | solution.py:567
  44.8 3.1 %collective-permute-start.17 = (bf16[2688,128]{1,0:T(8,128)(2,1)S(1)}, bf16[2688,128]{1,0:T(8,128)(2,1)S(1)}, u32[]{:S(2)}, u32[]{:S(2)}) collective-permute-start(bf16[2688,128]{1,0:T(8,128)(2,1)S(1)} %get-tuple-element.54.refs_8_), channel_id=1, source_target_pairs={{0,2},{2,0},{4,6},{6,4},{8,10},{10,8},{12,14},{14,12},{16,18},{18,... | collective-permute-start | bytes 2064392 | tf_op jit(solution)/shard_map/ppermute | solution.py:567
  47.4 1.6 %collective-permute-start.16 = (bf16[1040,128]{1,0:T(8,128)(2,1)S(1)}, bf16[1040,128]{1,0:T(8,128)(2,1)S(1)}, u32[]{:S(2)}, u32[]{:S(2)}) collective-permute-start(bf16[1040,128]{1,0:T(8,128)(2,1)S(1)} %shard_map.91.refs_2_), channel_id=1, source_target_pairs={{0,2},{2,0},{4,6},{6,4},{8,10},{10,8},{12,14},{14,12},{16,18},{18,... | collective-permute-start | bytes 798728 | tf_op jit(solution)/shard_map/ppermute | solution.py:567
  47.8 1.5 %collective-permute-start.15 = (bf16[1040,128]{1,0:T(8,128)(2,1)S(1)}, bf16[1040,128]{1,0:T(8,128)(2,1)S(1)}, u32[]{:S(2)}, u32[]{:S(2)}) collective-permute-start(bf16[1040,128]{1,0:T(8,128)(2,1)S(1)} %shard_map.90.refs_1_), channel_id=1, source_target_pairs={{0,2},{2,0},{4,6},{6,4},{8,10},{10,8},{12,14},{14,12},{16,18},{18,... | collective-permute-start | bytes 798728 | tf_op jit(solution)/shard_map/ppermute | solution.py:567
  51.7 10.7 %collective-permute-start.18 = (bf16[1296,128]{1,0:T(8,128)(2,1)S(1)}, bf16[1296,128]{1,0:T(8,128)(2,1)S(1)}, u32[]{:S(2)}, u32[]{:S(2)}) collective-permute-start(bf16[1296,128]{1,0:T(8,128)(2,1)S(1)} %get-tuple-element.63), channel_id=1, source_target_pairs={{0,1},{1,0},{2,3},{3,2},{4,5},{5,4},{6,7},{7,6},{8,9},{9,8},{10,11... | collective-permute-start | bytes 995336 | tf_op jit(solution)/shard_map/ppermute | solution.py:631
  53.8 13.8 %collective-permute-start.19 = (bf16[1040,128]{1,0:T(8,128)(2,1)S(1)}, bf16[1040,128]{1,0:T(8,128)(2,1)S(1)}, u32[]{:S(2)}, u32[]{:S(2)}) collective-permute-start(bf16[1040,128]{1,0:T(8,128)(2,1)S(1)} %get-tuple-element.67), channel_id=1, source_target_pairs={{0,1},{1,0},{2,3},{3,2},{4,5},{5,4},{6,7},{7,6},{8,9},{9,8},{10,11... | collective-permute-start | bytes 798728 | tf_op jit(solution)/shard_map/ppermute | solution.py:631

commit v8 on v7

--- a/solution.py
+++ b/solution.py
@@ -498,7 +498,8 @@
     def power_step(first, rows, carry):
         mine = pl.ds(pl.multiple_of(group * own_rows + first, rows), rows)
         power_ref[pl.ds(first, rows), :] = product(w_ref[mine, :], small_ref[...], NN)
-        power_copy(first, rows).start()
+        for at in range(0, rows, LANES):
+            power_copy(first + at, LANES).start()
         return carry
 
     def power_wait(first, rows, carry):
@@ -507,7 +508,7 @@
 
     blocks_of(own_rows, 4 * LANES, power_step)
     gram_copy.wait()
-    blocks_of(own_rows, 4 * LANES, power_wait)
+    blocks_of(own_rows, LANES, power_wait)
 
 
 def power(own, other, panel, reduced, w_down, square, group_count):
@@ -531,7 +532,7 @@
             pltpu.VMEM((hidden_width, hidden_width), BF16),
             pltpu.VMEM((hidden_width, rank), BF16),
             pltpu.VMEM((own_rows, rank), F32),
-            pltpu.SemaphoreType.DMA((1 + max(1, own_rows // (4 * LANES)),)),
+            pltpu.SemaphoreType.DMA((1 + own_rows // LANES,)),
         ],
         compiler_params=params(12),
         cost_estimate=pl.CostEstimate(

time: 71.3 us -> 71.4 us (level)
  no operation moved by 1% of the time
where the time goes in v8:
time: 71.4 us; the launch traced here: 71.2 us
  Pallas kernels  35.3 us (49%)
  starting transfers between devices  17.8 us (25%)
  waiting for transfers between devices  17.1 us (24%)
  between operations  0.96 us (1%)
    pallas_call x9, Pallas kernels, ffn(): pl.pallas_call(functools.partial(ffn_kernel, tok_dev=tok_dev, width=width...  20.9 us
    ppermute x18, starting transfers between devices, send(): return lax.ppermute(array, 'expert', pairs)  15.7 us
    ppermute x18, waiting for transfers between devices, send(): return lax.ppermute(array, 'expert', pairs)  9.48 us
    ppermute x2, waiting for transfers between devices, on_device(): other = [lax.ppermute(part, 'group', [(0, 1), (1, 0)]) for part in packed]  7.58 us
    pallas_call x1, Pallas kernels, own_side(): pl.pallas_call(own_kernel, out_shape=(kept((hidden_width, hidden_width),...  4.85 us
    pallas_call x1, Pallas kernels, power(): pl.pallas_call(functools.partial(power_kernel, has_other=len(other) > 0),...  3.49 us
    pallas_call x1, Pallas kernels, reduced_first(): pl.pallas_call(reduce_kernel, out_shape=(half, half, *(kept(array.shape,...  3.41 us
    ppermute x2, starting transfers between devices, on_device(): other = [lax.ppermute(part, 'group', [(0, 1), (1, 0)]) for part in packed]  2.17 us
  transfers between devices with their start and end apart: 20, of which 13 were waited for; matrix products, arithmetic and copies ran while one was open for 0% of the time, Pallas kernels for 40%

profile of v8, /device:TPU:0, one launch (start us, length us, event | category | flops | bytes accessed | tf_op | source)
XLA Modules:
  0.0 71.2 jit_solution(18393702920152668566)
XLA Ops:
  0.6 1.2 %shard_map.68 = (bf16[1040,128]{1,0:T(8,128)(2,1)S(1)}, bf16[1040,128]{1,0:T(8,128)(2,1)S(1)}) custom-call(bf16[128,2048]{1,0:T(8,128)(2,1)} %bitcast.19, s32[8,128]{1,0:T(8,128)} %bitcast.20), custom_call_target="tpu_custom_call" | custom-call | bytes 1048576 | tf_op jit(solution)/shard_map/pallas_call | solution.py:79
  1.8 3.1 %collective-permute-start.2 = (bf16[1040,128]{1,0:T(8,128)(2,1)S(1)}, bf16[1040,128]{1,0:T(8,128)(2,1)S(1)}, u32[]{:S(2)}, u32[]{:S(2)}) collective-permute-start(bf16[1040,128]{1,0:T(8,128)(2,1)S(1)} %get-tuple-element.38.refs_1_.refs_2_), channel_id=1, source_target_pairs={{12,4},{14,6},{20,12},{22,14},{28,20},{30,22},{24,28},{26,30},{16,... | collective-permute-start | bytes 798728 | tf_op jit(solution)/shard_map/ppermute | solution.py:568
  4.9 0.0 collective-permute-start
  4.9 0.0 collective-permute-start.4
  4.9 0.0 slice-start
  4.9 0.0 slice-start.1
  4.9 3.4 %shard_map.69 = (bf16[768,256]{1,0:T(8,128)(2,1)S(1)}, bf16[768,256]{1,0:T(8,128)(2,1)S(1)}, bf16[1040,128]{1,0:T(8,128)(2,1)S(1)}, bf16[1040,128]{1,0:T(8,128)(2,1)S(1)}) custom-call(bf16[2048,768]{1,0:T(8,128)(2,1)} %bitcast.17, bf16[2048,256]{1,0:T(8,128)(2,1)} %bitcast.21, bf16[1040,128]{1,0:T(8,128)(2,1)S(1)} %get-tuple-element.37.refs_0_.refs_1_, ...), custom_call_target="tpu_custom_call" | custom-call | flops 99999997952 | bytes 1000 | tf_op jit(solution)/shard_map/pallas_call | solution.py:122
  8.3 2.0 %collective-permute-start.5 = (bf16[1040,128]{1,0:T(8,128)(2,1)S(1)}, bf16[1040,128]{1,0:T(8,128)(2,1)S(1)}, u32[]{:S(2)}, u32[]{:S(2)}) collective-permute-start(bf16[1040,128]{1,0:T(8,128)(2,1)S(1)} %get-tuple-element.43), channel_id=1, source_target_pairs={{4,12},{6,14},{12,20},{14,22},{20,28},{22,30},{28,24},{30,26},{24,... | collective-permute-start | bytes 798728 | tf_op jit(solution)/shard_map/ppermute | solution.py:568
  10.3 0.1 collective-permute-start.3
  10.4 0.8 %collective-permute-done.2.refs_0_ = bf16[1040,128]{1,0:T(8,128)(2,1)S(1)} collective-permute-done((bf16[1040,128]{1,0:T(8,128)(2,1)S(1)}, bf16[1040,128]{1,0:T(8,128)(2,1)S(1)}, u32[]{:S(2)}, u32[]{:S(2)}) %collective-permute-start.2) | collective-permute-done | bytes 266272 | tf_op jit(solution)/shard_map/ppermute | solution.py:568
  11.2 1.8 %collective-permute-start.7 = (bf16[1040,128]{1,0:T(8,128)(2,1)S(1)}, bf16[1040,128]{1,0:T(8,128)(2,1)S(1)}, u32[]{:S(2)}, u32[]{:S(2)}) collective-permute-start(bf16[1040,128]{1,0:T(8,128)(2,1)S(1)} %shard_map.71.refs_4_.refs_2_), channel_id=1, source_target_pairs={{12,4},{14,6},{20,12},{22,14},{28,20},{30,22},{24,28},{26,30},{16,... | collective-permute-start | bytes 798728 | tf_op jit(solution)/shard_map/ppermute | solution.py:568
  13.0 0.7 collective-permute-done.refs_0_
  13.7 0.0 collective-permute-start.1
  13.7 0.0 slice-done
  13.7 0.0 slice-done.1
  13.7 2.2 %shard_map.72 = (f32[768,768]{1,0:T(8,128)S(1)}, f32[8,128]{1,0:T(8,128)S(1)}) custom-call(bf16[2048,1536]{1,0:T(8,128)(2,1)S(1)} %bitcast.12, bf16[1040,128]{1,0:T(8,128)(2,1)S(1)} %get-tuple-element.37.refs_0_.refs_1_, bf16[1040,128]{1,0:T(8,128)(2,1)S(1)} %get-tuple-element.38.refs_1_.refs_2_, bf16[1040,128]{1,0:T(8,128)(2,1)S(1)} %shard_map.70.refs_3_.refs_1_, ...), custom_call_target="tpu_custom_call" | custom-call | flops 1000 | bytes 1000 | tf_op jit(solution)/shard_map/pallas_call | solution.py:332
  15.9 0.0 collective-permute-done.4.refs_0_
  15.9 2.2 %shard_map.73 = (f32[768,768]{1,0:T(8,128)S(1)}, f32[8,128]{1,0:T(8,128)S(1)}) custom-call(bf16[2048,1536]{1,0:T(8,128)(2,1)S(1)} %collective-permute-done.4.refs_0_, bf16[1040,128]{1,0:T(8,128)(2,1)S(1)} %get-tuple-element.37.refs_0_.refs_1_, bf16[1040,128]{1,0:T(8,128)(2,1)S(1)} %get-tuple-element.38.refs_1_.refs_2_, ...), custom_call_target="tpu_custom_call" | custom-call | flops 1000 | bytes 1000 | tf_op jit(solution)/shard_map/pallas_call | solution.py:332
  18.1 1.3 %collective-permute-done.5.refs_0_ = bf16[1040,128]{1,0:T(8,128)(2,1)S(1)} collective-permute-done((bf16[1040,128]{1,0:T(8,128)(2,1)S(1)}, bf16[1040,128]{1,0:T(8,128)(2,1)S(1)}, u32[]{:S(2)}, u32[]{:S(2)}) %collective-permute-start.5) | collective-permute-done | bytes 266272 | tf_op jit(solution)/shard_map/ppermute | solution.py:568
  19.4 0.1 collective-permute-start.9
  19.5 0.0 collective-permute-done.3.refs_0_
  19.5 1.9 %collective-permute-start.8 = (bf16[1040,128]{1,0:T(8,128)(2,1)S(1)}, bf16[1040,128]{1,0:T(8,128)(2,1)S(1)}, u32[]{:S(2)}, u32[]{:S(2)}) collective-permute-start(bf16[1040,128]{1,0:T(8,128)(2,1)S(1)} %shard_map.74.refs_3_.refs_7_), channel_id=1, source_target_pairs={{12,4},{14,6},{20,12},{22,14},{28,20},{30,22},{24,28},{26,30},{16,... | collective-permute-start | bytes 798728 | tf_op jit(solution)/shard_map/ppermute | solution.py:568
  21.4 2.4 %shard_map.76 = (f32[768,768]{1,0:T(8,128)S(1)}, f32[8,128]{1,0:T(8,128)S(1)}) custom-call(bf16[2048,1536]{1,0:T(8,128)(2,1)S(1)} %bitcast.13, bf16[1040,128]{1,0:T(8,128)(2,1)S(1)} %shard_map.70.refs_3_.refs_1_, bf16[1040,128]{1,0:T(8,128)(2,1)S(1)} %shard_map.71.refs_4_.refs_2_, ...), custom_call_target="tpu_custom_call", output_to_operand_aliasing={{0}: (5, {})} | custom-call | flops 1000 | bytes 1000 | tf_op jit(solution)/shard_map/pallas_call | solution.py:332
  23.8 1.5 %collective-permute-done.7.refs_0_ = bf16[1040,128]{1,0:T(8,128)(2,1)S(1)} collective-permute-done((bf16[1040,128]{1,0:T(8,128)(2,1)S(1)}, bf16[1040,128]{1,0:T(8,128)(2,1)S(1)}, u32[]{:S(2)}, u32[]{:S(2)}) %collective-permute-start.7) | collective-permute-done | bytes 266272 | tf_op jit(solution)/shard_map/ppermute | solution.py:568
  25.2 0.1 collective-permute-start.11
  25.3 0.0 collective-permute-done.1.refs_0_
  25.3 1.9 %collective-permute-start.6 = (bf16[1040,128]{1,0:T(8,128)(2,1)S(1)}, bf16[1040,128]{1,0:T(8,128)(2,1)S(1)}, u32[]{:S(2)}, u32[]{:S(2)}) collective-permute-start(bf16[1040,128]{1,0:T(8,128)(2,1)S(1)} %shard_map.77.refs_6_.refs_1_), channel_id=1, source_target_pairs={{4,12},{6,14},{12,20},{14,22},{20,28},{22,30},{28,24},{30,26},{24,... | collective-permute-start | bytes 798728 | tf_op jit(solution)/shard_map/ppermute | solution.py:568
  27.3 2.4 %shard_map.79 = (f32[768,768]{1,0:T(8,128)S(1)}, f32[8,128]{1,0:T(8,128)S(1)}) custom-call(bf16[2048,1536]{1,0:T(8,128)(2,1)S(1)} %collective-permute-done.4.refs_0_, bf16[1040,128]{1,0:T(8,128)(2,1)S(1)} %shard_map.70.refs_3_.refs_1_, bf16[1040,128]{1,0:T(8,128)(2,1)S(1)} %shard_map.71.refs_4_.refs_2_, ...), custom_call_target="tpu_custom_call", output_to_operand_aliasing={{0}: (5, {})} | custom-call | flops 1000 | bytes 1000 | tf_op jit(solution)/shard_map/pallas_call | solution.py:332
  29.6 1.1 %collective-permute-done.9.refs_0_ = bf16[1040,128]{1,0:T(8,128)(2,1)S(1)} collective-permute-done((bf16[1040,128]{1,0:T(8,128)(2,1)S(1)}, bf16[1040,128]{1,0:T(8,128)(2,1)S(1)}, u32[]{:S(2)}, u32[]{:S(2)}) %collective-permute-start.9) | collective-permute-done | bytes 266272 | tf_op jit(solution)/shard_map/ppermute | solution.py:568
  30.8 0.5 collective-permute-start.13
  31.3 0.0 collective-permute-done.8.refs_0_
  31.3 1.5 %collective-permute-start.12 = (bf16[1040,128]{1,0:T(8,128)(2,1)S(1)}, bf16[1040,128]{1,0:T(8,128)(2,1)S(1)}, u32[]{:S(2)}, u32[]{:S(2)}) collective-permute-start(bf16[1040,128]{1,0:T(8,128)(2,1)S(1)} %shard_map.80.refs_3_.refs_7_), channel_id=1, source_target_pairs={{12,4},{14,6},{20,12},{22,14},{28,20},{30,22},{24,28},{26,30},{16,... | collective-permute-start | bytes 798728 | tf_op jit(solution)/shard_map/ppermute | solution.py:568
  32.8 2.4 %shard_map.82 = (f32[768,768]{1,0:T(8,128)S(1)}, f32[8,128]{1,0:T(8,128)S(1)}) custom-call(bf16[2048,1536]{1,0:T(8,128)(2,1)S(1)} %bitcast.14, bf16[1040,128]{1,0:T(8,128)(2,1)S(1)} %shard_map.77.refs_6_.refs_1_, bf16[1040,128]{1,0:T(8,128)(2,1)S(1)} %shard_map.78.refs_7_.refs_2_, ...), custom_call_target="tpu_custom_call", output_to_operand_aliasing={{0}: (5, {})} | custom-call | flops 1000 | bytes 1000 | tf_op jit(solution)/shard_map/pallas_call | solution.py:332
  35.2 1.5 %collective-permute-done.11.refs_0_ = bf16[1040,128]{1,0:T(8,128)(2,1)S(1)} collective-permute-done((bf16[1040,128]{1,0:T(8,128)(2,1)S(1)}, bf16[1040,128]{1,0:T(8,128)(2,1)S(1)}, u32[]{:S(2)}, u32[]{:S(2)}) %collective-permute-start.11) | collective-permute-done | bytes 266272 | tf_op jit(solution)/shard_map/ppermute | solution.py:568
  36.7 0.1 collective-permute-start.14
  36.7 0.0 collective-permute-done.6.refs_0_
  36.7 1.9 %collective-permute-start.10 = (bf16[1040,128]{1,0:T(8,128)(2,1)S(1)}, bf16[1040,128]{1,0:T(8,128)(2,1)S(1)}, u32[]{:S(2)}, u32[]{:S(2)}) collective-permute-start(bf16[1040,128]{1,0:T(8,128)(2,1)S(1)} %shard_map.83.refs_6_.refs_1_), channel_id=1, source_target_pairs={{4,12},{6,14},{12,20},{14,22},{20,28},{22,30},{28,24},{30,26},{24,... | collective-permute-start | bytes 798728 | tf_op jit(solution)/shard_map/ppermute | solution.py:568
  38.7 2.4 %shard_map.85 = (f32[768,768]{1,0:T(8,128)S(1)}, f32[8,128]{1,0:T(8,128)S(1)}) custom-call(bf16[2048,1536]{1,0:T(8,128)(2,1)S(1)} %collective-permute-done.4.refs_0_, bf16[1040,128]{1,0:T(8,128)(2,1)S(1)} %shard_map.77.refs_6_.refs_1_, bf16[1040,128]{1,0:T(8,128)(2,1)S(1)} %shard_map.78.refs_7_.refs_2_, ...), custom_call_target="tpu_custom_call", output_to_operand_aliasing={{0}: (5, {})} | custom-call | flops 1000 | bytes 1000 | tf_op jit(solution)/shard_map/pallas_call | solution.py:332
  41.0 1.1 %collective-permute-done.13.refs_0_ = bf16[1040,128]{1,0:T(8,128)(2,1)S(1)} collective-permute-done((bf16[1040,128]{1,0:T(8,128)(2,1)S(1)}, bf16[1040,128]{1,0:T(8,128)(2,1)S(1)}, u32[]{:S(2)}, u32[]{:S(2)}) %collective-permute-start.13) | collective-permute-done | bytes 266272 | tf_op jit(solution)/shard_map/ppermute | solution.py:568
  42.2 0.2 collective-permute-done.12.refs_0_
  42.4 2.4 %shard_map.88 = (f32[768,768]{1,0:T(8,128)S(1)}, bf16[2688,128]{1,0:T(8,128)(2,1)S(1)}) custom-call(bf16[2048,1536]{1,0:T(8,128)(2,1)S(1)} %collective-permute-done.4.refs_0_, bf16[1040,128]{1,0:T(8,128)(2,1)S(1)} %shard_map.83.refs_6_.refs_1_, bf16[1040,128]{1,0:T(8,128)(2,1)S(1)} %shard_map.84.refs_7_.refs_2_, ...), custom_call_target="tpu_custom_call", output_to_operand_aliasing={{0}: (5, {})} | custom-call | flops 1000 | bytes 1000 | tf_op jit(solution)/shard_map/pallas_call | solution.py:332
  44.8 0.1 collective-permute-start.17
  44.9 2.4 %shard_map.89 = (f32[768,768]{1,0:T(8,128)S(1)}, f32[8,128]{1,0:T(8,128)S(1)}) custom-call(bf16[2048,1536]{1,0:T(8,128)(2,1)S(1)} %bitcast.15, bf16[1040,128]{1,0:T(8,128)(2,1)S(1)} %shard_map.83.refs_6_.refs_1_, bf16[1040,128]{1,0:T(8,128)(2,1)S(1)} %shard_map.84.refs_7_.refs_2_, ...), custom_call_target="tpu_custom_call", output_to_operand_aliasing={{0}: (5, {})} | custom-call | flops 1000 | bytes 1000 | tf_op jit(solution)/shard_map/pallas_call | solution.py:332
  47.2 0.2 collective-permute-done.14.refs_0_
  47.4 0.4 collective-permute-start.16
  47.8 0.0 collective-permute-done.10.refs_0_
  47.8 0.1 collective-permute-start.15
  47.9 0.0 collective-permute-done.17.tiles_ref
  47.9 0.3 shard_map.93.refs_5_
  48.2 0.8 %collective-permute-done.16.refs_4_ = bf16[1040,128]{1,0:T(8,128)(2,1)S(1)} collective-permute-done((bf16[1040,128]{1,0:T(8,128)(2,1)S(1)}, bf16[1040,128]{1,0:T(8,128)(2,1)S(1)}, u32[]{:S(2)}, u32[]{:S(2)}) %collective-permute-start.16) | collective-permute-done | bytes 266272 | tf_op jit(solution)/shard_map/ppermute | solution.py:568
  49.0 0.4 collective-permute-done.15.refs_3_
  49.3 2.4 %shard_map.94 = (f32[768,768]{1,0:T(8,128)S(1)}, bf16[1296,128]{1,0:T(8,128)(2,1)S(1)}, bf16[768,256]{1,0:T(8,128)(2,1)S(1)}) custom-call(bf16[2048,1536]{1,0:T(8,128)(2,1)S(1)} %bitcast.16, bf16[1040,128]{1,0:T(8,128)(2,1)S(1)} %shard_map.90.refs_1_, bf16[1040,128]{1,0:T(8,128)(2,1)S(1)} %shard_map.91.refs_2_, ...), custom_call_target="tpu_custom_call", output_to_operand_aliasing={{0}: (5, {})} | custom-call | flops 1000 | bytes 1000 | tf_op jit(solution)/shard_map/pallas_call | solution.py:332
  51.7 1.6 %collective-permute-start.18 = (bf16[1296,128]{1,0:T(8,128)(2,1)S(1)}, bf16[1296,128]{1,0:T(8,128)(2,1)S(1)}, u32[]{:S(2)}, u32[]{:S(2)}) collective-permute-start(bf16[1296,128]{1,0:T(8,128)(2,1)S(1)} %get-tuple-element.63), channel_id=1, source_target_pairs={{0,1},{1,0},{2,3},{3,2},{4,5},{5,4},{6,7},{7,6},{8,9},{9,8},{10,11... | collective-permute-start | bytes 995336 | tf_op jit(solution)/shard_map/ppermute | solution.py:632
  53.3 0.5 shard_map.95
  53.8 0.6 collective-permute-start.19
  54.4 4.8 %shard_map.96 = (f32[768,768]{1,0:T(8,128)S(1)}, f32[768,256]{1,0:T(8,128)S(1)}, bf16[2048,768]{1,0:T(8,128)(2,1)S(1)}, bf16[768,768]{1,0:T(8,128)(2,1)S(1)}) custom-call(f32[768,768]{1,0:T(8,128)S(1)} %get-tuple-element.59.own_ref, bf16[768,256]{1,0:T(8,128)(2,1)S(1)} %get-tuple-element.39.refs_1_.refs_5_.high_ref.first_ref.refs_4_, ...), custom_call_target="tpu_custom_call" | custom-call | flops 1000 | bytes 1000 | tf_op jit(solution)/shard_map/pallas_call | solution.py:402
  59.2 3.2 %collective-permute-done.18.front_ref = bf16[1296,128]{1,0:T(8,128)(2,1)S(1)} collective-permute-done((bf16[1296,128]{1,0:T(8,128)(2,1)S(1)}, bf16[1296,128]{1,0:T(8,128)(2,1)S(1)}, u32[]{:S(2)}, u32[]{:S(2)}) %collective-permute-start.18) | collective-permute-done | bytes 331808 | tf_op jit(solution)/shard_map/ppermute | solution.py:632
  62.4 0.7 %shard_map.97 = (f32[768,768]{1,0:T(8,128)S(1)}, f32[768,256]{1,0:T(8,128)S(1)}, bf16[768,768]{1,0:T(8,128)(2,1)S(1)}) custom-call(f32[768,768]{1,0:T(8,128)S(1)} %get-tuple-element.61.own_in, f32[768,256]{1,0:T(8,128)S(1)} %get-tuple-element.62.panel_in, ...), custom_call_target="tpu_custom_call", output_to_operand_aliasing={{0}: (0, {}), {1}: (1, {})} | custom-call | flops 1000 | bytes 1000 | tf_op jit(solution)/shard_map/pallas_call | solution.py:436
  63.1 4.4 %collective-permute-done.19.refs_3_ = bf16[1040,128]{1,0:T(8,128)(2,1)S(1)} collective-permute-done((bf16[1040,128]{1,0:T(8,128)(2,1)S(1)}, bf16[1040,128]{1,0:T(8,128)(2,1)S(1)}, u32[]{:S(2)}, u32[]{:S(2)}) %collective-permute-start.19) | collective-permute-done | bytes 266272 | tf_op jit(solution)/shard_map/ppermute | solution.py:632
  67.6 3.5 %shard_map.98 = (f32[384,768]{1,0:T(8,128)}, f32[1024,256]{1,0:T(8,128)}) custom-call(f32[768,768]{1,0:T(8,128)S(1)} %get-tuple-element.64.refs_0_, f32[768,256]{1,0:T(8,128)S(1)} %get-tuple-element.65.refs_1_, bf16[768,768]{1,0:T(8,128)(2,1)S(1)} %get-tuple-element.66.refs_2_, bf16[1040,128]{1,0:T(8,128)(2,1)S(1)} %collective-permute-done.19.refs_3_, ...), custom_call_target="tpu_custom_call" | custom-call | flops 4227858432 | bytes 6291456 | tf_op jit(solution)/shard_map/pallas_call | solution.py:521
  (16 shorter events, 0.0 us)
Async XLA Ops:
  1.8 9.4 %collective-permute-start.2 = (bf16[1040,128]{1,0:T(8,128)(2,1)S(1)}, bf16[1040,128]{1,0:T(8,128)(2,1)S(1)}, u32[]{:S(2)}, u32[]{:S(2)}) collective-permute-start(bf16[1040,128]{1,0:T(8,128)(2,1)S(1)} %get-tuple-element.38.refs_1_.refs_2_), channel_id=1, source_target_pairs={{12,4},{14,6},{20,12},{22,14},{28,20},{30,22},{24,28},{26,30},{16,... | collective-permute-start | bytes 798728 | tf_op jit(solution)/shard_map/ppermute | solution.py:568
  4.9 8.8 %collective-permute-start = (bf16[1040,128]{1,0:T(8,128)(2,1)S(1)}, bf16[1040,128]{1,0:T(8,128)(2,1)S(1)}, u32[]{:S(2)}, u32[]{:S(2)}) collective-permute-start(bf16[1040,128]{1,0:T(8,128)(2,1)S(1)} %get-tuple-element.37.refs_0_.refs_1_), channel_id=1, source_target_pairs={{4,12},{6,14},{12,20},{14,22},{20,28},{22,30},{28,24},{30,26},{24,... | collective-permute-start | bytes 798728 | tf_op jit(solution)/shard_map/ppermute | solution.py:568
  4.9 11.0 %collective-permute-start.4 = (bf16[2048,1536]{1,0:T(8,128)(2,1)}, bf16[2048,1536]{1,0:T(8,128)(2,1)S(1)}, u32[]{:S(2)}, u32[]{:S(2)}) collective-permute-start(bf16[2048,1536]{1,0:T(8,128)(2,1)} %bitcast.9), channel_id=1, source_target_pairs={{0,2},{2,0},{4,6},{6,4},{8,10},{10,8},{12,14},{14,12},{16,18},{18,... | collective-permute-start | bytes 18874376 | tf_op jit(solution)/shard_map/ppermute | solution.py:568
  4.9 8.8 %slice-start = ((s8[6291456]{0:T(1024)(128)(4,1)}), s8[4194304]{0:T(1024)(128)(4,1)S(1)}, s32[]{:S(2)}) async-start(s8[6291456]{0:T(1024)(128)(4,1)} %bitcast.10), calls=%async_computation | async-start | bytes 8388608
  4.9 8.8 %slice-start.1 = ((s8[6291456]{0:T(1024)(128)(4,1)}), s8[2097152]{0:T(1024)(128)(4,1)S(1)}, s32[]{:S(2)}) async-start(s8[6291456]{0:T(1024)(128)(4,1)} %bitcast.10), calls=%async_computation.1 | async-start | bytes 4194304
  8.3 11.1 %collective-permute-start.5 = (bf16[1040,128]{1,0:T(8,128)(2,1)S(1)}, bf16[1040,128]{1,0:T(8,128)(2,1)S(1)}, u32[]{:S(2)}, u32[]{:S(2)}) collective-permute-start(bf16[1040,128]{1,0:T(8,128)(2,1)S(1)} %get-tuple-element.43), channel_id=1, source_target_pairs={{4,12},{6,14},{12,20},{14,22},{20,28},{22,30},{28,24},{30,26},{24,... | collective-permute-start | bytes 798728 | tf_op jit(solution)/shard_map/ppermute | solution.py:568
  10.3 9.2 %collective-permute-start.3 = (bf16[1040,128]{1,0:T(8,128)(2,1)S(1)}, bf16[1040,128]{1,0:T(8,128)(2,1)S(1)}, u32[]{:S(2)}, u32[]{:S(2)}) collective-permute-start(bf16[1040,128]{1,0:T(8,128)(2,1)S(1)} %get-tuple-element.40), channel_id=1, source_target_pairs={{12,4},{14,6},{20,12},{22,14},{28,20},{30,22},{24,28},{26,30},{16,... | collective-permute-start | bytes 798728 | tf_op jit(solution)/shard_map/ppermute | solution.py:568
  11.2 14.0 %collective-permute-start.7 = (bf16[1040,128]{1,0:T(8,128)(2,1)S(1)}, bf16[1040,128]{1,0:T(8,128)(2,1)S(1)}, u32[]{:S(2)}, u32[]{:S(2)}) collective-permute-start(bf16[1040,128]{1,0:T(8,128)(2,1)S(1)} %shard_map.71.refs_4_.refs_2_), channel_id=1, source_target_pairs={{12,4},{14,6},{20,12},{22,14},{28,20},{30,22},{24,28},{26,30},{16,... | collective-permute-start | bytes 798728 | tf_op jit(solution)/shard_map/ppermute | solution.py:568
  13.7 11.7 %collective-permute-start.1 = (bf16[1040,128]{1,0:T(8,128)(2,1)S(1)}, bf16[1040,128]{1,0:T(8,128)(2,1)S(1)}, u32[]{:S(2)}, u32[]{:S(2)}) collective-permute-start(bf16[1040,128]{1,0:T(8,128)(2,1)S(1)} %shard_map.70.refs_3_.refs_1_), channel_id=1, source_target_pairs={{4,12},{6,14},{12,20},{14,22},{20,28},{22,30},{28,24},{30,26},{24,... | collective-permute-start | bytes 798728 | tf_op jit(solution)/shard_map/ppermute | solution.py:568
  19.4 11.4 %collective-permute-start.9 = (bf16[1040,128]{1,0:T(8,128)(2,1)S(1)}, bf16[1040,128]{1,0:T(8,128)(2,1)S(1)}, u32[]{:S(2)}, u32[]{:S(2)}) collective-permute-start(bf16[1040,128]{1,0:T(8,128)(2,1)S(1)} %shard_map.75.refs_4_.refs_6_), channel_id=1, source_target_pairs={{4,12},{6,14},{12,20},{14,22},{20,28},{22,30},{28,24},{30,26},{24,... | collective-permute-start | bytes 798728 | tf_op jit(solution)/shard_map/ppermute | solution.py:568
  19.5 11.7 %collective-permute-start.8 = (bf16[1040,128]{1,0:T(8,128)(2,1)S(1)}, bf16[1040,128]{1,0:T(8,128)(2,1)S(1)}, u32[]{:S(2)}, u32[]{:S(2)}) collective-permute-start(bf16[1040,128]{1,0:T(8,128)(2,1)S(1)} %shard_map.74.refs_3_.refs_7_), channel_id=1, source_target_pairs={{12,4},{14,6},{20,12},{22,14},{28,20},{30,22},{24,28},{26,30},{16,... | collective-permute-start | bytes 798728 | tf_op jit(solution)/shard_map/ppermute | solution.py:568
  25.2 11.4 %collective-permute-start.11 = (bf16[1040,128]{1,0:T(8,128)(2,1)S(1)}, bf16[1040,128]{1,0:T(8,128)(2,1)S(1)}, u32[]{:S(2)}, u32[]{:S(2)}) collective-permute-start(bf16[1040,128]{1,0:T(8,128)(2,1)S(1)} %shard_map.78.refs_7_.refs_2_), channel_id=1, source_target_pairs={{12,4},{14,6},{20,12},{22,14},{28,20},{30,22},{24,28},{26,30},{16,... | collective-permute-start | bytes 798728 | tf_op jit(solution)/shard_map/ppermute | solution.py:568
  25.3 11.4 %collective-permute-start.6 = (bf16[1040,128]{1,0:T(8,128)(2,1)S(1)}, bf16[1040,128]{1,0:T(8,128)(2,1)S(1)}, u32[]{:S(2)}, u32[]{:S(2)}) collective-permute-start(bf16[1040,128]{1,0:T(8,128)(2,1)S(1)} %shard_map.77.refs_6_.refs_1_), channel_id=1, source_target_pairs={{4,12},{6,14},{12,20},{14,22},{20,28},{22,30},{28,24},{30,26},{24,... | collective-permute-start | bytes 798728 | tf_op jit(solution)/shard_map/ppermute | solution.py:568
  30.8 11.4 %collective-permute-start.13 = (bf16[1040,128]{1,0:T(8,128)(2,1)S(1)}, bf16[1040,128]{1,0:T(8,128)(2,1)S(1)}, u32[]{:S(2)}, u32[]{:S(2)}) collective-permute-start(bf16[1040,128]{1,0:T(8,128)(2,1)S(1)} %shard_map.81.refs_4_.refs_6_), channel_id=1, source_target_pairs={{4,12},{6,14},{12,20},{14,22},{20,28},{22,30},{28,24},{30,26},{24,... | collective-permute-start | bytes 798728 | tf_op jit(solution)/shard_map/ppermute | solution.py:568
  31.3 11.1 %collective-permute-start.12 = (bf16[1040,128]{1,0:T(8,128)(2,1)S(1)}, bf16[1040,128]{1,0:T(8,128)(2,1)S(1)}, u32[]{:S(2)}, u32[]{:S(2)}) collective-permute-start(bf16[1040,128]{1,0:T(8,128)(2,1)S(1)} %shard_map.80.refs_3_.refs_7_), channel_id=1, source_target_pairs={{12,4},{14,6},{20,12},{22,14},{28,20},{30,22},{24,28},{26,30},{16,... | collective-permute-start | bytes 798728 | tf_op jit(solution)/shard_map/ppermute | solution.py:568
  36.7 10.7 %collective-permute-start.14 = (bf16[1040,128]{1,0:T(8,128)(2,1)S(1)}, bf16[1040,128]{1,0:T(8,128)(2,1)S(1)}, u32[]{:S(2)}, u32[]{:S(2)}) collective-permute-start(bf16[1040,128]{1,0:T(8,128)(2,1)S(1)} %shard_map.84.refs_7_.refs_2_), channel_id=1, source_target_pairs={{12,4},{14,6},{20,12},{22,14},{28,20},{30,22},{24,28},{26,30},{16,... | collective-permute-start | bytes 798728 | tf_op jit(solution)/shard_map/ppermute | solution.py:568
  36.7 11.1 %collective-permute-start.10 = (bf16[1040,128]{1,0:T(8,128)(2,1)S(1)}, bf16[1040,128]{1,0:T(8,128)(2,1)S(1)}, u32[]{:S(2)}, u32[]{:S(2)}) collective-permute-start(bf16[1040,128]{1,0:T(8,128)(2,1)S(1)} %shard_map.83.refs_6_.refs_1_), channel_id=1, source_target_pairs={{4,12},{6,14},{12,20},{14,22},{20,28},{22,30},{28,24},{30,26},{24,... | collective-permute-start | bytes 798728 | tf_op jit(solution)/shard_map/ppermute | solution.py:568
  44.8 3.1 %collective-permute-start.17 = (bf16[2688,128]{1,0:T(8,128)(2,1)S(1)}, bf16[2688,128]{1,0:T(8,128)(2,1)S(1)}, u32[]{:S(2)}, u32[]{:S(2)}) collective-permute-start(bf16[2688,128]{1,0:T(8,128)(2,1)S(1)} %get-tuple-element.54.refs_8_), channel_id=1, source_target_pairs={{0,2},{2,0},{4,6},{6,4},{8,10},{10,8},{12,14},{14,12},{16,18},{18,... | collective-permute-start | bytes 2064392 | tf_op jit(solution)/shard_map/ppermute | solution.py:568
  47.4 1.6 %collective-permute-start.16 = (bf16[1040,128]{1,0:T(8,128)(2,1)S(1)}, bf16[1040,128]{1,0:T(8,128)(2,1)S(1)}, u32[]{:S(2)}, u32[]{:S(2)}) collective-permute-start(bf16[1040,128]{1,0:T(8,128)(2,1)S(1)} %shard_map.91.refs_2_), channel_id=1, source_target_pairs={{0,2},{2,0},{4,6},{6,4},{8,10},{10,8},{12,14},{14,12},{16,18},{18,... | collective-permute-start | bytes 798728 | tf_op jit(solution)/shard_map/ppermute | solution.py:568
  47.8 1.5 %collective-permute-start.15 = (bf16[1040,128]{1,0:T(8,128)(2,1)S(1)}, bf16[1040,128]{1,0:T(8,128)(2,1)S(1)}, u32[]{:S(2)}, u32[]{:S(2)}) collective-permute-start(bf16[1040,128]{1,0:T(8,128)(2,1)S(1)} %shard_map.90.refs_1_), channel_id=1, source_target_pairs={{0,2},{2,0},{4,6},{6,4},{8,10},{10,8},{12,14},{14,12},{16,18},{18,... | collective-permute-start | bytes 798728 | tf_op jit(solution)/shard_map/ppermute | solution.py:568
  51.7 10.7 %collective-permute-start.18 = (bf16[1296,128]{1,0:T(8,128)(2,1)S(1)}, bf16[1296,128]{1,0:T(8,128)(2,1)S(1)}, u32[]{:S(2)}, u32[]{:S(2)}) collective-permute-start(bf16[1296,128]{1,0:T(8,128)(2,1)S(1)} %get-tuple-element.63), channel_id=1, source_target_pairs={{0,1},{1,0},{2,3},{3,2},{4,5},{5,4},{6,7},{7,6},{8,9},{9,8},{10,11... | collective-permute-start | bytes 995336 | tf_op jit(solution)/shard_map/ppermute | solution.py:632
  53.8 13.8 %collective-permute-start.19 = (bf16[1040,128]{1,0:T(8,128)(2,1)S(1)}, bf16[1040,128]{1,0:T(8,128)(2,1)S(1)}, u32[]{:S(2)}, u32[]{:S(2)}) collective-permute-start(bf16[1040,128]{1,0:T(8,128)(2,1)S(1)} %get-tuple-element.67), channel_id=1, source_target_pairs={{0,1},{1,0},{2,3},{3,2},{4,5},{5,4},{6,7},{7,6},{8,9},{9,8},{10,11... | collective-permute-start | bytes 798728 | tf_op jit(solution)/shard_map/ppermute | solution.py:632
